TPU v7x, 512 devices: a whole 4x4x16 slice. The times are simulated.
512 devices in a mesh: src: 16 (over z_lo, core), dst: 32 (over z_hi, x, y).
Axes of the slice: x: 4, y: 4, z: 16 (z_hi: 2, z_lo: 8; z = z_hi * 8 + z_lo), core: 2. Of those that a mesh axis runs over, the one named last changes fastest.
Arguments:
- src_emb: float32 [16, 32, 384, 256], P('src', 'dst'), may hold values from -3 to 3
- src_state: float32 [16, 32, 384], P('src', 'dst'), may hold values from 0.01 to 1
- dst_emb: float32 [16, 32, 1024, 256], P('src', 'dst'), may hold values from -3 to 3
- dst_state: float32 [16, 32, 1024], P('src', 'dst'), may hold values from 0.01 to 1
- src_ids: int32 [16, 32, 256], P('src', 'dst'), may hold values from 0 to 6143
- dst_ids: int32 [16, 32, 256], P('src', 'dst'), may hold values from 0 to 1023
- neg_ids: int32 [16, 32, 1024], P('src', 'dst'), may hold values from 0 to 1023
- counts: int32 [16, 32], P('src', 'dst'), may hold values from 64 to 256, as said below
Outputs:
- src_new: float32 [16, 32, 384, 256], P('src', 'dst')
- src_state_new: float32 [16, 32, 384], P('src', 'dst')
- dst_new: float32 [16, 32, 1024, 256], P('src', 'dst')
- dst_state_new: float32 [16, 32, 1024], P('src', 'dst')
- edge_loss: float32 [16, 32, 256], P('src', 'dst')
Inputs may be any that keep to these rules, and one draw needn't show every extreme that they name: `counts`: each block has 64 to 256 live edges, and some block has exactly 256.
All inputs are finite; a program needn't handle non-finite values.
Results may differ from a plain program's by a relative error of at most 0.0003.
Values sent between devices are 32-bit elements; how exact they have to be, the bound alone decides.
No kernel may reach another device: no remote copies, remote signals or barrier semaphores. Data moves between devices by JAX's collectives and lax.ppermute only.
A program may use at most 64 MiB of HBM per device.

v0:
```python
import jax
import jax.numpy as jnp
from jax import lax
from jax.sharding import PartitionSpec as P


def from_behind(value, axis, steps):
    count = lax.axis_size(axis)
    pairs = [(source, (source + steps) % count) for source in range(count)]
    return lax.ppermute(value, axis, pairs)


def product(left, right):
    return jnp.dot(left, right, precision=lax.Precision.HIGHEST, preferred_element_type=jnp.float32)


def product_first(left, right):
    return lax.dot_general(
        left,
        right,
        (((0,), (0,)), ((), ())),
        precision=lax.Precision.HIGHEST,
        preferred_element_type=jnp.float32,
    )


def adagrad(emb, state, grad):
    state_new = state + jnp.mean(grad * grad, axis=-1)
    emb_new = emb - 0.1 * grad / (jnp.sqrt(state_new)[:, None] + 1e-10)
    return (emb_new, state_new)


def on_device(src_emb, src_state, dst_emb, dst_state, src_ids, dst_ids, neg_ids, counts):
    table, table_state = from_behind((dst_emb[0, 0], dst_state[0, 0]), "dst", 1)
    own_rows = src_emb[0, 0]
    own_state = src_state[0, 0]
    shard_rows = own_rows.shape[0]
    first_row = lax.axis_index("src") * shard_rows
    own_index = first_row + jnp.arange(shard_rows, dtype=jnp.int32)
    source_ids = src_ids[0, 0]
    edge_count = source_ids.shape[0]
    piece = lax.all_gather(own_rows, "src", axis=0, tiled=True)
    columns = jnp.arange(piece.shape[0], dtype=jnp.int32)
    onehot = (source_ids[:, None] == columns[None, :]).astype(jnp.float32)
    sources = product(onehot, piece)
    row_index = jnp.arange(table.shape[0], dtype=jnp.int32)
    hot_dest = (dst_ids[0, 0][:, None] == row_index[None, :]).astype(jnp.float32)
    hot_negative = (neg_ids[0, 0][:, None] == row_index[None, :]).astype(jnp.float32)
    targets = product(hot_dest, table)
    negatives = product(hot_negative, table)
    positive = jnp.sum(sources * targets, axis=1)
    scores = lax.dot_general(
        sources,
        negatives,
        (((1,), (1,)), ((), ())),
        precision=lax.Precision.HIGHEST,
        preferred_element_type=jnp.float32,
    )
    live = (jnp.arange(edge_count, dtype=jnp.int32) < counts[0, 0]).astype(jnp.float32)
    top = jnp.maximum(jnp.max(scores, axis=1), positive)
    total = jnp.exp(positive - top) + jnp.sum(jnp.exp(scores - top[:, None]), axis=1)
    logsum = top + jnp.log(total)
    loss = live * (logsum - positive)
    dpos = live * (jnp.exp(positive - logsum) - 1.0)
    dneg = live[:, None] * jnp.exp(scores - logsum[:, None])
    source_grad = dpos[:, None] * targets + product(dneg, negatives)
    target_grad = dpos[:, None] * sources
    negative_grad = product_first(dneg, sources)
    dest_grad = product_first(hot_dest, target_grad) + product_first(hot_negative, negative_grad)
    own_float = own_index.astype(jnp.float32)
    id_piece = lax.all_gather(source_ids.astype(jnp.float32), "src", axis=0, tiled=True)
    grad_piece = lax.all_gather(source_grad, "src", axis=0, tiled=True)
    onehot = (id_piece[:, None] == own_float[None, :]).astype(jnp.float32)
    own_grad = product_first(onehot, grad_piece)
    src_new, src_state_new = adagrad(own_rows, own_state, own_grad)
    dst_new, dst_state_new = adagrad(table, table_state, dest_grad)
    return (
        src_new[None, None],
        src_state_new[None, None],
        dst_new[None, None],
        dst_state_new[None, None],
        loss[None, None],
    )


def solution(mesh):
    return jax.shard_map(
        on_device,
        mesh=mesh,
        in_specs=(
            P("src", "dst", None, None),
            P("src", "dst", None),
            P("src", "dst", None, None),
            P("src", "dst", None),
            P("src", "dst", None),
            P("src", "dst", None),
            P("src", "dst", None),
            P("src", "dst"),
        ),
        out_specs=(
            P("src", "dst", None, None),
            P("src", "dst", None),
            P("src", "dst", None, None),
            P("src", "dst", None),
            P("src", "dst", None),
        ),
        check_vma=False,
    )
```

profile of v0, /device:TPU:22, one launch (start us, length us, event | category | flops | bytes accessed | tf_op | source)
XLA Modules:
  0.0 328.8 jit_solution(15379464114881136554)
XLA Ops:
  7.2 0.0 copy-start.1
  7.2 0.0 all-gather.7.cloned.1.call-start
  7.2 0.7 all-gather.7.cloned.1.call-update
  7.9 0.0 all-gather.5.cloned.1.call-start
  8.0 1.6 copy.18
  9.5 3.2 collective-permute-start
  13.4 22.9 %collective-permute-done = f32[1024,256]{0,1:T(8,128)S(1)} collective-permute-done((f32[1024,256]{0,1:T(8,128)S(1)}, f32[1024,256]{0,1:T(8,128)S(1)}, u32[]{:S(2)}, u32[]{:S(2)}) %collective-permute-start) | collective-permute-done | bytes 1048608 | tf_op jit(solution)/shard_map/ppermute | solution.py:10
  36.3 1.5 fusion.13
  37.8 0.0 copy-start
  37.8 2.8 fusion.5
  40.6 85.6 %all-gather.7.cloned.1.call-done = f32[1,1,6144,256]{3,2,1,0:T(8,128)} async-done(((f32[1,1,384,256]{3,2,1,0:T(8,128)}), f32[1,1,6144,256]{3,2,1,0:T(8,128)}) %all-gather.7.cloned.1.call-update) | async-done | bytes 6291472 | tf_op jit(solution)/shard_map/all_gather | solution.py:42
  126.2 0.0 copy-done.1
  126.2 8.8 %multiply_reduce_fusion.2 = (f32[256]{0:T(256)S(1)}, f32[256,256]{0,1:T(8,128)S(1)}) fusion(f32[256,256]{0,1:T(8,128)S(1)} %fusion.13, f32[1,1,6144,256]{3,2,1,0:T(8,128)} %all-gather.7.cloned.1.call-done, s32[256]{0:T(256)S(1)} %bitcast.37), kind=kOutput, calls=%fused_computation.34 | convolution fusion | flops 4833542144 | bytes 6817792 | tf_op jit(solution)/shard_map/dot_general | solution.py:14
  135.0 0.0 copy-done
  135.0 0.0 copy-start.5
  135.0 0.0 copy-start.2
  135.1 0.0 copy-start.3
  135.1 1.9 fusion.26
  137.0 0.0 copy-start.4
  137.0 0.3 exponential_reduce_fusion
  137.3 3.6 %multiply_add_fusion = f32[256,256]{0,1:T(8,128)} fusion(f32[256,256]{0,1:T(8,128)} %copy-done, f32[256]{0:T(256)S(1)} %get-tuple-element.17, f32[1024,256]{1,0:T(8,128)S(1)} %fusion.5, f32[256,1024]{1,0:T(8,128)S(1)} %get-tuple-element.24, f32[256]{0:T(256)S(1)} %get-tuple-element.18, f32[256]{0:T(256)S(1)} %fusion.25), kind=kOutput, calls=%fused_computation.33 | convolution fusion | flops 805961728 | bytes 2624512 | tf_op jit(solution)/shard_map/dot_general | solution.py:14
  140.9 0.0 all-gather.5.cloned.1.call-update
  140.9 0.0 copy-done.5
  140.9 73.4 %collective-permute-start.1 = (f32[1024]{0:T(1024)S(1)}, f32[1024]{0:T(1024)S(1)}, u32[]{:S(2)}, u32[]{:S(2)}) collective-permute-start(f32[1024]{0:T(1024)S(1)} %bitcast.49), channel_id=1, source_target_pairs={{0,1},{1,2},{2,3},{3,4},{4,5},{5,6},{6,7},{7,8},{8,9},{9,10},{10,1... | collective-permute-start | bytes 12296 | tf_op jit(solution)/shard_map/ppermute | solution.py:10
  214.3 1.2 copy.17
  215.5 0.0 copy-done.2
  215.5 27.1 %all-gather.1 = f32[16,1,256]{2,1,0:T(1,128)S(1)} all-gather(f32[1,1,256]{2,1,0:T(1,128)S(1)} %bitcast.43), channel_id=1, replica_groups=mesh['src'=16,'dst'=32] {'src'}, dimensions={0}, use_global_device_ids=true | all-gather | bytes 17408 | tf_op jit(solution)/shard_map/all_gather | solution.py:71
  242.6 0.0 copy-done.3
  242.6 0.8 fusion.12
  243.4 1.9 fusion.14
  245.3 0.0 copy-done.4
  245.3 2.4 multiply_reduce_fusion
  247.7 0.0 collective-permute-done.1
  247.7 0.6 sqrt_add_fusion
  248.3 0.2 subtract_bitcast_fusion
  248.6 1.3 copy.20
  249.9 0.6 compare_select_fusion
  250.4 63.7 %all-gather.5.cloned.1.call-done = f32[4096,256]{0,1:T(8,128)} async-done(((f32[256,256]{0,1:T(8,128)}), f32[4096,256]{0,1:T(8,128)}) %all-gather.5.cloned.1.call-update) | async-done | bytes 4194320 | tf_op jit(solution)/shard_map/all_gather | solution.py:72
  314.2 6.2 %multiply_reduce_fusion.1 = (f32[384]{0:T(512)S(1)}, f32[384,256]{0,1:T(8,128)S(1)}) fusion(f32[4096,256]{0,1:T(8,128)} %all-gather.5.cloned.1.call-done, f32[384]{0:T(512)S(1)} %add_convert_fusion, f32[4096]{0:T(1024)S(1)} %bitcast.40), kind=kOutput, calls=%fused_computation.31 | convolution fusion | flops 4833607168 | bytes 4606976 | tf_op jit(solution)/shard_map/dot_general | solution.py:18
  320.4 0.1 fusion.22
  320.4 0.9 copy.19
  321.4 0.6 reshape_add_fusion
  (7 shorter events, 0.1 us)
Async XLA Ops:
  7.2 119.0 %copy-start.1 = (s32[1,1,256]{2,1,0:T(1,128)S(1)}, s32[1,1,256]{2,1,0:T(1,128)}, u32[]{:S(2)}) copy-start(s32[1,1,256]{2,1,0:T(1,128)} %param.12) | copy-start | bytes 3076
  7.2 119.0 %all-gather.7.cloned.1.call-start = ((), (), s32[]{:S(2)}) async-start(), calls=%async_computation.1 | async-start | bytes 6684672 | tf_op jit(solution)/shard_map/all_gather | solution.py:42
  7.9 306.3 %all-gather.5.cloned.1.call-start = ((), (), s32[]{:S(2)}) async-start(), calls=%async_computation | async-start | bytes 4456448 | tf_op jit(solution)/shard_map/all_gather | solution.py:72
  9.5 26.8 %collective-permute-start = (f32[1024,256]{0,1:T(8,128)S(1)}, f32[1024,256]{0,1:T(8,128)S(1)}, u32[]{:S(2)}, u32[]{:S(2)}) collective-permute-start(f32[1024,256]{0,1:T(8,128)S(1)} %bitcast.36), channel_id=1, source_target_pairs={{0,1},{1,2},{2,3},{3,4},{4,5},{5,6},{6,7},{7,8},{8,9},{9,10},{10,1... | collective-permute-start | bytes 3145736 | tf_op jit(solution)/shard_map/ppermute | solution.py:10
  37.8 97.2 %copy-start = (f32[256,256]{0,1:T(8,128)}, f32[256,256]{0,1:T(8,128)S(1)}, u32[]{:S(2)}) copy-start(f32[256,256]{0,1:T(8,128)S(1)} %fusion.13) | copy-start | bytes 786436
  135.0 5.9 %copy-start.5 = (f32[1,1,1024]{2,1,0:T(1,128)S(1)}, f32[1,1,1024]{2,1,0:T(1,128)}, u32[]{:S(2)}) copy-start(f32[1,1,1024]{2,1,0:T(1,128)} %param.11) | copy-start | bytes 12292
  135.0 80.4 %copy-start.2 = (f32[1,1,384]{2,1,0:T(1,128)S(1)}, f32[1,1,384]{2,1,0:T(1,128)}, u32[]{:S(2)}) copy-start(f32[1,1,384]{2,1,0:T(1,128)} %param.9) | copy-start | bytes 4612
  135.1 107.6 %copy-start.3 = (s32[1,1,256]{2,1,0:T(1,128)S(1)}, s32[1,1,256]{2,1,0:T(1,128)}, u32[]{:S(2)}) copy-start(s32[1,1,256]{2,1,0:T(1,128)} %param.13) | copy-start | bytes 3076
  137.0 108.4 %copy-start.4 = (s32[1,1,1024]{2,1,0:T(1,128)S(1)}, s32[1,1,1024]{2,1,0:T(1,128)}, u32[]{:S(2)}) copy-start(s32[1,1,1024]{2,1,0:T(1,128)} %param.14) | copy-start | bytes 12292
  140.9 106.8 %collective-permute-start.1 = (f32[1024]{0:T(1024)S(1)}, f32[1024]{0:T(1024)S(1)}, u32[]{:S(2)}, u32[]{:S(2)}) collective-permute-start(f32[1024]{0:T(1024)S(1)} %bitcast.49), channel_id=1, source_target_pairs={{0,1},{1,2},{2,3},{3,4},{4,5},{5,6},{6,7},{7,8},{8,9},{9,10},{10,1... | collective-permute-start | bytes 12296 | tf_op jit(solution)/shard_map/ppermute | solution.py:10
Sparse Core Ops, SparseCore 0:
  10.1 116.0 all-gather.6
  141.0 173.0 all-gather.4
where the time goes:
time: 329 us
  waiting for transfers between devices  173 us (53%)
  starting transfers between devices  76.6 us (23%)
  matrix products  29.8 us (9%)
  blocking collectives  27.1 us (8%)
  between operations  14.9 us (5%)
  local copies, waits for them, and re-layouts  4.97 us (2%)
    all_gather x1, waiting for transfers between devices, on_device(): piece = lax.all_gather(own_rows, 'src', axis=0, tiled=True)  85.6 us
    ppermute x2, starting transfers between devices, from_behind(): return lax.ppermute(value, axis, pairs)  76.6 us
    all_gather x1, waiting for transfers between devices, on_device(): grad_piece = lax.all_gather(source_grad, 'src', axis=0, tiled=True)  63.7 us
    all_gather x1, blocking collectives, on_device(): lax.all_gather(source_ids.astype(jnp.float32), 'src', axis=0, tiled=True)  27.1 us
    ppermute x2, waiting for transfers between devices, from_behind(): return lax.ppermute(value, axis, pairs)  22.9 us
    dot_general x4, matrix products, product(): jnp.dot(left, right, precision=lax.Precision.HIGHEST, preferred_element_t...  16.7 us
    dot_general x4, matrix products, product_first(): lax.dot_general(left, right, (((0,), (0,)), ((), ())), precision=lax.Prec...  11.2 us
  transfers between devices with their start and end apart: 4, of which 3 were waited for; matrix products, arithmetic and copies ran while one was open for 5% of the time, Pallas kernels for 0%

commit v1 on v0

v1 whole, which is shorter than its diff:
```python
import functools

import jax
import jax.numpy as jnp
from jax import lax
from jax.experimental import pallas as pl
from jax.experimental.pallas import tpu as pltpu
from jax.sharding import PartitionSpec as P

SLOTS = 40
F32 = jnp.float32
BF16 = jnp.bfloat16
VMEM = pl.BlockSpec(memory_space=pltpu.VMEM)
SMEM = pl.BlockSpec(memory_space=pltpu.SMEM)
ROWS = (((1,), (0,)), ((), ()))
LANES = (((1,), (1,)), ((), ()))
FIRST = (((0,), (0,)), ((), ()))


def mxu(left, right, dims=ROWS):
    return lax.dot_general(left, right, dims, preferred_element_type=F32)


def parts_of(value, count):
    parts = []
    for _ in range(count - 1):
        part = value.astype(BF16)
        parts.append(part)
        value = value - part.astype(F32)
    parts.append(value.astype(BF16))
    return parts


def pick(onehot, parts, dims=ROWS):
    total = mxu(onehot, parts[-1], dims)
    for part in parts[-2::-1]:
        total = total + mxu(onehot, part, dims)
    return total


def product(left, right, dims=ROWS):
    total = mxu(left[0], right[1], dims) + mxu(left[1], right[0], dims)
    if len(left) > 2:
        small = mxu(left[0], right[2], dims) + mxu(left[2], right[0], dims)
        total = (small + mxu(left[1], right[1], dims)) + total
    return total + mxu(left[0], right[0], dims)


def flag(condition):
    return jnp.where(condition, 1.0, 0.0).astype(F32)


def to_column(row):
    size = row.shape[1]
    down = lax.broadcasted_iota(jnp.int32, (size, size), 0)
    across = lax.broadcasted_iota(jnp.int32, (size, size), 1)
    return jnp.sum(jnp.where(down == across, row, 0.0), axis=1, keepdims=True)


def pack_rows_kernel(own, slots, first_ref, ids_ref, rows_ref, send_ref, local_ref):
    devices, edges = ids_ref.shape
    local = ids_ref[...] - first_ref[0]
    owned = flag((local >= 0) & (local < own))
    down = lax.broadcasted_iota(jnp.int32, (edges, edges), 0)
    across = lax.broadcasted_iota(jnp.int32, (edges, edges), 1)
    rank = mxu(owned.astype(BF16), flag(down < across).astype(BF16))
    rank = jnp.where(owned > 0.0, rank, -1.0)
    mark = local.astype(F32) + 1.0
    slot = lax.broadcasted_iota(jnp.int32, (slots, edges), 0).astype(F32)
    columns = []
    for device in range(devices):
        chosen = jnp.where(rank[device : device + 1] == slot, mark[device : device + 1], 0.0)
        columns.append(jnp.sum(chosen, axis=1, keepdims=True))
    column = jnp.concatenate(columns, axis=0) - 1.0
    local_ref[...] = column
    across = lax.broadcasted_iota(jnp.int32, (devices * slots, own), 1).astype(F32)
    hot = flag(across == column).astype(BF16)
    send_ref[...] = pick(hot, parts_of(rows_ref[...], 3))


def pack_rows(first, ids, rows, slots):
    devices = ids.shape[0]
    own, width = rows.shape
    return pl.pallas_call(
        functools.partial(pack_rows_kernel, own, slots),
        out_shape=(
            jax.ShapeDtypeStruct((devices * slots, width), F32),
            jax.ShapeDtypeStruct((devices * slots, 1), F32),
        ),
        in_specs=[SMEM, VMEM, VMEM],
        out_specs=(VMEM, VMEM),
        compiler_params=pltpu.CompilerParams(vmem_limit_bytes=40 << 20),
        name="pack_rows",
    )(first, ids, rows)


def edge_kernel(
    devices, own, slots, count_ref, ids_ref, dest_ref, negative_ref, got_ref, table_ref,
    loss_ref, back_ref, source_ref, weight_ref,
):
    edges = ids_ref.shape[1]
    height = table_ref.shape[0]
    ids = ids_ref[...]
    owner = jnp.zeros(ids.shape, F32)
    for device in range(1, devices):
        owner = owner + flag(ids >= device * own)
    down = lax.broadcasted_iota(jnp.int32, (edges, edges), 0)
    across = lax.broadcasted_iota(jnp.int32, (edges, edges), 1)
    before = flag((to_column(owner) == owner) & (down < across))
    rank = jnp.sum(before, axis=0, keepdims=True)
    place = jnp.where(rank < slots, owner * slots + rank, -1.0)
    place_column = to_column(place)
    across = lax.broadcasted_iota(jnp.int32, (edges, devices * slots), 1).astype(F32)
    source = pick(flag(across == place_column).astype(BF16), parts_of(got_ref[...], 3))
    source_ref[...] = source

    table = parts_of(table_ref[...], 3)
    scores = product(parts_of(source, 3), table, LANES)

    negative = negative_ref[...]
    low = 128
    high = height // low
    row = lax.broadcasted_iota(jnp.int32, (high, negative.shape[1]), 0)
    hot_high = flag(row == lax.shift_right_logical(negative, 7)).astype(BF16)
    row = lax.broadcasted_iota(jnp.int32, (low, negative.shape[1]), 0)
    hot_low = flag(row == (negative & (low - 1))).astype(BF16)
    grid = mxu(hot_high, hot_low, LANES)
    times = jnp.concatenate([grid[i : i + 1] for i in range(high)], axis=1)

    dest = to_column(dest_ref[...].astype(F32))
    across = lax.broadcasted_iota(jnp.int32, (edges, height), 1).astype(F32)
    hot = across == dest
    positive = jnp.sum(jnp.where(hot, scores, 0.0), axis=1, keepdims=True)
    seen = times > 0.0
    top = jnp.max(jnp.where(seen, scores, -jnp.inf), axis=1, keepdims=True)
    top = jnp.maximum(top, positive)
    power = jnp.where(seen, jnp.exp(scores - top), 0.0) * times
    power_positive = jnp.exp(positive - top)
    total = power_positive + jnp.sum(power, axis=1, keepdims=True)
    logsum = top + jnp.log(total)
    edge = lax.broadcasted_iota(jnp.int32, (edges, 1), 0)
    live = flag(edge < count_ref[0, 0])
    loss = live * (logsum - positive)
    loss_ref[...] = jnp.transpose(jnp.broadcast_to(loss, (edges, 128)))[0:1]
    scale = live / total
    dpos = live * (jnp.exp(positive - logsum) - 1.0)
    weight = power * scale + jnp.where(hot, dpos, 0.0)
    weight_ref[...] = weight

    grad = product(parts_of(weight, 2), table)
    down = lax.broadcasted_iota(jnp.int32, (devices * slots, edges), 0).astype(F32)
    back_ref[...] = pick(flag(down == place).astype(BF16), parts_of(grad, 3))


def edge_step(count, ids, dest, negative, got, table, devices, own):
    slots = got.shape[0] // devices
    edges = ids.shape[1]
    height, width = table.shape
    return pl.pallas_call(
        functools.partial(edge_kernel, devices, own, slots),
        out_shape=(
            jax.ShapeDtypeStruct((1, edges), F32),
            jax.ShapeDtypeStruct(got.shape, F32),
            jax.ShapeDtypeStruct((edges, width), F32),
            jax.ShapeDtypeStruct((edges, height), F32),
        ),
        in_specs=[SMEM] + [VMEM] * 5,
        out_specs=(VMEM,) * 4,
        compiler_params=pltpu.CompilerParams(vmem_limit_bytes=48 << 20),
        name="edge_step",
    )(count, ids, dest, negative, got, table)


def row_of(column):
    return jnp.transpose(jnp.broadcast_to(column, (column.shape[0], 128)))[0:1]


def column_of(row):
    return jnp.transpose(jnp.broadcast_to(row, (128, row.shape[1])))[:, 0:1]


def adagrad_rows(emb, state, grad):
    state_new = column_of(state) + jnp.mean(grad * grad, axis=1, keepdims=True)
    emb_new = emb - grad * (0.1 / (jnp.sqrt(state_new) + 1e-10))
    return emb_new, row_of(state_new)


def table_kernel(weight_ref, source_ref, table_ref, state_ref, new_ref, state_new_ref):
    grad = product(parts_of(weight_ref[...], 2), parts_of(source_ref[...], 2), FIRST)
    new_ref[...], state_new_ref[...] = adagrad_rows(table_ref[...], state_ref[...], grad)


def table_step(weight, source, table, state):
    return pl.pallas_call(
        table_kernel,
        out_shape=(
            jax.ShapeDtypeStruct(table.shape, F32),
            jax.ShapeDtypeStruct(state.shape, F32),
        ),
        in_specs=[VMEM] * 4,
        out_specs=(VMEM, VMEM),
        compiler_params=pltpu.CompilerParams(vmem_limit_bytes=48 << 20),
        name="table_step",
    )(weight, source, table, state)


def source_kernel(local_ref, back_ref, rows_ref, state_ref, new_ref, state_new_ref):
    own = rows_ref.shape[0]
    across = lax.broadcasted_iota(jnp.int32, (local_ref.shape[0], own), 1).astype(F32)
    hot = flag(across == local_ref[...]).astype(BF16)
    grad = pick(hot, parts_of(back_ref[...], 3), FIRST)
    new_ref[...], state_new_ref[...] = adagrad_rows(rows_ref[...], state_ref[...], grad)


def source_step(local, back, rows, state):
    return pl.pallas_call(
        source_kernel,
        out_shape=(
            jax.ShapeDtypeStruct(rows.shape, F32),
            jax.ShapeDtypeStruct(state.shape, F32),
        ),
        in_specs=[VMEM] * 4,
        out_specs=(VMEM, VMEM),
        compiler_params=pltpu.CompilerParams(vmem_limit_bytes=40 << 20),
        name="source_step",
    )(local, back, rows, state)


def exact(left, right, dims=ROWS):
    return lax.dot_general(left, right, dims, precision=lax.Precision.HIGHEST, preferred_element_type=F32)


def adagrad(emb, state, grad):
    state_new = state + jnp.mean(grad * grad, axis=-1)
    emb_new = emb - 0.1 * grad / (jnp.sqrt(state_new)[:, None] + 1e-10)
    return emb_new, state_new


def whole_step(rows, rows_state, table, table_state, ids, all_ids, dest, negative, count, first):
    piece = lax.all_gather(rows, "src", axis=0, tiled=True)
    columns = jnp.arange(piece.shape[0], dtype=jnp.int32)
    sources = exact((ids[:, None] == columns[None, :]).astype(F32), piece)
    index = jnp.arange(table.shape[0], dtype=jnp.int32)
    hot_dest = (dest[:, None] == index[None, :]).astype(F32)
    hot_negative = (negative[:, None] == index[None, :]).astype(F32)
    targets = exact(hot_dest, table)
    negatives = exact(hot_negative, table)
    positive = jnp.sum(sources * targets, axis=1)
    scores = exact(sources, negatives, LANES)
    live = (jnp.arange(ids.shape[0], dtype=jnp.int32) < count).astype(F32)
    top = jnp.maximum(jnp.max(scores, axis=1), positive)
    total = jnp.exp(positive - top) + jnp.sum(jnp.exp(scores - top[:, None]), axis=1)
    logsum = top + jnp.log(total)
    loss = live * (logsum - positive)
    dpos = live * (jnp.exp(positive - logsum) - 1.0)
    dneg = live[:, None] * jnp.exp(scores - logsum[:, None])
    source_grad = dpos[:, None] * targets + exact(dneg, negatives)
    dest_grad = exact(hot_dest, dpos[:, None] * sources, FIRST)
    dest_grad = dest_grad + exact(hot_negative, exact(dneg, sources, FIRST), FIRST)
    grad_piece = lax.all_gather(source_grad, "src", axis=0, tiled=True)
    own_index = first + jnp.arange(rows.shape[0], dtype=jnp.int32)
    onehot = (all_ids.reshape(-1)[:, None] == own_index[None, :]).astype(F32)
    own_grad = exact(onehot, grad_piece, FIRST)
    new, new_state = adagrad(rows, rows_state, own_grad)
    table_new, table_state_new = adagrad(table, table_state, dest_grad)
    return new, new_state, table_new, table_state_new, loss


def on_device(src_emb, src_state, dst_emb, dst_state, src_ids, dst_ids, neg_ids, counts):
    devices = lax.axis_size("src")
    behind = lax.axis_size("dst")
    pairs = [(source, (source + 1) % behind) for source in range(behind)]
    rows, rows_state = src_emb[0, 0], src_state[0, 0]
    own, width = rows.shape
    ids = src_ids[0, 0]
    first = lax.axis_index("src") * own
    all_ids = lax.all_gather(ids, "src", axis=0, tiled=False)
    table = lax.ppermute(dst_emb[0, 0], "dst", pairs)
    table_state = lax.ppermute(dst_state[0, 0], "dst", pairs)

    owner = lax.broadcasted_iota(jnp.int32, (1, devices, 1), 1)
    used = jnp.sum((all_ids[:, None, :] // own == owner).astype(F32), axis=2)
    over = jnp.max(used) > SLOTS

    send, local = pack_rows(first.reshape(1), all_ids, rows, SLOTS)
    got = lax.all_to_all(send, "src", 0, 0, tiled=True)
    loss, back, source, weight = edge_step(
        counts, src_ids[0], dst_ids[0], neg_ids[0], got, table, devices, own
    )
    back = lax.all_to_all(back, "src", 0, 0, tiled=True)
    dst_new, dst_state_new = table_step(weight, source, table, table_state[None])
    src_new, src_state_new = source_step(local, back, rows, rows_state[None])

    def again(carry):
        found = whole_step(
            rows, rows_state, table, table_state, ids, all_ids, dst_ids[0, 0], neg_ids[0, 0], counts[0, 0], first
        )
        return (jnp.bool_(False),) + found

    fast = (over, src_new, src_state_new[0], dst_new, dst_state_new[0], loss[0])
    done = lax.while_loop(lambda carry: carry[0], again, fast)
    return tuple(value[None, None] for value in done[1:])


def solution(mesh):
    spec = lambda rank: P("src", "dst", *([None] * (rank - 2)))
    return jax.shard_map(
        on_device,
        mesh=mesh,
        in_specs=tuple(spec(rank) for rank in (4, 3, 4, 3, 3, 3, 3, 2)),
        out_specs=tuple(spec(rank) for rank in (4, 3, 4, 3, 3)),
        check_vma=False,
    )
```

time: 329 us -> 245 us (0.74)
  the two profiles are of different devices: /device:TPU:22 before, /device:TPU:64 now
where the time goes in v1:
time: 245 us; the launch traced here: 244 us
  waiting for transfers between devices  131 us (53%)
  starting transfers between devices  42 us (17%)
  blocking collectives  28 us (11%)
  local copies, waits for them, and re-layouts  16 us (7%)
  between operations  15.4 us (6%)
  Pallas kernels  10.6 us (4%)
    ppermute x1, waiting for transfers between devices, on_device(): table = lax.ppermute(dst_emb[0, 0], 'dst', pairs)  107 us
    all_gather x1, blocking collectives, on_device(): all_ids = lax.all_gather(ids, 'src', axis=0, tiled=False)  28 us
    all_to_all x1, starting transfers between devices, on_device(): back = lax.all_to_all(back, 'src', 0, 0, tiled=True)  25.1 us
    ppermute x1, waiting for transfers between devices, on_device(): table_state = lax.ppermute(dst_state[0, 0], 'dst', pairs)  23.2 us
    all_to_all x1, starting transfers between devices, on_device(): got = lax.all_to_all(send, 'src', 0, 0, tiled=True)  11.5 us
    while x6, local copies, waits for them, and re-layouts, on_device(): done = lax.while_loop(lambda carry: carry[0], again, fast)  10.3 us
    pallas_call x1, Pallas kernels, edge_step(): pl.pallas_call(functools.partial(edge_kernel, devices, own, slots), out_s...  5.56 us
  transfers between devices with their start and end apart: 4, of which 2 were waited for; matrix products, arithmetic and copies ran while one was open for 2% of the time, Pallas kernels for 1%

profile of v1, /device:TPU:64, one launch (start us, length us, event | category | flops | bytes accessed | tf_op | source)
XLA Modules:
  0.0 244.2 jit_solution(16122664477276683921)
XLA Ops:
  7.2 0.0 copy-start.14
  7.2 0.0 copy-start.6
  7.2 28.0 %all-gather = s32[16,1,256]{2,1,0:T(1,128)S(1)} all-gather(s32[1,1,256]{2,1,0:T(1,128)} %param.14), channel_id=2, replica_groups=mesh['src'=16,'dst'=32] {'src'}, dimensions={0}, use_global_device_ids=true | all-gather | bytes 17408 | tf_op jit(solution)/shard_map/all_gather | solution.py:277
  35.2 0.0 copy-start
  35.2 1.0 copy-done
  36.2 0.0 copy-start.1
  36.2 2.0 pack_rows.1
  38.2 11.5 %all-to-all-start = ((f32[16,40,256]{2,1,0:T(8,128)}), f32[16,40,256]{2,1,0:T(8,128)S(1)}, u32[]{:S(2)}, u32[]{:S(2)}) async-start(f32[16,40,256]{2,1,0:T(8,128)} %bitcast.9), calls=%async_computation | async-start | bytes 1310720 | tf_op jit(solution)/shard_map/all_to_all | solution.py:286
  49.6 3.5 %collective-permute-start = (f32[1024,256]{1,0:T(8,128)}, f32[1024,256]{1,0:T(8,128)S(1)}, u32[]{:S(2)}, u32[]{:S(2)}) collective-permute-start(f32[1024,256]{1,0:T(8,128)} %bitcast.61), channel_id=1, source_target_pairs={{0,1},{1,2},{2,3},{3,4},{4,5},{5,6},{6,7},{7,8},{8,9},{9,10},{10,1... | collective-permute-start | bytes 3145736 | tf_op jit(solution)/shard_map/ppermute | solution.py:278
  53.8 107.4 %collective-permute-done.table_ref = f32[1024,256]{1,0:T(8,128)S(1)} collective-permute-done((f32[1024,256]{1,0:T(8,128)}, f32[1024,256]{1,0:T(8,128)S(1)}, u32[]{:S(2)}, u32[]{:S(2)}) %collective-permute-start) | collective-permute-done | bytes 1048608 | tf_op jit(solution)/shard_map/ppermute | solution.py:278
  161.1 0.0 all-to-all-done
  161.1 5.6 %edge_step.1 = (f32[1,256]{1,0:T(1,128)}, f32[640,256]{1,0:T(8,128)S(1)}, f32[256,256]{1,0:T(8,128)S(1)}, f32[256,1024]{1,0:T(8,128)S(1)}) custom-call(s32[1,1]{1,0:T(1,128)S(6)} %copy.59.count_ref, s32[1,256]{1,0:T(1,128)} %bitcast.50, s32[1,256]{1,0:T(1,128)} %bitcast.55, s32[1,1024]{1,0:T(1,128)} %bitcast.58, f32[640,256]{1,0:T(8,128)S(1)} %bitcast.42, ...), custom_call_target="tpu_custom_call" | custom-call | tf_op jit(solution)/shard_map/edge_step/pallas_call | solution.py:159
  166.7 0.0 copy-start.3
  166.7 0.9 copy-done.3
  167.6 0.0 copy-start.4
  167.6 0.7 copy-done.4
  168.3 25.1 %all-to-all-start.1 = ((f32[16,40,256]{2,1,0:T(8,128)}), f32[16,40,256]{2,1,0:T(8,128)S(1)}, u32[]{:S(2)}, u32[]{:S(2)}) async-start(f32[16,40,256]{2,1,0:T(8,128)} %bitcast.44), calls=%async_computation.1 | async-start | bytes 1310720 | tf_op jit(solution)/shard_map/all_to_all | solution.py:290
  193.4 0.0 copy-done.14
  193.4 1.9 collective-permute-start.1
  195.4 0.1 convert_reduce_fusion
  195.5 0.0 copy-done.1
  195.5 0.9 copy.29
  196.4 0.6 reduce_max.18
  197.7 0.0 copy-done.6
  197.7 0.0 copy-start.11
  197.7 0.0 copy-start.12
  197.7 0.0 copy-start.13
  197.7 1.3 copy.30
  199.0 23.2 %collective-permute-done.1 = f32[1024]{0:T(1024)S(1)} collective-permute-done((f32[1024]{0:T(1024)S(1)}, f32[1024]{0:T(1024)S(1)}, u32[]{:S(2)}, u32[]{:S(2)}) %collective-permute-start.1) | collective-permute-done | bytes 4128 | tf_op jit(solution)/shard_map/ppermute | solution.py:279
  222.2 0.0 copy-start.5
  222.2 0.9 copy-done.5
  223.2 1.9 table_step.1
  225.1 0.0 copy-start.2
  225.1 1.0 copy-done.2
  226.1 0.0 copy-start.7
  226.1 0.0 copy-start.9
  226.1 2.6 %copy.28 = f32[1024,256]{0,1:T(8,128)} copy(f32[1024,256]{1,0:T(8,128)} %copy-done.2) | data formatting | bytes 2097152 | tf_op jit(solution)/shard_map/while | solution.py:301
  228.7 0.0 all-to-all-done.1
  228.7 1.1 source_step.1
  229.8 1.0 copy.27
  230.8 0.6 reduce
  231.4 0.0 copy-done.11
  231.4 0.0 copy-done.12
  231.4 0.0 copy-done.13
  231.4 0.0 copy-done.7
  231.4 0.0 copy-done.9
  231.4 0.2 while.17
  231.7 2.5 %copy.32 = f32[1024,256]{1,0:T(8,128)} copy(f32[1024,256]{0,1:T(8,128)} %get-tuple-element.279) | data formatting | bytes 2097152 | tf_op jit(solution)/shard_map/while | solution.py:301
  234.2 1.9 copy.31
  236.1 1.2 broadcast_in_dim.25
  (3 shorter events, 0.0 us)
Async XLA Ops:
  7.2 186.2 %copy-start.14 = (f32[1,1,1024]{2,1,0:T(1,128)S(1)}, f32[1,1,1024]{2,1,0:T(1,128)}, u32[]{:S(2)}) copy-start(f32[1,1,1024]{2,1,0:T(1,128)} %param.13) | copy-start | bytes 12292
  7.2 190.5 %copy-start.6 = (f32[1,1,384]{2,1,0:T(1,128)S(1)}, f32[1,1,384]{2,1,0:T(1,128)}, u32[]{:S(2)}) copy-start(f32[1,1,384]{2,1,0:T(1,128)} %param.11) | copy-start | bytes 4612
  35.2 1.0 copy-start
  36.2 159.3 %copy-start.1 = (f32[1,1,384,256]{3,2,1,0:T(8,128)S(1)}, f32[1,1,384,256]{3,2,1,0:T(8,128)}, u32[]{:S(2)}) copy-start(f32[1,1,384,256]{3,2,1,0:T(8,128)} %param.10) | copy-start | bytes 1179652
  38.2 123.0 %all-to-all-start = ((f32[16,40,256]{2,1,0:T(8,128)}), f32[16,40,256]{2,1,0:T(8,128)S(1)}, u32[]{:S(2)}, u32[]{:S(2)}) async-start(f32[16,40,256]{2,1,0:T(8,128)} %bitcast.9), calls=%async_computation | async-start | bytes 1310720 | tf_op jit(solution)/shard_map/all_to_all | solution.py:286
  49.6 111.5 %collective-permute-start = (f32[1024,256]{1,0:T(8,128)}, f32[1024,256]{1,0:T(8,128)S(1)}, u32[]{:S(2)}, u32[]{:S(2)}) collective-permute-start(f32[1024,256]{1,0:T(8,128)} %bitcast.61), channel_id=1, source_target_pairs={{0,1},{1,2},{2,3},{3,4},{4,5},{5,6},{6,7},{7,8},{8,9},{9,10},{10,1... | collective-permute-start | bytes 3145736 | tf_op jit(solution)/shard_map/ppermute | solution.py:278
  166.7 0.9 copy-start.3
  167.6 0.7 copy-start.4
  168.3 60.4 %all-to-all-start.1 = ((f32[16,40,256]{2,1,0:T(8,128)}), f32[16,40,256]{2,1,0:T(8,128)S(1)}, u32[]{:S(2)}, u32[]{:S(2)}) async-start(f32[16,40,256]{2,1,0:T(8,128)} %bitcast.44), calls=%async_computation.1 | async-start | bytes 1310720 | tf_op jit(solution)/shard_map/all_to_all | solution.py:290
  193.4 28.8 %collective-permute-start.1 = (f32[1024]{0:T(1024)S(1)}, f32[1024]{0:T(1024)S(1)}, u32[]{:S(2)}, u32[]{:S(2)}) collective-permute-start(f32[1024]{0:T(1024)S(1)} %bitcast.62), channel_id=1, source_target_pairs={{0,1},{1,2},{2,3},{3,4},{4,5},{5,6},{6,7},{7,8},{8,9},{9,10},{10,1... | collective-permute-start | bytes 12296 | tf_op jit(solution)/shard_map/ppermute | solution.py:279
  197.7 33.7 %copy-start.11 = (s32[1,1,256]{2,1,0:T(1,128)S(1)}, s32[1,1,256]{2,1,0:T(1,128)}, u32[]{:S(2)}) copy-start(s32[1,1,256]{2,1,0:T(1,128)} %param.14) | copy-start | bytes 3076
  197.7 33.7 %copy-start.12 = (s32[1,1,256]{2,1,0:T(1,128)S(1)}, s32[1,1,256]{2,1,0:T(1,128)}, u32[]{:S(2)}) copy-start(s32[1,1,256]{2,1,0:T(1,128)} %param.15) | copy-start | bytes 3076
  197.7 33.7 %copy-start.13 = (s32[1,1,1024]{2,1,0:T(1,128)S(1)}, s32[1,1,1024]{2,1,0:T(1,128)}, u32[]{:S(2)}) copy-start(s32[1,1,1024]{2,1,0:T(1,128)} %param.16) | copy-start | bytes 12292
  222.2 1.0 copy-start.5
  225.1 1.0 copy-start.2
  226.1 5.4 %copy-start.7 = (f32[1024,256]{0,1:T(8,128)S(1)}, f32[1024,256]{0,1:T(8,128)}, u32[]{:S(2)}) copy-start(f32[1024,256]{0,1:T(8,128)} %copy.30) | copy-start | bytes 3145732
  226.1 5.4 %copy-start.9 = (f32[384,256]{0,1:T(8,128)S(1)}, f32[384,256]{0,1:T(8,128)}, u32[]{:S(2)}) copy-start(f32[384,256]{0,1:T(8,128)} %copy.29) | copy-start | bytes 1179652

commit v2 on v1

--- a/solution.py
+++ b/solution.py
@@ -1,13 +1,16 @@
 import functools
+import math
 
 import jax
 import jax.numpy as jnp
 from jax import lax
 from jax.experimental import pallas as pl
 from jax.experimental.pallas import tpu as pltpu
-from jax.sharding import PartitionSpec as P
+from jax.sharding import Mesh, PartitionSpec as P
 
 SLOTS = 40
+LEAVE = ((-1, -1), (-1, 0), (0, -1), (-1, -2), (-2, -1))
+LAND = ((0, 0), (-1, 0), (0, -1), (0, 1), (1, 0))
 F32 = jnp.float32
 BF16 = jnp.bfloat16
 VMEM = pl.BlockSpec(memory_space=pltpu.VMEM)
@@ -95,9 +98,17 @@
 
 
 def edge_kernel(
-    devices, own, slots, count_ref, ids_ref, dest_ref, negative_ref, got_ref, table_ref,
-    loss_ref, back_ref, source_ref, weight_ref,
+    devices, own, slots, starts, count_ref, crossed_ref, ids_ref, dest_ref, negative_ref, got_ref, near_ref, *refs
 ):
+    joined = refs[: len(starts)]
+    loss_ref, back_ref, source_ref, weight_ref, table_ref = refs[len(starts) :]
+    table_ref[...] = near_ref[...]
+
+    @pl.when(crossed_ref[0] == 1)
+    def _():
+        for start, piece in zip(starts, joined):
+            table_ref[start : start + piece.shape[0]] = piece[...]
+
     edges = ids_ref.shape[1]
     height = table_ref.shape[0]
     ids = ids_ref[...]
@@ -152,23 +163,24 @@
     back_ref[...] = pick(flag(down == place).astype(BF16), parts_of(grad, 3))
 
 
-def edge_step(count, ids, dest, negative, got, table, devices, own):
+def edge_step(count, crossed, ids, dest, negative, got, table, joined, starts, devices, own):
     slots = got.shape[0] // devices
     edges = ids.shape[1]
     height, width = table.shape
     return pl.pallas_call(
-        functools.partial(edge_kernel, devices, own, slots),
+        functools.partial(edge_kernel, devices, own, slots, tuple(starts)),
         out_shape=(
             jax.ShapeDtypeStruct((1, edges), F32),
             jax.ShapeDtypeStruct(got.shape, F32),
             jax.ShapeDtypeStruct((edges, width), F32),
             jax.ShapeDtypeStruct((edges, height), F32),
+            jax.ShapeDtypeStruct(table.shape, F32),
         ),
-        in_specs=[SMEM] + [VMEM] * 5,
-        out_specs=(VMEM,) * 4,
+        in_specs=[SMEM] * 2 + [VMEM] * (5 + len(joined)),
+        out_specs=(VMEM,) * 5,
         compiler_params=pltpu.CompilerParams(vmem_limit_bytes=48 << 20),
         name="edge_step",
-    )(count, ids, dest, negative, got, table)
+    )(count, crossed, ids, dest, negative, got, table, *joined)
 
 
 def row_of(column):
@@ -185,23 +197,32 @@
     return emb_new, row_of(state_new)
 
 
-def table_kernel(weight_ref, source_ref, table_ref, state_ref, new_ref, state_new_ref):
+def table_kernel(
+    own, weight_ref, source_ref, table_ref, state_ref, ids_ref, new_ref, state_new_ref, used_ref
+):
+    ids = ids_ref[...]
+    most = jnp.zeros((ids.shape[0], 1), F32)
+    for device in range(ids.shape[0]):
+        mine = flag((ids >= device * own) & (ids < (device + 1) * own))
+        most = jnp.maximum(most, jnp.sum(mine, axis=1, keepdims=True))
+    used_ref[...] = jnp.max(most, axis=0, keepdims=True)
     grad = product(parts_of(weight_ref[...], 2), parts_of(source_ref[...], 2), FIRST)
     new_ref[...], state_new_ref[...] = adagrad_rows(table_ref[...], state_ref[...], grad)
 
 
-def table_step(weight, source, table, state):
-    return pl.pallas_call(
-        table_kernel,
+def table_step(weight, source, table, state, ids, own):
+    return pl.pallas_call(
+        functools.partial(table_kernel, own),
         out_shape=(
             jax.ShapeDtypeStruct(table.shape, F32),
             jax.ShapeDtypeStruct(state.shape, F32),
+            jax.ShapeDtypeStruct((1, 1), F32),
         ),
-        in_specs=[VMEM] * 4,
-        out_specs=(VMEM, VMEM),
+        in_specs=[VMEM] * 5,
+        out_specs=(VMEM,) * 3,
         compiler_params=pltpu.CompilerParams(vmem_limit_bytes=48 << 20),
         name="table_step",
-    )(weight, source, table, state)
+    )(weight, source, table, state, ids)
 
 
 def source_kernel(local_ref, back_ref, rows_ref, state_ref, new_ref, state_new_ref):
@@ -230,14 +251,45 @@
     return lax.dot_general(left, right, dims, precision=lax.Precision.HIGHEST, preferred_element_type=F32)
 
 
-def adagrad(emb, state, grad):
-    state_new = state + jnp.mean(grad * grad, axis=-1)
-    emb_new = emb - 0.1 * grad / (jnp.sqrt(state_new)[:, None] + 1e-10)
-    return emb_new, state_new
+def held_kernel(rows_ref, table_ref, rows_out, table_out):
+    rows_out[...] = rows_ref[...]
+    table_out[...] = table_ref[...]
+
+
+def held(rows, table):
+    return pl.pallas_call(
+        held_kernel,
+        out_shape=(jax.ShapeDtypeStruct(rows.shape, F32), jax.ShapeDtypeStruct(table.shape, F32)),
+        in_specs=[VMEM] * 2,
+        out_specs=(VMEM, VMEM),
+        compiler_params=pltpu.CompilerParams(vmem_limit_bytes=40 << 20),
+        name="held",
+    )(rows, table)
+
+
+def update_kernel(emb_ref, state_ref, grad_ref, new_ref, state_new_ref):
+    new_ref[...], state_new_ref[...] = adagrad_rows(emb_ref[...], state_ref[...], grad_ref[...])
+
+
+def update(emb, state, grad):
+    return pl.pallas_call(
+        update_kernel,
+        out_shape=(jax.ShapeDtypeStruct(emb.shape, F32), jax.ShapeDtypeStruct(state.shape, F32)),
+        in_specs=[VMEM] * 3,
+        out_specs=(VMEM, VMEM),
+        compiler_params=pltpu.CompilerParams(vmem_limit_bytes=40 << 20),
+        name="update",
+    )(emb, state, grad)
+
+
+def everywhere(value):
+    copies = jnp.broadcast_to(value, (lax.axis_size("src"),) + value.shape)
+    return lax.all_to_all(copies, "src", 0, 0, tiled=True).reshape(-1, value.shape[-1])
 
 
 def whole_step(rows, rows_state, table, table_state, ids, all_ids, dest, negative, count, first):
-    piece = lax.all_gather(rows, "src", axis=0, tiled=True)
+    rows, table = held(rows, table)
+    piece = everywhere(rows)
     columns = jnp.arange(piece.shape[0], dtype=jnp.int32)
     sources = exact((ids[:, None] == columns[None, :]).astype(F32), piece)
     index = jnp.arange(table.shape[0], dtype=jnp.int32)
@@ -257,53 +309,84 @@
     source_grad = dpos[:, None] * targets + exact(dneg, negatives)
     dest_grad = exact(hot_dest, dpos[:, None] * sources, FIRST)
     dest_grad = dest_grad + exact(hot_negative, exact(dneg, sources, FIRST), FIRST)
-    grad_piece = lax.all_gather(source_grad, "src", axis=0, tiled=True)
+    grad_piece = everywhere(source_grad)
     own_index = first + jnp.arange(rows.shape[0], dtype=jnp.int32)
     onehot = (all_ids.reshape(-1)[:, None] == own_index[None, :]).astype(F32)
     own_grad = exact(onehot, grad_piece, FIRST)
-    new, new_state = adagrad(rows, rows_state, own_grad)
-    table_new, table_state_new = adagrad(table, table_state, dest_grad)
-    return new, new_state, table_new, table_state_new, loss
+    return update(rows, rows_state, own_grad) + update(table, table_state, dest_grad) + (loss[None],)
+
+
+def after(value, *others):
+    return lax.optimization_barrier((value,) + others)[0]
+
+
+def permute(value, axes, pairs):
+    return lax.ppermute(value, axes, pairs)
+
+
+def shifted(table):
+    height = table.shape[0]
+    wide, deep = lax.axis_size("x"), lax.axis_size("y")
+    plane = wide * deep
+    count = len(LEAVE)
+    size = -(-height // (8 * count)) * 8
+    starts = [min(size * piece, height - size) for piece in range(count)]
+    spot = lambda at: (at[0] % wide) * deep + at[1] % deep
+    leave, land = [spot(at) for at in LEAVE], [spot(at) for at in LAND]
+    near = permute(
+        table, ("zh", "x", "y"), [(j, j + 1) for j in range(2 * plane - 1) if j != plane - 1]
+    )
+    pieces = [table[start : start + size] for start in starts]
+    spread = [permute(pieces[k], ("x", "y"), [(leave[0], leave[k])]) for k in range(1, count)]
+    at = lax.axis_index("x") * deep + lax.axis_index("y")
+    going = jnp.where(at == leave[0], pieces[0], sum(spread))
+    come = permute(
+        going,
+        ("zh", "x", "y"),
+        [(z * plane + leave[k], (1 - z) * plane + land[k]) for z in range(2) for k in range(count)],
+    )
+    joined = [come] + [permute(come, ("x", "y"), [(land[k], land[0])]) for k in range(1, count)]
+    return near, joined, starts, (at == land[0]).astype(jnp.int32), going
 
 
 def on_device(src_emb, src_state, dst_emb, dst_state, src_ids, dst_ids, neg_ids, counts):
     devices = lax.axis_size("src")
-    behind = lax.axis_size("dst")
+    behind = lax.axis_size("zh") * lax.axis_size("x") * lax.axis_size("y")
     pairs = [(source, (source + 1) % behind) for source in range(behind)]
-    rows, rows_state = src_emb[0, 0], src_state[0, 0]
+    rows, rows_state = src_emb[0, 0], src_state[0]
     own, width = rows.shape
-    ids = src_ids[0, 0]
+    ids = src_ids[0]
     first = lax.axis_index("src") * own
-    all_ids = lax.all_gather(ids, "src", axis=0, tiled=False)
-    table = lax.ppermute(dst_emb[0, 0], "dst", pairs)
-    table_state = lax.ppermute(dst_state[0, 0], "dst", pairs)
-
-    owner = lax.broadcasted_iota(jnp.int32, (1, devices, 1), 1)
-    used = jnp.sum((all_ids[:, None, :] // own == owner).astype(F32), axis=2)
-    over = jnp.max(used) > SLOTS
+    all_ids = lax.all_to_all(jnp.broadcast_to(ids, (devices, ids.shape[1])), "src", 0, 0, tiled=True)
+    near, joined, starts, crossed, going = shifted(dst_emb[0, 0])
 
     send, local = pack_rows(first.reshape(1), all_ids, rows, SLOTS)
-    got = lax.all_to_all(send, "src", 0, 0, tiled=True)
-    loss, back, source, weight = edge_step(
-        counts, src_ids[0], dst_ids[0], neg_ids[0], got, table, devices, own
+    table_state = permute(after(dst_state[0], local), ("zh", "x", "y"), pairs)
+    got = lax.all_to_all(after(send, going), "src", 0, 0, tiled=True)
+    loss, back, source, weight, table = edge_step(
+        counts, crossed.reshape(1), ids, dst_ids[0], neg_ids[0], got, near, joined, starts, devices, own
     )
     back = lax.all_to_all(back, "src", 0, 0, tiled=True)
-    dst_new, dst_state_new = table_step(weight, source, table, table_state[None])
-    src_new, src_state_new = source_step(local, back, rows, rows_state[None])
+    dst_new, dst_state_new, over = table_step(weight, source, table, table_state, all_ids, own)
+    src_new, src_state_new = source_step(local, back, rows, rows_state)
 
     def again(carry):
         found = whole_step(
-            rows, rows_state, table, table_state, ids, all_ids, dst_ids[0, 0], neg_ids[0, 0], counts[0, 0], first
+            rows, rows_state, table, table_state, ids[0], all_ids, dst_ids[0, 0], neg_ids[0, 0], counts[0, 0], first
         )
-        return (jnp.bool_(False),) + found
-
-    fast = (over, src_new, src_state_new[0], dst_new, dst_state_new[0], loss[0])
-    done = lax.while_loop(lambda carry: carry[0], again, fast)
-    return tuple(value[None, None] for value in done[1:])
+        return (jnp.float32(0.0),) + found
+
+    fast = (over[0, 0], src_new, src_state_new, dst_new, dst_state_new, loss)
+    done = lax.while_loop(lambda carry: carry[0] > SLOTS, again, fast)
+    src_new, src_state_new, dst_new, dst_state_new, loss = done[1:]
+    return src_new[None, None], src_state_new[None], dst_new[None, None], dst_state_new[None], loss[None]
 
 
 def solution(mesh):
-    spec = lambda rank: P("src", "dst", *([None] * (rank - 2)))
+    sources, dests = mesh.devices.shape
+    side = int(math.isqrt(dests // 2))
+    mesh = Mesh(mesh.devices.reshape(sources, 2, side, side), ("src", "zh", "x", "y"))
+    spec = lambda rank: P("src", ("zh", "x", "y"), *([None] * (rank - 2)))
     return jax.shard_map(
         on_device,
         mesh=mesh,

time: 245 us -> 166 us (0.68)
  the two profiles are of different devices: /device:TPU:64 before, /device:TPU:33 now
where the time goes in v2:
time: 166 us; the launch traced here: 165 us
  starting transfers between devices  73.6 us (44%)
  waiting for transfers between devices  63.1 us (38%)
  Pallas kernels  15.5 us (9%)
  local copies, waits for them, and re-layouts  9.69 us (6%)
    ppermute x11, waiting for transfers between devices, permute(): return lax.ppermute(value, axes, pairs)  42.9 us
    all_to_all x1, starting transfers between devices, on_device(): back = lax.all_to_all(back, 'src', 0, 0, tiled=True)  41.3 us
    ppermute x11, starting transfers between devices, permute(): return lax.ppermute(value, axes, pairs)  14.3 us
    all_to_all x1, starting transfers between devices, on_device(): lax.all_to_all(jnp.broadcast_to(ids, (devices, ids.shape[1])), 'src', 0,...  13 us
    all_to_all x1, waiting for transfers between devices, on_device(): back = lax.all_to_all(back, 'src', 0, 0, tiled=True)  11.3 us
    all_to_all x1, waiting for transfers between devices, on_device(): lax.all_to_all(jnp.broadcast_to(ids, (devices, ids.shape[1])), 'src', 0,...  8.89 us
    unnamed x19, local copies, waits for them, and re-layouts  7.09 us
    pallas_call x1, Pallas kernels, edge_step(): pl.pallas_call(functools.partial(edge_kernel, devices, own, slots, tuple(...  6.39 us
  transfers between devices with their start and end apart: 14, of which 6 were waited for; matrix products, arithmetic and copies ran while one was open for 1% of the time, Pallas kernels for 4%

profile of v2, /device:TPU:33, one launch (start us, length us, event | category | flops | bytes accessed | tf_op | source)
XLA Modules:
  0.0 165.3 jit_solution(9081238695623613214)
XLA Ops:
  0.6 1.3 slice_bitcast_fusion.2
  2.0 0.7 collective-permute-start
  2.6 0.7 collective-permute-start.1
  3.3 0.7 collective-permute-start.2
  4.0 0.7 collective-permute-start.3
  4.7 1.3 broadcast_in_dim.28
  6.0 13.0 %all-to-all-start.2 = ((s32[16,1,256]{2,1,0:T(1,128)}), s32[16,1,256]{2,1,0:T(1,128)S(1)}, u32[]{:S(2)}, u32[]{:S(2)}) async-start(s32[16,1,256]{2,1,0:T(1,128)} %broadcast_in_dim.28), calls=%async_computation.2 | async-start | bytes 32768 | tf_op jit(solution)/shard_map/all_to_all | solution.py:360
  18.9 8.9 %all-to-all-done.2 = s32[16,1,256]{2,1,0:T(1,128)S(1)} async-done(((s32[16,1,256]{2,1,0:T(1,128)}), s32[16,1,256]{2,1,0:T(1,128)S(1)}, u32[]{:S(2)}, u32[]{:S(2)}) %all-to-all-start.2) | async-done | bytes 16416 | tf_op jit(solution)/shard_map/all_to_all | solution.py:360
  27.8 0.0 copy-start.11
  27.8 0.6 copy-done.11
  28.4 3.0 %pack_rows.1 = (f32[640,256]{1,0:T(8,128)}, f32[640,1]{1,0:T(8,128)S(1)}) custom-call(s32[1]{0:T(128)} %bitcast.13.first_ref, s32[16,256]{1,0:T(8,128)S(1)} %bitcast.58, f32[384,256]{1,0:T(8,128)} %bitcast.55), custom_call_target="tpu_custom_call" | custom-call | tf_op jit(solution)/shard_map/pack_rows/pallas_call | solution.py:87
  31.4 0.0 collective-permute-done
  31.4 0.0 collective-permute-done.1
  31.4 0.0 collective-permute-done.2
  31.4 0.0 collective-permute-done.3
  31.4 1.0 bitcast_select_fusion
  32.4 5.0 %all-to-all-start.3 = ((f32[16,40,256]{2,1,0:T(8,128)}), f32[16,40,256]{2,1,0:T(8,128)S(1)}, u32[]{:S(2)}, u32[]{:S(2)}) async-start(f32[16,40,256]{2,1,0:T(8,128)} %bitcast.21), calls=%async_computation.3 | async-start | bytes 1310720 | tf_op jit(solution)/shard_map/all_to_all | solution.py:365
  37.5 3.3 %collective-permute-start.4 = (f32[1024,256]{1,0:T(8,128)}, f32[1024,256]{1,0:T(8,128)S(1)}, u32[]{:S(2)}, u32[]{:S(2)}) collective-permute-start(f32[1024,256]{1,0:T(8,128)} %bitcast.23), channel_id=1, source_target_pairs={{0,1},{1,2},{2,3},{3,4},{4,5},{5,6},{6,7},{7,8},{8,9},{9,10},{10,1... | collective-permute-start | bytes 3145736 | tf_op jit(solution)/shard_map/ppermute | solution.py:324
  40.7 1.3 collective-permute-start.5
  42.0 23.3 %collective-permute-done.5.refs_0_ = f32[208,256]{1,0:T(8,128)S(1)} collective-permute-done((f32[208,256]{1,0:T(8,128)S(1)}, f32[208,256]{1,0:T(8,128)S(1)}, u32[]{:S(2)}, u32[]{:S(2)}) %collective-permute-start.5) | collective-permute-done | bytes 213024 | tf_op jit(solution)/shard_map/ppermute | solution.py:324
  65.4 1.3 collective-permute-start.6
  66.6 1.3 collective-permute-start.7
  67.9 1.3 collective-permute-start.8
  69.2 1.3 collective-permute-start.9
  71.2 3.3 %collective-permute-done.6.refs_1_ = f32[208,256]{1,0:T(8,128)S(1)} collective-permute-done((f32[208,256]{1,0:T(8,128)S(1)}, f32[208,256]{1,0:T(8,128)S(1)}, u32[]{:S(2)}, u32[]{:S(2)}) %collective-permute-start.6) | collective-permute-done | bytes 213024 | tf_op jit(solution)/shard_map/ppermute | solution.py:324
  74.5 0.0 copy-start
  74.5 0.7 copy-done
  75.1 0.6 collective-permute-done.7.refs_2_
  75.8 0.0 copy-start.2
  75.8 0.7 copy-done.2
  76.5 0.0 collective-permute-done.8.refs_3_
  76.5 0.0 copy-start.4
  76.5 0.7 copy-done.4
  77.2 0.0 collective-permute-done.9.refs_4_
  77.2 0.0 copy-start.6
  77.2 0.7 copy-done.6
  77.8 0.0 collective-permute-done.4.near_ref
  77.8 0.0 all-to-all-done.3
  77.9 0.0 copy-start.1
  77.9 0.9 copy-done.1
  78.8 0.0 copy-start.3
  78.8 0.9 copy-done.3
  79.7 0.0 copy-start.5
  79.7 0.9 copy-done.5
  80.7 0.0 copy-start.7
  80.7 0.9 copy-done.7
  81.6 6.4 %edge_step.1 = (f32[1,256]{1,0:T(1,128)}, f32[640,256]{1,0:T(8,128)}, f32[256,256]{1,0:T(8,128)S(1)}, f32[256,1024]{1,0:T(8,128)S(1)}, f32[1024,256]{1,0:T(8,128)}) custom-call(s32[1,1]{1,0:T(1,128)S(6)} %copy.41.count_ref, s32[1]{0:T(128)} %bitcast.9.crossed_ref, s32[1,256]{1,0:T(1,128)} %bitcast.63, s32[1,256]{1,0:T(1,128)} %bitcast.69, ...), custom_call_target="tpu_custom_call" | custom-call | tf_op jit(solution)/shard_map/edge_step/pallas_call | solution.py:170
  88.0 41.3 %all-to-all-start.4 = ((f32[16,40,256]{2,1,0:T(8,128)}), f32[16,40,256]{2,1,0:T(8,128)S(1)}, u32[]{:S(2)}, u32[]{:S(2)}) async-start(f32[16,40,256]{2,1,0:T(8,128)} %bitcast.26), calls=%async_computation.4 | async-start | bytes 1310720 | tf_op jit(solution)/shard_map/all_to_all | solution.py:369
  129.2 1.9 %collective-permute-start.10 = (f32[1,1024]{1,0:T(1,128)}, f32[1,1024]{1,0:T(1,128)S(1)}, u32[]{:S(2)}, u32[]{:S(2)}) collective-permute-start(f32[1,1024]{1,0:T(1,128)} %bitcast.79), channel_id=1, source_target_pairs={{0,1},{1,2},{2,3},{3,4},{4,5},{5,6},{6,7},{7,8},{8,9},{9,10},{10,1... | collective-permute-start | bytes 12296 | tf_op jit(solution)/shard_map/ppermute | solution.py:324
  131.2 15.7 %collective-permute-done.10.state_ref = f32[1,1024]{1,0:T(1,128)S(1)} collective-permute-done((f32[1,1024]{1,0:T(1,128)}, f32[1,1024]{1,0:T(1,128)S(1)}, u32[]{:S(2)}, u32[]{:S(2)}) %collective-permute-start.10) | collective-permute-done | bytes 4128 | tf_op jit(solution)/shard_map/ppermute | solution.py:324
  146.8 3.2 %table_step.1 = (f32[1024,256]{1,0:T(8,128)}, f32[1,1024]{1,0:T(1,128)}, f32[1,1]{1,0:T(1,128)}) custom-call(f32[256,1024]{1,0:T(8,128)S(1)} %get-tuple-element.107.weight_ref, f32[256,256]{1,0:T(8,128)S(1)} %get-tuple-element.108.source_ref, f32[1024,256]{1,0:T(8,128)} %get-tuple-element.189.table_ref, f32[1,1024]{1,0:T(1,128)S(1)} %collective-permute-done.10.state_ref, ...), custom_call_target="tpu_custom_call" | custom-call | tf_op jit(solution)/shard_map/table_step/pallas_call | solution.py:214
  150.1 11.3 %all-to-all-done.4 = f32[16,40,256]{2,1,0:T(8,128)S(1)} async-done(((f32[16,40,256]{2,1,0:T(8,128)}), f32[16,40,256]{2,1,0:T(8,128)S(1)}, u32[]{:S(2)}, u32[]{:S(2)}) %all-to-all-start.4) | async-done | bytes 655392 | tf_op jit(solution)/shard_map/all_to_all | solution.py:369
  161.4 2.9 %source_step.1 = (f32[384,256]{1,0:T(8,128)}, f32[1,384]{1,0:T(1,128)}) custom-call(f32[640,1]{1,0:T(8,128)S(1)} %get-tuple-element.110.local_ref, f32[640,256]{1,0:T(8,128)S(1)} %bitcast.53, f32[384,256]{1,0:T(8,128)} %bitcast.56, f32[1,384]{1,0:T(1,128)} %bitcast.72), custom_call_target="tpu_custom_call" | custom-call | tf_op jit(solution)/shard_map/source_step/pallas_call | solution.py:237
  164.2 0.9 while.17
  (1 shorter events, 0.0 us)
Async XLA Ops:
  2.0 29.5 %collective-permute-start = (f32[208,256]{1,0:T(8,128)S(1)}, f32[208,256]{1,0:T(8,128)S(1)}, u32[]{:S(2)}, u32[]{:S(2)}) collective-permute-start(f32[208,256]{1,0:T(8,128)S(1)} %get-tuple-element.164), channel_id=1, source_target_pairs={{15,12},{31,28},{47,44},{63,60},{79,76},{95,92},{111,108},{127,124... | collective-permute-start | bytes 638984 | tf_op jit(solution)/shard_map/ppermute | solution.py:324
  2.6 28.8 %collective-permute-start.1 = (f32[208,256]{1,0:T(8,128)S(1)}, f32[208,256]{1,0:T(8,128)S(1)}, u32[]{:S(2)}, u32[]{:S(2)}) collective-permute-start(f32[208,256]{1,0:T(8,128)S(1)} %get-tuple-element.162), channel_id=1, source_target_pairs={{15,3},{31,19},{47,35},{63,51},{79,67},{95,83},{111,99},{127,115},... | collective-permute-start | bytes 638984 | tf_op jit(solution)/shard_map/ppermute | solution.py:324
  3.3 28.1 %collective-permute-start.2 = (f32[208,256]{1,0:T(8,128)S(1)}, f32[208,256]{1,0:T(8,128)S(1)}, u32[]{:S(2)}, u32[]{:S(2)}) collective-permute-start(f32[208,256]{1,0:T(8,128)S(1)} %get-tuple-element.163), channel_id=1, source_target_pairs={{15,14},{31,30},{47,46},{63,62},{79,78},{95,94},{111,110},{127,126... | collective-permute-start | bytes 638984 | tf_op jit(solution)/shard_map/ppermute | solution.py:324
  4.0 27.4 %collective-permute-start.3 = (f32[208,256]{1,0:T(8,128)S(1)}, f32[208,256]{1,0:T(8,128)S(1)}, u32[]{:S(2)}, u32[]{:S(2)}) collective-permute-start(f32[208,256]{1,0:T(8,128)S(1)} %get-tuple-element.165), channel_id=1, source_target_pairs={{15,11},{31,27},{47,43},{63,59},{79,75},{95,91},{111,107},{127,123... | collective-permute-start | bytes 638984 | tf_op jit(solution)/shard_map/ppermute | solution.py:324
  6.0 21.8 %all-to-all-start.2 = ((s32[16,1,256]{2,1,0:T(1,128)}), s32[16,1,256]{2,1,0:T(1,128)S(1)}, u32[]{:S(2)}, u32[]{:S(2)}) async-start(s32[16,1,256]{2,1,0:T(1,128)} %broadcast_in_dim.28), calls=%async_computation.2 | async-start | bytes 32768 | tf_op jit(solution)/shard_map/all_to_all | solution.py:360
  27.8 0.6 copy-start.11
  32.4 45.4 %all-to-all-start.3 = ((f32[16,40,256]{2,1,0:T(8,128)}), f32[16,40,256]{2,1,0:T(8,128)S(1)}, u32[]{:S(2)}, u32[]{:S(2)}) async-start(f32[16,40,256]{2,1,0:T(8,128)} %bitcast.21), calls=%async_computation.3 | async-start | bytes 1310720 | tf_op jit(solution)/shard_map/all_to_all | solution.py:365
  37.5 40.4 %collective-permute-start.4 = (f32[1024,256]{1,0:T(8,128)}, f32[1024,256]{1,0:T(8,128)S(1)}, u32[]{:S(2)}, u32[]{:S(2)}) collective-permute-start(f32[1024,256]{1,0:T(8,128)} %bitcast.23), channel_id=1, source_target_pairs={{0,1},{1,2},{2,3},{3,4},{4,5},{5,6},{6,7},{7,8},{8,9},{9,10},{10,1... | collective-permute-start | bytes 3145736 | tf_op jit(solution)/shard_map/ppermute | solution.py:324
  40.7 24.6 %collective-permute-start.5 = (f32[208,256]{1,0:T(8,128)S(1)}, f32[208,256]{1,0:T(8,128)S(1)}, u32[]{:S(2)}, u32[]{:S(2)}) collective-permute-start(f32[208,256]{1,0:T(8,128)S(1)} %bitcast_select_fusion), channel_id=1, source_target_pairs={{15,16},{12,28},{3,19},{14,17},{11,20},{31,0},{28,12},{19,3},{30,1... | collective-permute-start | bytes 638984 | tf_op jit(solution)/shard_map/ppermute | solution.py:324
  65.4 9.1 %collective-permute-start.6 = (f32[208,256]{1,0:T(8,128)S(1)}, f32[208,256]{1,0:T(8,128)S(1)}, u32[]{:S(2)}, u32[]{:S(2)}) collective-permute-start(f32[208,256]{1,0:T(8,128)S(1)} %collective-permute-done.5.refs_0_), channel_id=1, source_target_pairs={{12,0},{28,16},{44,32},{60,48},{76,64},{92,80},{108,96},{124,112},... | collective-permute-start | bytes 638984 | tf_op jit(solution)/shard_map/ppermute | solution.py:324
  66.6 9.1 %collective-permute-start.7 = (f32[208,256]{1,0:T(8,128)S(1)}, f32[208,256]{1,0:T(8,128)S(1)}, u32[]{:S(2)}, u32[]{:S(2)}) collective-permute-start(f32[208,256]{1,0:T(8,128)S(1)} %collective-permute-done.5.refs_0_), channel_id=1, source_target_pairs={{3,0},{19,16},{35,32},{51,48},{67,64},{83,80},{99,96},{115,112},{1... | collective-permute-start | bytes 638984 | tf_op jit(solution)/shard_map/ppermute | solution.py:324
  67.9 8.5 %collective-permute-start.8 = (f32[208,256]{1,0:T(8,128)S(1)}, f32[208,256]{1,0:T(8,128)S(1)}, u32[]{:S(2)}, u32[]{:S(2)}) collective-permute-start(f32[208,256]{1,0:T(8,128)S(1)} %collective-permute-done.5.refs_0_), channel_id=1, source_target_pairs={{1,0},{17,16},{33,32},{49,48},{65,64},{81,80},{97,96},{113,112},{1... | collective-permute-start | bytes 638984 | tf_op jit(solution)/shard_map/ppermute | solution.py:324
  69.2 7.9 %collective-permute-start.9 = (f32[208,256]{1,0:T(8,128)S(1)}, f32[208,256]{1,0:T(8,128)S(1)}, u32[]{:S(2)}, u32[]{:S(2)}) collective-permute-start(f32[208,256]{1,0:T(8,128)S(1)} %collective-permute-done.5.refs_0_), channel_id=1, source_target_pairs={{4,0},{20,16},{36,32},{52,48},{68,64},{84,80},{100,96},{116,112},{... | collective-permute-start | bytes 638984 | tf_op jit(solution)/shard_map/ppermute | solution.py:324
  74.5 0.7 copy-start
  75.8 0.7 copy-start.2
  76.5 0.7 copy-start.4
  77.2 0.7 copy-start.6
  77.9 0.9 copy-start.1
  78.8 0.9 copy-start.3
  79.7 0.9 copy-start.5
  80.7 0.9 copy-start.7
  88.0 73.4 %all-to-all-start.4 = ((f32[16,40,256]{2,1,0:T(8,128)}), f32[16,40,256]{2,1,0:T(8,128)S(1)}, u32[]{:S(2)}, u32[]{:S(2)}) async-start(f32[16,40,256]{2,1,0:T(8,128)} %bitcast.26), calls=%async_computation.4 | async-start | bytes 1310720 | tf_op jit(solution)/shard_map/all_to_all | solution.py:369
  129.2 17.6 %collective-permute-start.10 = (f32[1,1024]{1,0:T(1,128)}, f32[1,1024]{1,0:T(1,128)S(1)}, u32[]{:S(2)}, u32[]{:S(2)}) collective-permute-start(f32[1,1024]{1,0:T(1,128)} %bitcast.79), channel_id=1, source_target_pairs={{0,1},{1,2},{2,3},{3,4},{4,5},{5,6},{6,7},{7,8},{8,9},{9,10},{10,1... | collective-permute-start | bytes 12296 | tf_op jit(solution)/shard_map/ppermute | solution.py:324

commit v3 on v2

--- a/solution.py
+++ b/solution.py
@@ -8,9 +8,12 @@
 from jax.experimental.pallas import tpu as pltpu
 from jax.sharding import Mesh, PartitionSpec as P
 
-SLOTS = 40
-LEAVE = ((-1, -1), (-1, 0), (0, -1), (-1, -2), (-2, -1))
-LAND = ((0, 0), (-1, 0), (0, -1), (0, 1), (1, 0))
+SLOTS = 56
+BACK_SLOTS = 40
+LEAVE = ((-1, -1), (-1, 0), (0, -1), (-1, -2), (-2, -1), (0, 0))
+LAND = ((0, 0), (-1, 0), (0, -1), (0, 1), (1, 0), (1, 1))
+SRC = ("zl", "core")
+DST = ("zh", "x", "y")
 F32 = jnp.float32
 BF16 = jnp.bfloat16
 VMEM = pl.BlockSpec(memory_space=pltpu.VMEM)
@@ -60,68 +63,87 @@
     return jnp.sum(jnp.where(down == across, row, 0.0), axis=1, keepdims=True)
 
 
-def pack_rows_kernel(own, slots, first_ref, ids_ref, rows_ref, send_ref, local_ref):
-    devices, edges = ids_ref.shape
-    local = ids_ref[...] - first_ref[0]
-    owned = flag((local >= 0) & (local < own))
+def slot_column(rank, mark, slots):
+    slot = lax.broadcasted_iota(jnp.int32, (slots, rank.shape[1]), 0).astype(F32)
+    columns = []
+    for device in range(rank.shape[0]):
+        chosen = jnp.where(rank[device : device + 1] == slot, mark[device : device + 1], 0.0)
+        columns.append(jnp.sum(chosen, axis=1, keepdims=True))
+    return jnp.concatenate(columns, axis=0) - 1.0
+
+
+def rank_of(owned):
+    edges = owned.shape[1]
     down = lax.broadcasted_iota(jnp.int32, (edges, edges), 0)
     across = lax.broadcasted_iota(jnp.int32, (edges, edges), 1)
     rank = mxu(owned.astype(BF16), flag(down < across).astype(BF16))
-    rank = jnp.where(owned > 0.0, rank, -1.0)
-    mark = local.astype(F32) + 1.0
-    slot = lax.broadcasted_iota(jnp.int32, (slots, edges), 0).astype(F32)
-    columns = []
-    for device in range(devices):
-        chosen = jnp.where(rank[device : device + 1] == slot, mark[device : device + 1], 0.0)
-        columns.append(jnp.sum(chosen, axis=1, keepdims=True))
-    column = jnp.concatenate(columns, axis=0) - 1.0
-    local_ref[...] = column
-    across = lax.broadcasted_iota(jnp.int32, (devices * slots, own), 1).astype(F32)
+    return jnp.where(owned > 0.0, rank, -1.0)
+
+
+def pack_rows_kernel(slots, place_ref, ids_ref, rows_ref, other_ref, send_ref):
+    own = rows_ref.shape[0]
+    first, first_other = place_ref[0], place_ref[1]
+    pairs = [[ids_ref[core + 2 * chip : core + 2 * chip + 1] for chip in range(ids_ref.shape[0] // 2)] for core in (0, 1)]
+    ids = jnp.where(place_ref[2] == 0, jnp.concatenate(pairs[0], axis=0), jnp.concatenate(pairs[1], axis=0))
+    local, beside = ids - first, ids - first_other
+    mine = (local >= 0) & (local < own)
+    near = (beside >= 0) & (beside < own)
+    mark = jnp.where(mine, local + 1, beside + (own + 1)).astype(F32)
+    column = slot_column(rank_of(flag(mine | near)), mark, slots)
+    across = lax.broadcasted_iota(jnp.int32, (column.shape[0], own), 1).astype(F32)
     hot = flag(across == column).astype(BF16)
-    send_ref[...] = pick(hot, parts_of(rows_ref[...], 3))
-
-
-def pack_rows(first, ids, rows, slots):
-    devices = ids.shape[0]
-    own, width = rows.shape
-    return pl.pallas_call(
-        functools.partial(pack_rows_kernel, own, slots),
-        out_shape=(
-            jax.ShapeDtypeStruct((devices * slots, width), F32),
-            jax.ShapeDtypeStruct((devices * slots, 1), F32),
-        ),
-        in_specs=[SMEM, VMEM, VMEM],
-        out_specs=(VMEM, VMEM),
-        compiler_params=pltpu.CompilerParams(vmem_limit_bytes=40 << 20),
+    hot_other = flag(across == column - float(own)).astype(BF16)
+    rows, other = parts_of(rows_ref[...], 3), parts_of(other_ref[...], 3)
+    send_ref[...] = pick(hot, rows) + pick(hot_other, other)
+
+
+def pack_rows(place, ids, rows, other, slots):
+    chips = ids.shape[0] // 2
+    return pl.pallas_call(
+        functools.partial(pack_rows_kernel, slots),
+        out_shape=jax.ShapeDtypeStruct((chips * slots, rows.shape[1]), F32),
+        in_specs=[SMEM, VMEM, VMEM, VMEM],
+        out_specs=VMEM,
+        compiler_params=pltpu.CompilerParams(vmem_limit_bytes=16 << 20),
         name="pack_rows",
-    )(first, ids, rows)
-
-
-def edge_kernel(
-    devices, own, slots, starts, count_ref, crossed_ref, ids_ref, dest_ref, negative_ref, got_ref, near_ref, *refs
-):
-    joined = refs[: len(starts)]
-    loss_ref, back_ref, source_ref, weight_ref, table_ref = refs[len(starts) :]
-    table_ref[...] = near_ref[...]
-
-    @pl.when(crossed_ref[0] == 1)
-    def _():
-        for start, piece in zip(starts, joined):
-            table_ref[start : start + piece.shape[0]] = piece[...]
-
-    edges = ids_ref.shape[1]
-    height = table_ref.shape[0]
-    ids = ids_ref[...]
+    )(place, ids, rows, other)
+
+
+def place_of(ids, span, owners, slots):
+    edges = ids.shape[1]
     owner = jnp.zeros(ids.shape, F32)
-    for device in range(1, devices):
-        owner = owner + flag(ids >= device * own)
+    for device in range(1, owners):
+        owner = owner + flag(ids >= device * span)
+    owner = jnp.where(ids >= 0, owner, -1.0)
     down = lax.broadcasted_iota(jnp.int32, (edges, edges), 0)
     across = lax.broadcasted_iota(jnp.int32, (edges, edges), 1)
     before = flag((to_column(owner) == owner) & (down < across))
     rank = jnp.sum(before, axis=0, keepdims=True)
-    place = jnp.where(rank < slots, owner * slots + rank, -1.0)
-    place_column = to_column(place)
-    across = lax.broadcasted_iota(jnp.int32, (edges, devices * slots), 1).astype(F32)
+    return jnp.where((rank < slots) & (owner >= 0.0), owner * slots + rank, -1.0)
+
+
+def edge_kernel(
+    own, slots, back_slots, starts, count_ref, crossed_ref, ids_ref, dest_ref, negative_ref, got_ref, near_ref, *refs
+):
+    joined = refs[: len(starts)]
+    loss_ref, back_ref, source_ref, weight_ref, table_ref, done = refs[len(starts) :]
+    table_ref[...] = near_ref[...]
+
+    @pl.when(crossed_ref[0] == 1)
+    def _():
+        for start, piece in zip(starts, joined):
+            rows = table_ref.at[start : start + piece.shape[0]]
+            copy = pltpu.make_async_copy(piece, rows, done)
+            copy.start()
+            copy.wait()
+
+    edges = ids_ref.shape[1]
+    height = table_ref.shape[0]
+    ids = ids_ref[...]
+    got_rows, back_rows = got_ref.shape[0], back_ref.shape[0]
+    place_column = to_column(place_of(ids, 2 * own, got_rows // slots, slots))
+    place = place_of(ids, own, back_rows // back_slots, back_slots)
+    across = lax.broadcasted_iota(jnp.int32, (edges, got_rows), 1).astype(F32)
     source = pick(flag(across == place_column).astype(BF16), parts_of(got_ref[...], 3))
     source_ref[...] = source
 
@@ -159,26 +181,26 @@
     weight_ref[...] = weight
 
     grad = product(parts_of(weight, 2), table)
-    down = lax.broadcasted_iota(jnp.int32, (devices * slots, edges), 0).astype(F32)
+    down = lax.broadcasted_iota(jnp.int32, (back_rows, edges), 0).astype(F32)
     back_ref[...] = pick(flag(down == place).astype(BF16), parts_of(grad, 3))
 
 
 def edge_step(count, crossed, ids, dest, negative, got, table, joined, starts, devices, own):
-    slots = got.shape[0] // devices
     edges = ids.shape[1]
     height, width = table.shape
     return pl.pallas_call(
-        functools.partial(edge_kernel, devices, own, slots, tuple(starts)),
+        functools.partial(edge_kernel, own, SLOTS, BACK_SLOTS, tuple(starts)),
         out_shape=(
             jax.ShapeDtypeStruct((1, edges), F32),
-            jax.ShapeDtypeStruct(got.shape, F32),
+            jax.ShapeDtypeStruct((devices * BACK_SLOTS, width), F32),
             jax.ShapeDtypeStruct((edges, width), F32),
             jax.ShapeDtypeStruct((edges, height), F32),
             jax.ShapeDtypeStruct(table.shape, F32),
         ),
-        in_specs=[SMEM] * 2 + [VMEM] * (5 + len(joined)),
+        in_specs=[SMEM] * 2 + [VMEM] * 5 + [pl.BlockSpec(memory_space=pl.ANY)] * len(joined),
         out_specs=(VMEM,) * 5,
-        compiler_params=pltpu.CompilerParams(vmem_limit_bytes=48 << 20),
+        scratch_shapes=[pltpu.SemaphoreType.DMA],
+        compiler_params=pltpu.CompilerParams(vmem_limit_bytes=24 << 20),
         name="edge_step",
     )(count, crossed, ids, dest, negative, got, table, *joined)
 
@@ -198,31 +220,41 @@
 
 
 def table_kernel(
-    own, weight_ref, source_ref, table_ref, state_ref, ids_ref, new_ref, state_new_ref, used_ref
+    own, slots, back_slots, first_ref, weight_ref, source_ref, table_ref, state_ref, ids_ref,
+    new_ref, state_new_ref, used_ref, local_ref,
 ):
     ids = ids_ref[...]
-    most = jnp.zeros((ids.shape[0], 1), F32)
-    for device in range(ids.shape[0]):
-        mine = flag((ids >= device * own) & (ids < (device + 1) * own))
-        most = jnp.maximum(most, jnp.sum(mine, axis=1, keepdims=True))
+    devices = ids.shape[0]
+    most = jnp.zeros((devices, 1), F32)
+    for chip in range(devices // 2):
+        counts = []
+        for device in (2 * chip, 2 * chip + 1):
+            mine = flag((ids >= device * own) & (ids < (device + 1) * own))
+            counts.append(jnp.sum(mine, axis=1, keepdims=True))
+            most = jnp.maximum(most, counts[-1] - back_slots)
+        most = jnp.maximum(most, counts[0] + counts[1] - slots)
     used_ref[...] = jnp.max(most, axis=0, keepdims=True)
+    local = ids - first_ref[0]
+    rank = rank_of(flag((local >= 0) & (local < own)))
+    local_ref[...] = slot_column(rank, local.astype(F32) + 1.0, back_slots)
     grad = product(parts_of(weight_ref[...], 2), parts_of(source_ref[...], 2), FIRST)
     new_ref[...], state_new_ref[...] = adagrad_rows(table_ref[...], state_ref[...], grad)
 
 
-def table_step(weight, source, table, state, ids, own):
-    return pl.pallas_call(
-        functools.partial(table_kernel, own),
+def table_step(place, weight, source, table, state, ids, own):
+    return pl.pallas_call(
+        functools.partial(table_kernel, own, SLOTS, BACK_SLOTS),
         out_shape=(
             jax.ShapeDtypeStruct(table.shape, F32),
             jax.ShapeDtypeStruct(state.shape, F32),
             jax.ShapeDtypeStruct((1, 1), F32),
+            jax.ShapeDtypeStruct((ids.shape[0] * BACK_SLOTS, 1), F32),
         ),
-        in_specs=[VMEM] * 5,
-        out_specs=(VMEM,) * 3,
-        compiler_params=pltpu.CompilerParams(vmem_limit_bytes=48 << 20),
+        in_specs=[SMEM] + [VMEM] * 5,
+        out_specs=(VMEM,) * 4,
+        compiler_params=pltpu.CompilerParams(vmem_limit_bytes=24 << 20),
         name="table_step",
-    )(weight, source, table, state, ids)
+    )(place, weight, source, table, state, ids)
 
 
 def source_kernel(local_ref, back_ref, rows_ref, state_ref, new_ref, state_new_ref):
@@ -242,7 +274,7 @@
         ),
         in_specs=[VMEM] * 4,
         out_specs=(VMEM, VMEM),
-        compiler_params=pltpu.CompilerParams(vmem_limit_bytes=40 << 20),
+        compiler_params=pltpu.CompilerParams(vmem_limit_bytes=16 << 20),
         name="source_step",
     )(local, back, rows, state)
 
@@ -262,7 +294,7 @@
         out_shape=(jax.ShapeDtypeStruct(rows.shape, F32), jax.ShapeDtypeStruct(table.shape, F32)),
         in_specs=[VMEM] * 2,
         out_specs=(VMEM, VMEM),
-        compiler_params=pltpu.CompilerParams(vmem_limit_bytes=40 << 20),
+        compiler_params=pltpu.CompilerParams(vmem_limit_bytes=16 << 20),
         name="held",
     )(rows, table)
 
@@ -277,14 +309,14 @@
         out_shape=(jax.ShapeDtypeStruct(emb.shape, F32), jax.ShapeDtypeStruct(state.shape, F32)),
         in_specs=[VMEM] * 3,
         out_specs=(VMEM, VMEM),
-        compiler_params=pltpu.CompilerParams(vmem_limit_bytes=40 << 20),
+        compiler_params=pltpu.CompilerParams(vmem_limit_bytes=16 << 20),
         name="update",
     )(emb, state, grad)
 
 
 def everywhere(value):
-    copies = jnp.broadcast_to(value, (lax.axis_size("src"),) + value.shape)
-    return lax.all_to_all(copies, "src", 0, 0, tiled=True).reshape(-1, value.shape[-1])
+    copies = jnp.broadcast_to(value, (lax.axis_size(SRC),) + value.shape)
+    return lax.all_to_all(copies, SRC, 0, 0, tiled=True).reshape(-1, value.shape[-1])
 
 
 def whole_step(rows, rows_state, table, table_state, ids, all_ids, dest, negative, count, first):
@@ -329,12 +361,12 @@
     wide, deep = lax.axis_size("x"), lax.axis_size("y")
     plane = wide * deep
     count = len(LEAVE)
-    size = -(-height // (8 * count)) * 8
+    size = -(-height // (16 * count)) * 16
     starts = [min(size * piece, height - size) for piece in range(count)]
     spot = lambda at: (at[0] % wide) * deep + at[1] % deep
     leave, land = [spot(at) for at in LEAVE], [spot(at) for at in LAND]
     near = permute(
-        table, ("zh", "x", "y"), [(j, j + 1) for j in range(2 * plane - 1) if j != plane - 1]
+        table, DST, [(j, j + 1) for j in range(2 * plane - 1) if j != plane - 1]
     )
     pieces = [table[start : start + size] for start in starts]
     spread = [permute(pieces[k], ("x", "y"), [(leave[0], leave[k])]) for k in range(1, count)]
@@ -342,32 +374,38 @@
     going = jnp.where(at == leave[0], pieces[0], sum(spread))
     come = permute(
         going,
-        ("zh", "x", "y"),
+        DST,
         [(z * plane + leave[k], (1 - z) * plane + land[k]) for z in range(2) for k in range(count)],
     )
     joined = [come] + [permute(come, ("x", "y"), [(land[k], land[0])]) for k in range(1, count)]
-    return near, joined, starts, (at == land[0]).astype(jnp.int32), going
+    return near, joined, starts, (at == land[0]).astype(jnp.int32), going, come
 
 
 def on_device(src_emb, src_state, dst_emb, dst_state, src_ids, dst_ids, neg_ids, counts):
-    devices = lax.axis_size("src")
-    behind = lax.axis_size("zh") * lax.axis_size("x") * lax.axis_size("y")
+    devices = lax.axis_size(SRC)
+    behind = lax.axis_size(DST)
     pairs = [(source, (source + 1) % behind) for source in range(behind)]
     rows, rows_state = src_emb[0, 0], src_state[0]
-    own, width = rows.shape
+    own = rows.shape[0]
+    core = lax.axis_index("core")
+    first = lax.axis_index(SRC) * own
+    place = jnp.stack([first, first + own * (1 - 2 * core), core])
     ids = src_ids[0]
-    first = lax.axis_index("src") * own
-    all_ids = lax.all_to_all(jnp.broadcast_to(ids, (devices, ids.shape[1])), "src", 0, 0, tiled=True)
-    near, joined, starts, crossed, going = shifted(dst_emb[0, 0])
-
-    send, local = pack_rows(first.reshape(1), all_ids, rows, SLOTS)
-    table_state = permute(after(dst_state[0], local), ("zh", "x", "y"), pairs)
-    got = lax.all_to_all(after(send, going), "src", 0, 0, tiled=True)
+    edge = lax.broadcasted_iota(jnp.int32, ids.shape, 1)
+    ids = jnp.where(edge < counts[0, 0], ids, -1)
+    near, joined, starts, crossed, going, come = shifted(dst_emb[0, 0])
+    other = permute(rows, "core", [(0, 1), (1, 0)])
+    all_ids = jnp.broadcast_to(after(ids, going), (devices, ids.shape[1]))
+    all_ids = lax.all_to_all(all_ids, SRC, 0, 0, tiled=True)
+
+    send = pack_rows(place, all_ids, rows, other, SLOTS)
+    got = lax.all_to_all(after(send, come), "zl", 0, 0, tiled=True)
+    table_state = permute(after(dst_state[0], send), DST, pairs)
     loss, back, source, weight, table = edge_step(
         counts, crossed.reshape(1), ids, dst_ids[0], neg_ids[0], got, near, joined, starts, devices, own
     )
-    back = lax.all_to_all(back, "src", 0, 0, tiled=True)
-    dst_new, dst_state_new, over = table_step(weight, source, table, table_state, all_ids, own)
+    back = lax.all_to_all(back, SRC, 0, 0, tiled=True)
+    dst_new, dst_state_new, over, local = table_step(place, weight, source, table, table_state, all_ids, own)
     src_new, src_state_new = source_step(local, back, rows, rows_state)
 
     def again(carry):
@@ -377,16 +415,16 @@
         return (jnp.float32(0.0),) + found
 
     fast = (over[0, 0], src_new, src_state_new, dst_new, dst_state_new, loss)
-    done = lax.while_loop(lambda carry: carry[0] > SLOTS, again, fast)
+    done = lax.while_loop(lambda carry: carry[0] > 0.0, again, fast)
     src_new, src_state_new, dst_new, dst_state_new, loss = done[1:]
     return src_new[None, None], src_state_new[None], dst_new[None, None], dst_state_new[None], loss[None]
 
 
 def solution(mesh):
     sources, dests = mesh.devices.shape
-    side = int(math.isqrt(dests // 2))
-    mesh = Mesh(mesh.devices.reshape(sources, 2, side, side), ("src", "zh", "x", "y"))
-    spec = lambda rank: P("src", ("zh", "x", "y"), *([None] * (rank - 2)))
+    side = math.isqrt(dests // 2)
+    mesh = Mesh(mesh.devices.reshape(sources // 2, 2, 2, side, side), SRC + DST)
+    spec = lambda rank: P(SRC, DST, *([None] * (rank - 2)))
     return jax.shard_map(
         on_device,
         mesh=mesh,

time: 166 us -> 151 us (0.910)
  the two profiles are of different devices: /device:TPU:33 before, /device:TPU:64 now
where the time goes in v3:
time: 151 us; the launch traced here: 150 us
  waiting for transfers between devices  70.5 us (47%)
  starting transfers between devices  53.6 us (35%)
  Pallas kernels  16.8 us (11%)
  local copies, waits for them, and re-layouts  5.12 us (3%)
  other arithmetic  1.76 us (1%)
  between operations  1.7 us (1%)
    ppermute x14, waiting for transfers between devices, permute(): return lax.ppermute(value, axes, pairs)  62.5 us
    ppermute x14, starting transfers between devices, permute(): return lax.ppermute(value, axes, pairs)  21.7 us
    all_to_all x1, starting transfers between devices, on_device(): got = lax.all_to_all(after(send, come), 'zl', 0, 0, tiled=True)  13 us
    all_to_all x1, starting transfers between devices, on_device(): back = lax.all_to_all(back, SRC, 0, 0, tiled=True)  9.93 us
    all_to_all x1, starting transfers between devices, on_device(): all_ids = lax.all_to_all(all_ids, SRC, 0, 0, tiled=True)  9.03 us
    all_to_all x1, waiting for transfers between devices, on_device(): all_ids = lax.all_to_all(all_ids, SRC, 0, 0, tiled=True)  7.96 us
    pallas_call x1, Pallas kernels, edge_step(): pl.pallas_call(functools.partial(edge_kernel, own, SLOTS, BACK_SLOTS, tup...  7.59 us
    pallas_call x1, Pallas kernels, table_step(): pl.pallas_call(functools.partial(table_kernel, own, SLOTS, BACK_SLOTS), o...  3.3 us
  transfers between devices with their start and end apart: 17, of which 6 were waited for; matrix products, arithmetic and copies ran while one was open for 2% of the time, Pallas kernels for 4%

profile of v3, /device:TPU:64, one launch (start us, length us, event | category | flops | bytes accessed | tf_op | source)
XLA Modules:
  0.0 150.3 jit_solution(1578293508449078748)
XLA Ops:
  0.6 0.0 copy-start.15
  0.6 1.3 slice_bitcast_fusion.3
  2.0 0.7 collective-permute-start
  2.6 0.7 collective-permute-start.1
  3.3 0.7 collective-permute-start.2
  4.0 0.7 collective-permute-start.3
  4.7 1.3 collective-permute-start.4
  6.6 0.0 collective-permute-done
  6.6 1.9 %collective-permute-start.5 = (f32[384,256]{1,0:T(8,128)}, f32[384,256]{1,0:T(8,128)S(1)}, u32[]{:S(2)}, u32[]{:S(2)}) collective-permute-start(f32[384,256]{1,0:T(8,128)} %bitcast.62), channel_id=1, source_target_pairs={{0,32},{32,0},{1,33},{33,1},{2,34},{34,2},{3,35},{35,3},{4,36},{36... | collective-permute-start | bytes 1179656 | tf_op jit(solution)/shard_map/ppermute | solution.py:356
  8.6 0.0 collective-permute-done.1
  8.6 0.0 collective-permute-done.2
  8.6 0.0 collective-permute-done.3
  8.6 10.2 %collective-permute-done.4 = f32[176,256]{1,0:T(8,128)S(1)} collective-permute-done((f32[176,256]{1,0:T(8,128)S(1)}, f32[176,256]{1,0:T(8,128)S(1)}, u32[]{:S(2)}, u32[]{:S(2)}) %collective-permute-start.4) | collective-permute-done | bytes 180256 | tf_op jit(solution)/shard_map/ppermute | solution.py:356
  18.8 1.0 bitcast_select_fusion
  19.8 5.1 %collective-permute-start.6 = (f32[176,256]{1,0:T(8,128)S(1)}, f32[176,256]{1,0:T(8,128)S(1)}, u32[]{:S(2)}, u32[]{:S(2)}) collective-permute-start(f32[176,256]{1,0:T(8,128)S(1)} %bitcast_select_fusion), channel_id=1, source_target_pairs={{15,16},{12,28},{3,19},{14,17},{11,20},{0,21},{31,0},{28,12},{19,3... | collective-permute-start | bytes 540680 | tf_op jit(solution)/shard_map/ppermute | solution.py:356
  24.9 0.7 compare_select_fusion.1.ids_ref
  25.6 0.6 broadcast_in_dim.33
  26.2 9.0 %all-to-all-start.2 = ((s32[16,1,256]{2,1,0:T(1,128)}), s32[16,1,256]{2,1,0:T(1,128)S(1)}, u32[]{:S(2)}, u32[]{:S(2)}) async-start(s32[16,1,256]{2,1,0:T(1,128)} %broadcast_in_dim.33), calls=%async_computation.2 | async-start | bytes 32768 | tf_op jit(solution)/shard_map/all_to_all | solution.py:399
  35.2 0.1 pad_add_fusion.place_ref.first_ref
  35.3 8.0 %all-to-all-done.2 = s32[16,1,256]{2,1,0:T(1,128)S(1)} async-done(((s32[16,1,256]{2,1,0:T(1,128)}), s32[16,1,256]{2,1,0:T(1,128)S(1)}, u32[]{:S(2)}, u32[]{:S(2)}) %all-to-all-start.2) | async-done | bytes 16416 | tf_op jit(solution)/shard_map/all_to_all | solution.py:399
  43.2 0.0 copy-start.7
  43.2 0.0 collective-permute-done.5.other_ref
  43.2 0.0 copy-start.19
  43.3 3.1 %pack_rows.1 = f32[448,256]{1,0:T(8,128)} custom-call(s32[3]{0:T(128)S(1)} %pad_add_fusion.place_ref.first_ref, s32[16,256]{1,0:T(8,128)S(1)} %bitcast.66, f32[384,256]{1,0:T(8,128)} %bitcast.63, f32[384,256]{1,0:T(8,128)S(1)} %collective-permute-done.5.other_ref), custom_call_target="tpu_custom_call" | custom-call | tf_op jit(solution)/shard_map/pack_rows/pallas_call | solution.py:102
  46.3 0.0 collective-permute-done.6.refs_0_
  46.3 0.0 copy-done.7
  46.3 13.0 %all-to-all-start.3 = ((f32[8,56,256]{2,1,0:T(8,128)}), f32[8,56,256]{2,1,0:T(8,128)S(1)}, u32[]{:S(2)}, u32[]{:S(2)}) async-start(f32[8,56,256]{2,1,0:T(8,128)} %bitcast.25), calls=%async_computation.3 | async-start | bytes 917504 | tf_op jit(solution)/shard_map/all_to_all | solution.py:402
  59.3 1.3 collective-permute-start.7
  60.7 1.3 collective-permute-start.10
  62.0 1.3 collective-permute-start.11
  63.3 1.3 collective-permute-start.12
  64.6 1.3 collective-permute-start.8
  65.9 6.1 %collective-permute-done.10.refs_3_ = f32[176,256]{1,0:T(8,128)S(1)} collective-permute-done((f32[176,256]{1,0:T(8,128)S(1)}, f32[176,256]{1,0:T(8,128)S(1)}, u32[]{:S(2)}, u32[]{:S(2)}) %collective-permute-start.10) | collective-permute-done | bytes 180256 | tf_op jit(solution)/shard_map/ppermute | solution.py:356
  71.9 1.3 collective-permute-start.9
  73.2 0.0 collective-permute-done.11.refs_4_
  73.2 0.0 collective-permute-done.12.refs_5_
  73.2 0.0 collective-permute-done.8.refs_1_
  73.2 0.0 copy-start
  73.3 0.7 copy-done
  73.9 6.6 %collective-permute-done.9.refs_2_ = f32[176,256]{1,0:T(8,128)S(1)} collective-permute-done((f32[176,256]{1,0:T(8,128)S(1)}, f32[176,256]{1,0:T(8,128)S(1)}, u32[]{:S(2)}, u32[]{:S(2)}) %collective-permute-start.9) | collective-permute-done | bytes 180256 | tf_op jit(solution)/shard_map/ppermute | solution.py:356
  80.5 0.0 copy-start.2
  80.5 0.7 copy-done.2
  81.2 1.6 %collective-permute-done.7.near_ref = f32[1024,256]{1,0:T(8,128)S(1)} collective-permute-done((f32[1024,256]{1,0:T(8,128)}, f32[1024,256]{1,0:T(8,128)S(1)}, u32[]{:S(2)}, u32[]{:S(2)}) %collective-permute-start.7) | collective-permute-done | bytes 1048608 | tf_op jit(solution)/shard_map/ppermute | solution.py:356
  82.8 0.0 all-to-all-done.3
  82.8 0.0 copy-done.15
  82.8 0.0 copy-start.1
  82.8 0.9 copy-done.1
  83.7 0.0 copy-start.3
  83.7 0.9 copy-done.3
  84.7 7.6 %edge_step.1 = (f32[1,256]{1,0:T(1,128)}, f32[640,256]{1,0:T(8,128)}, f32[256,256]{1,0:T(8,128)S(1)}, f32[256,1024]{1,0:T(8,128)S(1)}, f32[1024,256]{1,0:T(8,128)}) custom-call(s32[1,1]{1,0:T(1,128)} %copy.41.count_ref, s32[1]{0:T(128)} %bitcast.12.crossed_ref, s32[1,256]{1,0:T(1,128)S(1)} %compare_select_fusion.1.ids_ref, s32[1,256]{1,0:T(1,128)S(1)} %bitcast.76, ...), custom_call_target="tpu_custom_call" | custom-call | tf_op jit(solution)/shard_map/edge_step/pallas_call | solution.py:191
  92.3 9.9 %all-to-all-start.4 = ((f32[16,40,256]{2,1,0:T(8,128)}), f32[16,40,256]{2,1,0:T(8,128)S(1)}, u32[]{:S(2)}, u32[]{:S(2)}) async-start(f32[16,40,256]{2,1,0:T(8,128)} %bitcast.30), calls=%async_computation.4 | async-start | bytes 1310720 | tf_op jit(solution)/shard_map/all_to_all | solution.py:407
  102.2 2.9 %collective-permute-start.13 = (f32[1,1024]{1,0:T(1,128)}, f32[1,1024]{1,0:T(1,128)S(1)}, u32[]{:S(2)}, u32[]{:S(2)}) collective-permute-start(f32[1,1024]{1,0:T(1,128)} %bitcast.88), channel_id=1, source_target_pairs={{0,1},{1,2},{2,3},{3,4},{4,5},{5,6},{6,7},{7,8},{8,9},{9,10},{10,1... | collective-permute-start | bytes 12296 | tf_op jit(solution)/shard_map/ppermute | solution.py:356
  105.1 38.0 %collective-permute-done.13.state_ref = f32[1,1024]{1,0:T(1,128)S(1)} collective-permute-done((f32[1,1024]{1,0:T(1,128)}, f32[1,1024]{1,0:T(1,128)S(1)}, u32[]{:S(2)}, u32[]{:S(2)}) %collective-permute-start.13) | collective-permute-done | bytes 4128 | tf_op jit(solution)/shard_map/ppermute | solution.py:356
  143.1 3.3 %table_step.1 = (f32[1024,256]{1,0:T(8,128)}, f32[1,1024]{1,0:T(1,128)}, f32[1,1]{1,0:T(1,128)}, f32[640,1]{1,0:T(8,128)S(1)}) custom-call(s32[3]{0:T(128)S(1)} %pad_add_fusion.place_ref.first_ref, f32[256,1024]{1,0:T(8,128)S(1)} %get-tuple-element.107.weight_ref, f32[256,256]{1,0:T(8,128)S(1)} %get-tuple-element.108.source_ref, ...), custom_call_target="tpu_custom_call" | custom-call | tf_op jit(solution)/shard_map/table_step/pallas_call | solution.py:245
  146.4 0.0 all-to-all-done.4
  146.4 0.0 copy-done.19
  146.4 2.9 %source_step.1 = (f32[384,256]{1,0:T(8,128)}, f32[1,384]{1,0:T(1,128)}) custom-call(f32[640,1]{1,0:T(8,128)S(1)} %get-tuple-element.112.local_ref, f32[640,256]{1,0:T(8,128)S(1)} %bitcast.60, f32[384,256]{1,0:T(8,128)} %bitcast.64, f32[1,384]{1,0:T(1,128)S(1)} %bitcast.79), custom_call_target="tpu_custom_call" | custom-call | tf_op jit(solution)/shard_map/source_step/pallas_call | solution.py:269
  149.3 0.8 while.17
  (1 shorter events, 0.0 us)
Async XLA Ops:
  0.6 82.2 %copy-start.15 = (s32[1,1,256]{2,1,0:T(1,128)S(1)}, s32[1,1,256]{2,1,0:T(1,128)}, u32[]{:S(2)}) copy-start(s32[1,1,256]{2,1,0:T(1,128)} %param.15) | copy-start | bytes 3076
  2.0 4.7 %collective-permute-start = (f32[176,256]{1,0:T(8,128)S(1)}, f32[176,256]{1,0:T(8,128)S(1)}, u32[]{:S(2)}, u32[]{:S(2)}) collective-permute-start(f32[176,256]{1,0:T(8,128)S(1)} %get-tuple-element.165), channel_id=1, source_target_pairs={{15,12},{31,28},{47,44},{63,60},{79,76},{95,92},{111,108},{127,124... | collective-permute-start | bytes 540680 | tf_op jit(solution)/shard_map/ppermute | solution.py:356
  2.6 5.9 %collective-permute-start.1 = (f32[176,256]{1,0:T(8,128)S(1)}, f32[176,256]{1,0:T(8,128)S(1)}, u32[]{:S(2)}, u32[]{:S(2)}) collective-permute-start(f32[176,256]{1,0:T(8,128)S(1)} %get-tuple-element.162), channel_id=1, source_target_pairs={{15,3},{31,19},{47,35},{63,51},{79,67},{95,83},{111,99},{127,115},... | collective-permute-start | bytes 540680 | tf_op jit(solution)/shard_map/ppermute | solution.py:356
  3.3 5.3 %collective-permute-start.2 = (f32[176,256]{1,0:T(8,128)S(1)}, f32[176,256]{1,0:T(8,128)S(1)}, u32[]{:S(2)}, u32[]{:S(2)}) collective-permute-start(f32[176,256]{1,0:T(8,128)S(1)} %get-tuple-element.164), channel_id=1, source_target_pairs={{15,14},{31,30},{47,46},{63,62},{79,78},{95,94},{111,110},{127,126... | collective-permute-start | bytes 540680 | tf_op jit(solution)/shard_map/ppermute | solution.py:356
  4.0 4.6 %collective-permute-start.3 = (f32[176,256]{1,0:T(8,128)S(1)}, f32[176,256]{1,0:T(8,128)S(1)}, u32[]{:S(2)}, u32[]{:S(2)}) collective-permute-start(f32[176,256]{1,0:T(8,128)S(1)} %get-tuple-element.163), channel_id=1, source_target_pairs={{15,11},{31,27},{47,43},{63,59},{79,75},{95,91},{111,107},{127,123... | collective-permute-start | bytes 540680 | tf_op jit(solution)/shard_map/ppermute | solution.py:356
  4.7 14.1 %collective-permute-start.4 = (f32[176,256]{1,0:T(8,128)S(1)}, f32[176,256]{1,0:T(8,128)S(1)}, u32[]{:S(2)}, u32[]{:S(2)}) collective-permute-start(f32[176,256]{1,0:T(8,128)S(1)} %get-tuple-element.166), channel_id=1, source_target_pairs={{15,0},{31,16},{47,32},{63,48},{79,64},{95,80},{111,96},{127,112},... | collective-permute-start | bytes 540680 | tf_op jit(solution)/shard_map/ppermute | solution.py:356
  6.6 36.6 %collective-permute-start.5 = (f32[384,256]{1,0:T(8,128)}, f32[384,256]{1,0:T(8,128)S(1)}, u32[]{:S(2)}, u32[]{:S(2)}) collective-permute-start(f32[384,256]{1,0:T(8,128)} %bitcast.62), channel_id=1, source_target_pairs={{0,32},{32,0},{1,33},{33,1},{2,34},{34,2},{3,35},{35,3},{4,36},{36... | collective-permute-start | bytes 1179656 | tf_op jit(solution)/shard_map/ppermute | solution.py:356
  19.8 26.6 %collective-permute-start.6 = (f32[176,256]{1,0:T(8,128)S(1)}, f32[176,256]{1,0:T(8,128)S(1)}, u32[]{:S(2)}, u32[]{:S(2)}) collective-permute-start(f32[176,256]{1,0:T(8,128)S(1)} %bitcast_select_fusion), channel_id=1, source_target_pairs={{15,16},{12,28},{3,19},{14,17},{11,20},{0,21},{31,0},{28,12},{19,3... | collective-permute-start | bytes 540680 | tf_op jit(solution)/shard_map/ppermute | solution.py:356
  26.2 17.1 %all-to-all-start.2 = ((s32[16,1,256]{2,1,0:T(1,128)}), s32[16,1,256]{2,1,0:T(1,128)S(1)}, u32[]{:S(2)}, u32[]{:S(2)}) async-start(s32[16,1,256]{2,1,0:T(1,128)} %broadcast_in_dim.33), calls=%async_computation.2 | async-start | bytes 32768 | tf_op jit(solution)/shard_map/all_to_all | solution.py:399
  43.2 3.1 %copy-start.7 = (s32[16,1,256]{2,0,1:T(8,128)}, s32[16,1,256]{2,0,1:T(8,128)S(1)}, u32[]{:S(2)}) copy-start(s32[16,1,256]{2,0,1:T(8,128)S(1)} %copy.21) | copy-start | bytes 49156
  43.2 103.2 %copy-start.19 = (f32[1,1,384]{2,1,0:T(1,128)S(1)}, f32[1,1,384]{2,1,0:T(1,128)}, u32[]{:S(2)}) copy-start(f32[1,1,384]{2,1,0:T(1,128)} %param.11) | copy-start | bytes 4612
  46.3 36.5 %all-to-all-start.3 = ((f32[8,56,256]{2,1,0:T(8,128)}), f32[8,56,256]{2,1,0:T(8,128)S(1)}, u32[]{:S(2)}, u32[]{:S(2)}) async-start(f32[8,56,256]{2,1,0:T(8,128)} %bitcast.25), calls=%async_computation.3 | async-start | bytes 917504 | tf_op jit(solution)/shard_map/all_to_all | solution.py:402
  59.3 23.5 %collective-permute-start.7 = (f32[1024,256]{1,0:T(8,128)}, f32[1024,256]{1,0:T(8,128)S(1)}, u32[]{:S(2)}, u32[]{:S(2)}) collective-permute-start(f32[1024,256]{1,0:T(8,128)} %bitcast.27), channel_id=1, source_target_pairs={{0,1},{1,2},{2,3},{3,4},{4,5},{5,6},{6,7},{7,8},{8,9},{9,10},{10,1... | collective-permute-start | bytes 3145736 | tf_op jit(solution)/shard_map/ppermute | solution.py:356
  60.7 11.3 %collective-permute-start.10 = (f32[176,256]{1,0:T(8,128)S(1)}, f32[176,256]{1,0:T(8,128)S(1)}, u32[]{:S(2)}, u32[]{:S(2)}) collective-permute-start(f32[176,256]{1,0:T(8,128)S(1)} %collective-permute-done.6.refs_0_), channel_id=1, source_target_pairs={{1,0},{17,16},{33,32},{49,48},{65,64},{81,80},{97,96},{113,112},{1... | collective-permute-start | bytes 540680 | tf_op jit(solution)/shard_map/ppermute | solution.py:356
  62.0 11.3 %collective-permute-start.11 = (f32[176,256]{1,0:T(8,128)S(1)}, f32[176,256]{1,0:T(8,128)S(1)}, u32[]{:S(2)}, u32[]{:S(2)}) collective-permute-start(f32[176,256]{1,0:T(8,128)S(1)} %collective-permute-done.6.refs_0_), channel_id=1, source_target_pairs={{4,0},{20,16},{36,32},{52,48},{68,64},{84,80},{100,96},{116,112},{... | collective-permute-start | bytes 540680 | tf_op jit(solution)/shard_map/ppermute | solution.py:356
  63.3 10.0 %collective-permute-start.12 = (f32[176,256]{1,0:T(8,128)S(1)}, f32[176,256]{1,0:T(8,128)S(1)}, u32[]{:S(2)}, u32[]{:S(2)}) collective-permute-start(f32[176,256]{1,0:T(8,128)S(1)} %collective-permute-done.6.refs_0_), channel_id=1, source_target_pairs={{5,0},{21,16},{37,32},{53,48},{69,64},{85,80},{101,96},{117,112},{... | collective-permute-start | bytes 540680 | tf_op jit(solution)/shard_map/ppermute | solution.py:356
  64.6 8.7 %collective-permute-start.8 = (f32[176,256]{1,0:T(8,128)S(1)}, f32[176,256]{1,0:T(8,128)S(1)}, u32[]{:S(2)}, u32[]{:S(2)}) collective-permute-start(f32[176,256]{1,0:T(8,128)S(1)} %collective-permute-done.6.refs_0_), channel_id=1, source_target_pairs={{12,0},{28,16},{44,32},{60,48},{76,64},{92,80},{108,96},{124,112},... | collective-permute-start | bytes 540680 | tf_op jit(solution)/shard_map/ppermute | solution.py:356
  71.9 8.6 %collective-permute-start.9 = (f32[176,256]{1,0:T(8,128)S(1)}, f32[176,256]{1,0:T(8,128)S(1)}, u32[]{:S(2)}, u32[]{:S(2)}) collective-permute-start(f32[176,256]{1,0:T(8,128)S(1)} %collective-permute-done.6.refs_0_), channel_id=1, source_target_pairs={{3,0},{19,16},{35,32},{51,48},{67,64},{83,80},{99,96},{115,112},{1... | collective-permute-start | bytes 540680 | tf_op jit(solution)/shard_map/ppermute | solution.py:356
  73.2 0.7 copy-start
  80.5 0.7 copy-start.2
  82.8 0.9 copy-start.1
  83.7 0.9 copy-start.3
  92.3 54.2 %all-to-all-start.4 = ((f32[16,40,256]{2,1,0:T(8,128)}), f32[16,40,256]{2,1,0:T(8,128)S(1)}, u32[]{:S(2)}, u32[]{:S(2)}) async-start(f32[16,40,256]{2,1,0:T(8,128)} %bitcast.30), calls=%async_computation.4 | async-start | bytes 1310720 | tf_op jit(solution)/shard_map/all_to_all | solution.py:407
  102.2 40.9 %collective-permute-start.13 = (f32[1,1024]{1,0:T(1,128)}, f32[1,1024]{1,0:T(1,128)S(1)}, u32[]{:S(2)}, u32[]{:S(2)}) collective-permute-start(f32[1,1024]{1,0:T(1,128)} %bitcast.88), channel_id=1, source_target_pairs={{0,1},{1,2},{2,3},{3,4},{4,5},{5,6},{6,7},{7,8},{8,9},{9,10},{10,1... | collective-permute-start | bytes 12296 | tf_op jit(solution)/shard_map/ppermute | solution.py:356

commit v4 on v3

--- a/solution.py
+++ b/solution.py
@@ -10,8 +10,8 @@
 
 SLOTS = 56
 BACK_SLOTS = 40
-LEAVE = ((-1, -1), (-1, 0), (0, -1), (-1, -2), (-2, -1), (0, 0))
-LAND = ((0, 0), (-1, 0), (0, -1), (0, 1), (1, 0), (1, 1))
+LEAVE = ((-1, -1), (-1, 0), (0, -1), (-1, -2), (-2, -1))
+LAND = ((0, 0), (-1, 0), (0, -1), (0, 1), (1, 0))
 SRC = ("zl", "core")
 DST = ("zh", "x", "y")
 F32 = jnp.float32
@@ -395,12 +395,12 @@
     ids = jnp.where(edge < counts[0, 0], ids, -1)
     near, joined, starts, crossed, going, come = shifted(dst_emb[0, 0])
     other = permute(rows, "core", [(0, 1), (1, 0)])
-    all_ids = jnp.broadcast_to(after(ids, going), (devices, ids.shape[1]))
-    all_ids = lax.all_to_all(all_ids, SRC, 0, 0, tiled=True)
-
-    send = pack_rows(place, all_ids, rows, other, SLOTS)
-    got = lax.all_to_all(after(send, come), "zl", 0, 0, tiled=True)
+    all_ids = lax.all_to_all(jnp.broadcast_to(ids, (devices, ids.shape[1])), SRC, 0, 0, tiled=True)
+
+    send = pack_rows(place, after(all_ids, going), rows, other, SLOTS)
+    got = lax.all_to_all(after(send, come, near), "zl", 0, 0, tiled=True)
     table_state = permute(after(dst_state[0], send), DST, pairs)
+    got = after(got, table_state)
     loss, back, source, weight, table = edge_step(
         counts, crossed.reshape(1), ids, dst_ids[0], neg_ids[0], got, near, joined, starts, devices, own
     )

time: 151 us -> 162 us (1.073)
  the two profiles are of different devices: /device:TPU:64 before, /device:TPU:33 now
where the time goes in v4:
time: 162 us
  waiting for transfers between devices  87 us (54%)
  starting transfers between devices  48.3 us (30%)
  Pallas kernels  16.8 us (10%)
  local copies, waits for them, and re-layouts  5.16 us (3%)
  other arithmetic  1.77 us (1%)
  between operations  1.67 us (1%)
    ppermute x12, waiting for transfers between devices, permute(): return lax.ppermute(value, axes, pairs)  43.5 us
    all_to_all x1, waiting for transfers between devices, on_device(): back = lax.all_to_all(back, SRC, 0, 0, tiled=True)  28.8 us
    ppermute x12, starting transfers between devices, permute(): return lax.ppermute(value, axes, pairs)  17.3 us
    all_to_all x1, starting transfers between devices, on_device(): back = lax.all_to_all(back, SRC, 0, 0, tiled=True)  14.9 us
    all_to_all x1, starting transfers between devices, on_device(): lax.all_to_all(jnp.broadcast_to(ids, (devices, ids.shape[1])), SRC, 0, 0,...  12.4 us
    all_to_all x1, waiting for transfers between devices, on_device(): lax.all_to_all(jnp.broadcast_to(ids, (devices, ids.shape[1])), SRC, 0, 0,...  8.81 us
    pallas_call x1, Pallas kernels, edge_step(): pl.pallas_call(functools.partial(edge_kernel, own, SLOTS, BACK_SLOTS, tup...  7.58 us
    all_to_all x1, waiting for transfers between devices, on_device(): got = lax.all_to_all(after(send, come, near), 'zl', 0, 0, tiled=True)  5.84 us
  transfers between devices with their start and end apart: 15, of which 5 were waited for; matrix products, arithmetic and copies ran while one was open for 2% of the time, Pallas kernels for 4%

profile of v4, /device:TPU:33, one launch (start us, length us, event | category | flops | bytes accessed | tf_op | source)
XLA Modules:
  0.0 161.5 jit_solution(15414325887307142809)
XLA Ops:
  0.6 0.0 copy-start.21
  0.6 0.0 copy-start.22
  0.7 3.4 %collective-permute-start.6 = (f32[1024,256]{1,0:T(8,128)}, f32[1024,256]{1,0:T(8,128)S(1)}, u32[]{:S(2)}, u32[]{:S(2)}) collective-permute-start(f32[1024,256]{1,0:T(8,128)} %bitcast.65), channel_id=1, source_target_pairs={{0,1},{1,2},{2,3},{3,4},{4,5},{5,6},{6,7},{7,8},{8,9},{9,10},{10,1... | collective-permute-start | bytes 3145736 | tf_op jit(solution)/shard_map/ppermute | solution.py:356
  4.1 1.3 slice_bitcast_fusion.2
  5.4 0.7 collective-permute-start
  6.1 0.7 collective-permute-start.1
  6.7 0.7 collective-permute-start.2
  7.4 0.7 collective-permute-start.3
  8.8 0.0 collective-permute-done
  8.8 2.9 %collective-permute-start.4 = (f32[384,256]{1,0:T(8,128)}, f32[384,256]{1,0:T(8,128)S(1)}, u32[]{:S(2)}, u32[]{:S(2)}) collective-permute-start(f32[384,256]{1,0:T(8,128)} %bitcast.61), channel_id=1, source_target_pairs={{0,32},{32,0},{1,33},{33,1},{2,34},{34,2},{3,35},{35,3},{4,36},{36... | collective-permute-start | bytes 1179656 | tf_op jit(solution)/shard_map/ppermute | solution.py:356
  11.6 0.0 collective-permute-done.1
  11.7 0.0 collective-permute-done.2
  11.7 0.0 collective-permute-done.3
  11.7 1.0 bitcast_select_fusion
  12.7 1.3 collective-permute-start.5
  14.0 0.7 compare_select_fusion.2
  14.7 0.6 broadcast_in_dim.44
  15.3 12.4 %all-to-all-start.2 = ((s32[16,1,256]{2,1,0:T(1,128)}), s32[16,1,256]{2,1,0:T(1,128)S(1)}, u32[]{:S(2)}, u32[]{:S(2)}) async-start(s32[16,1,256]{2,1,0:T(1,128)} %broadcast_in_dim.44), calls=%async_computation.2 | async-start | bytes 32768 | tf_op jit(solution)/shard_map/all_to_all | solution.py:398
  27.7 0.1 pad_add_fusion.place_ref.first_ref
  27.8 8.8 %all-to-all-done.2 = s32[16,1,256]{2,1,0:T(1,128)S(1)} async-done(((s32[16,1,256]{2,1,0:T(1,128)}), s32[16,1,256]{2,1,0:T(1,128)S(1)}, u32[]{:S(2)}, u32[]{:S(2)}) %all-to-all-start.2) | async-done | bytes 16416 | tf_op jit(solution)/shard_map/all_to_all | solution.py:398
  36.6 0.0 collective-permute-done.4.other_ref
  36.6 3.1 %pack_rows.1 = f32[448,256]{1,0:T(8,128)} custom-call(s32[3]{0:T(128)S(1)} %pad_add_fusion.place_ref.first_ref, s32[16,256]{1,0:T(8,128)S(1)} %bitcast.66, f32[384,256]{1,0:T(8,128)} %bitcast.62, f32[384,256]{1,0:T(8,128)S(1)} %collective-permute-done.4.other_ref), custom_call_target="tpu_custom_call" | custom-call | tf_op jit(solution)/shard_map/pack_rows/pallas_call | solution.py:102
  39.7 33.1 %collective-permute-done.5.refs_0_ = f32[208,256]{1,0:T(8,128)S(1)} collective-permute-done((f32[208,256]{1,0:T(8,128)S(1)}, f32[208,256]{1,0:T(8,128)S(1)}, u32[]{:S(2)}, u32[]{:S(2)}) %collective-permute-start.5) | collective-permute-done | bytes 213024 | tf_op jit(solution)/shard_map/ppermute | solution.py:356
  72.7 0.0 collective-permute-done.6.near_ref
  72.7 3.7 %all-to-all-start.3 = ((f32[8,56,256]{2,1,0:T(8,128)}), f32[8,56,256]{2,1,0:T(8,128)S(1)}, u32[]{:S(2)}, u32[]{:S(2)}) async-start(f32[8,56,256]{2,1,0:T(8,128)} %bitcast.25), calls=%async_computation.3 | async-start | bytes 917504 | tf_op jit(solution)/shard_map/all_to_all | solution.py:401
  76.4 0.0 copy-done.22
  76.4 1.9 %collective-permute-start.7 = (f32[1,1024]{1,0:T(1,128)S(1)}, f32[1,1024]{1,0:T(1,128)}, u32[]{:S(2)}, u32[]{:S(2)}) collective-permute-start(f32[1,1024]{1,0:T(1,128)S(1)} %bitcast.78), channel_id=1, source_target_pairs={{0,1},{1,2},{2,3},{3,4},{4,5},{5,6},{6,7},{7,8},{8,9},{9,10},{10,1... | collective-permute-start | bytes 12296 | tf_op jit(solution)/shard_map/ppermute | solution.py:356
  78.3 1.3 collective-permute-start.10
  79.6 1.3 collective-permute-start.11
  80.9 1.3 collective-permute-start.8
  82.2 1.3 collective-permute-start.9
  83.5 0.0 copy-done.21
  83.6 10.4 %collective-permute-done.7.state_ref = f32[1,1024]{1,0:T(1,128)} collective-permute-done((f32[1,1024]{1,0:T(1,128)S(1)}, f32[1,1024]{1,0:T(1,128)}, u32[]{:S(2)}, u32[]{:S(2)}) %collective-permute-start.7) | collective-permute-done | bytes 4128 | tf_op jit(solution)/shard_map/ppermute | solution.py:356
  94.0 5.8 %all-to-all-done.3 = f32[8,56,256]{2,1,0:T(8,128)S(1)} async-done(((f32[8,56,256]{2,1,0:T(8,128)}), f32[8,56,256]{2,1,0:T(8,128)S(1)}, u32[]{:S(2)}, u32[]{:S(2)}) %all-to-all-start.3) | async-done | bytes 458784 | tf_op jit(solution)/shard_map/all_to_all | solution.py:401
  99.8 0.0 collective-permute-done.10.refs_3_
  99.8 0.0 collective-permute-done.11.refs_4_
  99.8 0.0 collective-permute-done.8.refs_1_
  99.8 0.0 copy-start
  99.8 0.7 copy-done
  100.5 0.0 collective-permute-done.9.refs_2_
  100.5 0.0 copy-start.2
  100.5 0.7 copy-done.2
  101.2 0.0 copy-start.1
  101.2 0.9 copy-done.1
  102.1 0.0 copy-start.3
  102.1 0.9 copy-done.3
  103.0 7.6 %edge_step.1 = (f32[1,256]{1,0:T(1,128)}, f32[640,256]{1,0:T(8,128)}, f32[256,256]{1,0:T(8,128)S(1)}, f32[256,1024]{1,0:T(8,128)S(1)}, f32[1024,256]{1,0:T(8,128)}) custom-call(s32[1,1]{1,0:T(1,128)} %copy.41.count_ref, s32[1]{0:T(128)} %bitcast.12.crossed_ref, s32[1,256]{1,0:T(1,128)S(1)} %compare_select_fusion.1.ids_ref, s32[1,256]{1,0:T(1,128)} %bitcast.15.dest_ref, ...), custom_call_target="tpu_custom_call" | custom-call | tf_op jit(solution)/shard_map/edge_step/pallas_call | solution.py:191
  110.6 14.9 %all-to-all-start.4 = ((f32[16,40,256]{2,1,0:T(8,128)}), f32[16,40,256]{2,1,0:T(8,128)S(1)}, u32[]{:S(2)}, u32[]{:S(2)}) async-start(f32[16,40,256]{2,1,0:T(8,128)} %bitcast.29), calls=%async_computation.4 | async-start | bytes 1310720 | tf_op jit(solution)/shard_map/all_to_all | solution.py:407
  125.5 3.3 %table_step.1 = (f32[1024,256]{1,0:T(8,128)}, f32[1,1024]{1,0:T(1,128)}, f32[1,1]{1,0:T(1,128)}, f32[640,1]{1,0:T(8,128)S(1)}) custom-call(s32[3]{0:T(128)S(1)} %pad_add_fusion.place_ref.first_ref, f32[256,1024]{1,0:T(8,128)S(1)} %get-tuple-element.110.weight_ref, f32[256,256]{1,0:T(8,128)S(1)} %get-tuple-element.111.source_ref, ...), custom_call_target="tpu_custom_call" | custom-call | tf_op jit(solution)/shard_map/table_step/pallas_call | solution.py:245
  128.8 28.8 %all-to-all-done.4 = f32[16,40,256]{2,1,0:T(8,128)S(1)} async-done(((f32[16,40,256]{2,1,0:T(8,128)}), f32[16,40,256]{2,1,0:T(8,128)S(1)}, u32[]{:S(2)}, u32[]{:S(2)}) %all-to-all-start.4) | async-done | bytes 655392 | tf_op jit(solution)/shard_map/all_to_all | solution.py:407
  157.7 2.9 %source_step.1 = (f32[384,256]{1,0:T(8,128)}, f32[1,384]{1,0:T(1,128)}) custom-call(f32[640,1]{1,0:T(8,128)S(1)} %get-tuple-element.114.local_ref, f32[640,256]{1,0:T(8,128)S(1)} %bitcast.59, f32[384,256]{1,0:T(8,128)} %bitcast.63, f32[1,384]{1,0:T(1,128)} %bitcast.31.state_ref), custom_call_target="tpu_custom_call" | custom-call | tf_op jit(solution)/shard_map/source_step/pallas_call | solution.py:269
  160.5 0.8 while.17
  (2 shorter events, 0.0 us)
Async XLA Ops:
  0.6 82.9 %copy-start.21 = (s32[1,1,256]{2,1,0:T(1,128)S(1)}, s32[1,1,256]{2,1,0:T(1,128)}, u32[]{:S(2)}) copy-start(s32[1,1,256]{2,1,0:T(1,128)} %param.14) | copy-start | bytes 3076
  0.6 75.8 %copy-start.22 = (f32[1,1,1024]{2,1,0:T(1,128)S(1)}, f32[1,1,1024]{2,1,0:T(1,128)}, u32[]{:S(2)}) copy-start(f32[1,1,1024]{2,1,0:T(1,128)} %param.13) | copy-start | bytes 12292
  0.7 72.1 %collective-permute-start.6 = (f32[1024,256]{1,0:T(8,128)}, f32[1024,256]{1,0:T(8,128)S(1)}, u32[]{:S(2)}, u32[]{:S(2)}) collective-permute-start(f32[1024,256]{1,0:T(8,128)} %bitcast.65), channel_id=1, source_target_pairs={{0,1},{1,2},{2,3},{3,4},{4,5},{5,6},{6,7},{7,8},{8,9},{9,10},{10,1... | collective-permute-start | bytes 3145736 | tf_op jit(solution)/shard_map/ppermute | solution.py:356
  5.4 3.4 %collective-permute-start = (f32[208,256]{1,0:T(8,128)S(1)}, f32[208,256]{1,0:T(8,128)S(1)}, u32[]{:S(2)}, u32[]{:S(2)}) collective-permute-start(f32[208,256]{1,0:T(8,128)S(1)} %get-tuple-element.166), channel_id=1, source_target_pairs={{15,12},{31,28},{47,44},{63,60},{79,76},{95,92},{111,108},{127,124... | collective-permute-start | bytes 638984 | tf_op jit(solution)/shard_map/ppermute | solution.py:356
  6.1 5.6 %collective-permute-start.1 = (f32[208,256]{1,0:T(8,128)S(1)}, f32[208,256]{1,0:T(8,128)S(1)}, u32[]{:S(2)}, u32[]{:S(2)}) collective-permute-start(f32[208,256]{1,0:T(8,128)S(1)} %get-tuple-element.164), channel_id=1, source_target_pairs={{15,3},{31,19},{47,35},{63,51},{79,67},{95,83},{111,99},{127,115},... | collective-permute-start | bytes 638984 | tf_op jit(solution)/shard_map/ppermute | solution.py:356
  6.7 4.9 %collective-permute-start.2 = (f32[208,256]{1,0:T(8,128)S(1)}, f32[208,256]{1,0:T(8,128)S(1)}, u32[]{:S(2)}, u32[]{:S(2)}) collective-permute-start(f32[208,256]{1,0:T(8,128)S(1)} %get-tuple-element.165), channel_id=1, source_target_pairs={{15,14},{31,30},{47,46},{63,62},{79,78},{95,94},{111,110},{127,126... | collective-permute-start | bytes 638984 | tf_op jit(solution)/shard_map/ppermute | solution.py:356
  7.4 4.2 %collective-permute-start.3 = (f32[208,256]{1,0:T(8,128)S(1)}, f32[208,256]{1,0:T(8,128)S(1)}, u32[]{:S(2)}, u32[]{:S(2)}) collective-permute-start(f32[208,256]{1,0:T(8,128)S(1)} %get-tuple-element.167), channel_id=1, source_target_pairs={{15,11},{31,27},{47,43},{63,59},{79,75},{95,91},{111,107},{127,123... | collective-permute-start | bytes 638984 | tf_op jit(solution)/shard_map/ppermute | solution.py:356
  8.8 27.8 %collective-permute-start.4 = (f32[384,256]{1,0:T(8,128)}, f32[384,256]{1,0:T(8,128)S(1)}, u32[]{:S(2)}, u32[]{:S(2)}) collective-permute-start(f32[384,256]{1,0:T(8,128)} %bitcast.61), channel_id=1, source_target_pairs={{0,32},{32,0},{1,33},{33,1},{2,34},{34,2},{3,35},{35,3},{4,36},{36... | collective-permute-start | bytes 1179656 | tf_op jit(solution)/shard_map/ppermute | solution.py:356
  12.7 60.1 %collective-permute-start.5 = (f32[208,256]{1,0:T(8,128)S(1)}, f32[208,256]{1,0:T(8,128)S(1)}, u32[]{:S(2)}, u32[]{:S(2)}) collective-permute-start(f32[208,256]{1,0:T(8,128)S(1)} %bitcast_select_fusion), channel_id=1, source_target_pairs={{15,16},{12,28},{3,19},{14,17},{11,20},{31,0},{28,12},{19,3},{30,1... | collective-permute-start | bytes 638984 | tf_op jit(solution)/shard_map/ppermute | solution.py:356
  15.3 21.3 %all-to-all-start.2 = ((s32[16,1,256]{2,1,0:T(1,128)}), s32[16,1,256]{2,1,0:T(1,128)S(1)}, u32[]{:S(2)}, u32[]{:S(2)}) async-start(s32[16,1,256]{2,1,0:T(1,128)} %broadcast_in_dim.44), calls=%async_computation.2 | async-start | bytes 32768 | tf_op jit(solution)/shard_map/all_to_all | solution.py:398
  72.7 27.0 %all-to-all-start.3 = ((f32[8,56,256]{2,1,0:T(8,128)}), f32[8,56,256]{2,1,0:T(8,128)S(1)}, u32[]{:S(2)}, u32[]{:S(2)}) async-start(f32[8,56,256]{2,1,0:T(8,128)} %bitcast.25), calls=%async_computation.3 | async-start | bytes 917504 | tf_op jit(solution)/shard_map/all_to_all | solution.py:401
  76.4 17.5 %collective-permute-start.7 = (f32[1,1024]{1,0:T(1,128)S(1)}, f32[1,1024]{1,0:T(1,128)}, u32[]{:S(2)}, u32[]{:S(2)}) collective-permute-start(f32[1,1024]{1,0:T(1,128)S(1)} %bitcast.78), channel_id=1, source_target_pairs={{0,1},{1,2},{2,3},{3,4},{4,5},{5,6},{6,7},{7,8},{8,9},{9,10},{10,1... | collective-permute-start | bytes 12296 | tf_op jit(solution)/shard_map/ppermute | solution.py:356
  78.3 21.4 %collective-permute-start.10 = (f32[208,256]{1,0:T(8,128)S(1)}, f32[208,256]{1,0:T(8,128)S(1)}, u32[]{:S(2)}, u32[]{:S(2)}) collective-permute-start(f32[208,256]{1,0:T(8,128)S(1)} %collective-permute-done.5.refs_0_), channel_id=1, source_target_pairs={{1,0},{17,16},{33,32},{49,48},{65,64},{81,80},{97,96},{113,112},{1... | collective-permute-start | bytes 638984 | tf_op jit(solution)/shard_map/ppermute | solution.py:356
  79.6 20.1 %collective-permute-start.11 = (f32[208,256]{1,0:T(8,128)S(1)}, f32[208,256]{1,0:T(8,128)S(1)}, u32[]{:S(2)}, u32[]{:S(2)}) collective-permute-start(f32[208,256]{1,0:T(8,128)S(1)} %collective-permute-done.5.refs_0_), channel_id=1, source_target_pairs={{4,0},{20,16},{36,32},{52,48},{68,64},{84,80},{100,96},{116,112},{... | collective-permute-start | bytes 638984 | tf_op jit(solution)/shard_map/ppermute | solution.py:356
  80.9 18.8 %collective-permute-start.8 = (f32[208,256]{1,0:T(8,128)S(1)}, f32[208,256]{1,0:T(8,128)S(1)}, u32[]{:S(2)}, u32[]{:S(2)}) collective-permute-start(f32[208,256]{1,0:T(8,128)S(1)} %collective-permute-done.5.refs_0_), channel_id=1, source_target_pairs={{12,0},{28,16},{44,32},{60,48},{76,64},{92,80},{108,96},{124,112},... | collective-permute-start | bytes 638984 | tf_op jit(solution)/shard_map/ppermute | solution.py:356
  82.2 18.2 %collective-permute-start.9 = (f32[208,256]{1,0:T(8,128)S(1)}, f32[208,256]{1,0:T(8,128)S(1)}, u32[]{:S(2)}, u32[]{:S(2)}) collective-permute-start(f32[208,256]{1,0:T(8,128)S(1)} %collective-permute-done.5.refs_0_), channel_id=1, source_target_pairs={{3,0},{19,16},{35,32},{51,48},{67,64},{83,80},{99,96},{115,112},{1... | collective-permute-start | bytes 638984 | tf_op jit(solution)/shard_map/ppermute | solution.py:356
  99.8 0.7 copy-start
  100.5 0.7 copy-start.2
  101.2 0.9 copy-start.1
  102.1 0.9 copy-start.3
  110.6 47.0 %all-to-all-start.4 = ((f32[16,40,256]{2,1,0:T(8,128)}), f32[16,40,256]{2,1,0:T(8,128)S(1)}, u32[]{:S(2)}, u32[]{:S(2)}) async-start(f32[16,40,256]{2,1,0:T(8,128)} %bitcast.29), calls=%async_computation.4 | async-start | bytes 1310720 | tf_op jit(solution)/shard_map/all_to_all | solution.py:407

commit v5 on v4

--- a/solution.py
+++ b/solution.py
@@ -10,8 +10,7 @@
 
 SLOTS = 56
 BACK_SLOTS = 40
-LEAVE = ((-1, -1), (-1, 0), (0, -1), (-1, -2), (-2, -1))
-LAND = ((0, 0), (-1, 0), (0, -1), (0, 1), (1, 0))
+LEAVE = ((-1, -1), (0, -1), (-2, -1), (-1, -2), (0, -2))
 SRC = ("zl", "core")
 DST = ("zh", "x", "y")
 F32 = jnp.float32
@@ -122,21 +121,43 @@
     return jnp.where((rank < slots) & (owner >= 0.0), owner * slots + rank, -1.0)
 
 
-def edge_kernel(
-    own, slots, back_slots, starts, count_ref, crossed_ref, ids_ref, dest_ref, negative_ref, got_ref, near_ref, *refs
-):
+def join_kernel(starts, crossed_ref, near_ref, *refs):
     joined = refs[: len(starts)]
-    loss_ref, back_ref, source_ref, weight_ref, table_ref, done = refs[len(starts) :]
-    table_ref[...] = near_ref[...]
+    table_ref, state_ref, full_ref, done = refs[len(starts) :]
+    height, width = table_ref.shape
+    full_ref[...] = near_ref[...]
 
     @pl.when(crossed_ref[0] == 1)
     def _():
         for start, piece in zip(starts, joined):
-            rows = table_ref.at[start : start + piece.shape[0]]
-            copy = pltpu.make_async_copy(piece, rows, done)
+            copy = pltpu.make_async_copy(piece, full_ref.at[start : start + piece.shape[0]], done)
             copy.start()
             copy.wait()
 
+    table_ref[...] = full_ref[:height]
+    rows = [full_ref[row : row + 1] for row in range(height, height + height // width)]
+    state_ref[...] = jnp.concatenate(rows, axis=1)
+
+
+def join(crossed, near, joined, starts, height):
+    return pl.pallas_call(
+        functools.partial(join_kernel, tuple(starts)),
+        out_shape=(
+            jax.ShapeDtypeStruct((height, near.shape[1]), F32),
+            jax.ShapeDtypeStruct((1, height), F32),
+        ),
+        in_specs=[SMEM, VMEM] + [pl.BlockSpec(memory_space=pl.ANY)] * len(joined),
+        out_specs=(VMEM, VMEM),
+        scratch_shapes=[pltpu.VMEM(near.shape, F32), pltpu.SemaphoreType.DMA],
+        compiler_params=pltpu.CompilerParams(vmem_limit_bytes=8 << 20),
+        name="join",
+    )(crossed, near, *joined)
+
+
+def edge_kernel(
+    own, slots, back_slots, count_ref, ids_ref, dest_ref, negative_ref, got_ref, table_ref,
+    loss_ref, back_ref, source_ref, weight_ref,
+):
     edges = ids_ref.shape[1]
     height = table_ref.shape[0]
     ids = ids_ref[...]
@@ -185,24 +206,22 @@
     back_ref[...] = pick(flag(down == place).astype(BF16), parts_of(grad, 3))
 
 
-def edge_step(count, crossed, ids, dest, negative, got, table, joined, starts, devices, own):
+def edge_step(count, ids, dest, negative, got, table, devices, own):
     edges = ids.shape[1]
     height, width = table.shape
     return pl.pallas_call(
-        functools.partial(edge_kernel, own, SLOTS, BACK_SLOTS, tuple(starts)),
+        functools.partial(edge_kernel, own, SLOTS, BACK_SLOTS),
         out_shape=(
             jax.ShapeDtypeStruct((1, edges), F32),
             jax.ShapeDtypeStruct((devices * BACK_SLOTS, width), F32),
             jax.ShapeDtypeStruct((edges, width), F32),
             jax.ShapeDtypeStruct((edges, height), F32),
-            jax.ShapeDtypeStruct(table.shape, F32),
         ),
-        in_specs=[SMEM] * 2 + [VMEM] * 5 + [pl.BlockSpec(memory_space=pl.ANY)] * len(joined),
-        out_specs=(VMEM,) * 5,
-        scratch_shapes=[pltpu.SemaphoreType.DMA],
+        in_specs=[SMEM] + [VMEM] * 5,
+        out_specs=(VMEM,) * 4,
         compiler_params=pltpu.CompilerParams(vmem_limit_bytes=24 << 20),
         name="edge_step",
-    )(count, crossed, ids, dest, negative, got, table, *joined)
+    )(count, ids, dest, negative, got, table)
 
 
 def row_of(column):
@@ -356,6 +375,26 @@
     return lax.ppermute(value, axes, pairs)
 
 
+def with_state_kernel(table_ref, state_ref, full_ref):
+    height, width = table_ref.shape
+    full_ref[:height] = table_ref[...]
+    for row in range(height // width):
+        full_ref[height + row : height + row + 1] = state_ref[:, row * width : (row + 1) * width]
+    full_ref[height + height // width :] = jnp.zeros((full_ref.shape[0] - height - height // width, width), F32)
+
+
+def with_state(table, state):
+    height, width = table.shape
+    return pl.pallas_call(
+        with_state_kernel,
+        out_shape=jax.ShapeDtypeStruct((height + -(-height // (8 * width)) * 8, width), F32),
+        in_specs=[VMEM] * 2,
+        out_specs=VMEM,
+        compiler_params=pltpu.CompilerParams(vmem_limit_bytes=8 << 20),
+        name="with_state",
+    )(table, state)
+
+
 def shifted(table):
     height = table.shape[0]
     wide, deep = lax.axis_size("x"), lax.axis_size("y")
@@ -363,28 +402,18 @@
     count = len(LEAVE)
     size = -(-height // (16 * count)) * 16
     starts = [min(size * piece, height - size) for piece in range(count)]
-    spot = lambda at: (at[0] % wide) * deep + at[1] % deep
-    leave, land = [spot(at) for at in LEAVE], [spot(at) for at in LAND]
-    near = permute(
-        table, DST, [(j, j + 1) for j in range(2 * plane - 1) if j != plane - 1]
-    )
+    leave = [(x % wide) * deep + y % deep for x, y in LEAVE]
+    near = permute(table, DST, [(j, j + 1) for j in range(2 * plane - 1) if j != plane - 1])
     pieces = [table[start : start + size] for start in starts]
-    spread = [permute(pieces[k], ("x", "y"), [(leave[0], leave[k])]) for k in range(1, count)]
+    for k in range(1, count):
+        pieces[k] = permute(pieces[k], ("x", "y"), [(leave[0], leave[k])])
+    joined = [permute(pieces[k], DST, [(z * plane + leave[k], (1 - z) * plane) for z in range(2)]) for k in range(count)]
     at = lax.axis_index("x") * deep + lax.axis_index("y")
-    going = jnp.where(at == leave[0], pieces[0], sum(spread))
-    come = permute(
-        going,
-        DST,
-        [(z * plane + leave[k], (1 - z) * plane + land[k]) for z in range(2) for k in range(count)],
-    )
-    joined = [come] + [permute(come, ("x", "y"), [(land[k], land[0])]) for k in range(1, count)]
-    return near, joined, starts, (at == land[0]).astype(jnp.int32), going, come
+    return near, joined, starts, (at == 0).astype(jnp.int32), pieces[1:]
 
 
 def on_device(src_emb, src_state, dst_emb, dst_state, src_ids, dst_ids, neg_ids, counts):
     devices = lax.axis_size(SRC)
-    behind = lax.axis_size(DST)
-    pairs = [(source, (source + 1) % behind) for source in range(behind)]
     rows, rows_state = src_emb[0, 0], src_state[0]
     own = rows.shape[0]
     core = lax.axis_index("core")
@@ -393,17 +422,14 @@
     ids = src_ids[0]
     edge = lax.broadcasted_iota(jnp.int32, ids.shape, 1)
     ids = jnp.where(edge < counts[0, 0], ids, -1)
-    near, joined, starts, crossed, going, come = shifted(dst_emb[0, 0])
+    near, joined, starts, crossed, spread = shifted(with_state(dst_emb[0, 0], dst_state[0]))
     other = permute(rows, "core", [(0, 1), (1, 0)])
     all_ids = lax.all_to_all(jnp.broadcast_to(ids, (devices, ids.shape[1])), SRC, 0, 0, tiled=True)
 
-    send = pack_rows(place, after(all_ids, going), rows, other, SLOTS)
-    got = lax.all_to_all(after(send, come, near), "zl", 0, 0, tiled=True)
-    table_state = permute(after(dst_state[0], send), DST, pairs)
-    got = after(got, table_state)
-    loss, back, source, weight, table = edge_step(
-        counts, crossed.reshape(1), ids, dst_ids[0], neg_ids[0], got, near, joined, starts, devices, own
-    )
+    send = pack_rows(place, all_ids, rows, other, SLOTS)
+    got = lax.all_to_all(after(send, near, *spread), "zl", 0, 0, tiled=True)
+    table, table_state = join(crossed.reshape(1), near, joined, starts, dst_emb.shape[2])
+    loss, back, source, weight = edge_step(counts, ids, dst_ids[0], neg_ids[0], got, table, devices, own)
     back = lax.all_to_all(back, SRC, 0, 0, tiled=True)
     dst_new, dst_state_new, over, local = table_step(place, weight, source, table, table_state, all_ids, own)
     src_new, src_state_new = source_step(local, back, rows, rows_state)

time: 162 us -> 162 us (level)
  starting transfers between devices: 48.3 us -> 68.9 us
  waiting for transfers between devices: 87 us -> 70.8 us
  local copies, waits for them, and re-layouts: 5.16 us -> 3.46 us
  other arithmetic: 1.77 us -> 0.08 us
    all_to_all x1, starting transfers between devices: 14.9 us -> 34.2 us  [on_device(): back = lax.all_to_all(back, SRC, 0, 0, tiled=True)]
    ppermute x12 -> x11, waiting for transfers between devices: 43.5 us -> 32.5 us  [permute(): return lax.ppermute(value, axes, pairs)]
    all_to_all x1, waiting for transfers between devices: 5.84 us -> 0.01 us  [on_device(): got = lax.all_to_all(after(send, near, *spread), 'zl', 0, 0, tiled=True)]
    pallas_call x1 -> x3, Pallas kernels: 7.58 us -> 6.69 us  [the longest x1 5.1 us: edge_step(): pl.pallas_call(functools.partial(edge_kernel, own, SLOTS, BACK_SLOTS), ou...]
    ppermute x12 -> x11, starting transfers between devices: 17.3 us -> 18 us  [permute(): return lax.ppermute(value, axes, pairs)]
  transfers between devices with their start and end apart: 15 -> 14, of which waited for: 5 -> 5; matrix products, arithmetic and copies ran while one was open for 2% -> 1% of each run, Pallas kernels for 4% -> 4%
where the time goes in v5:
time: 162 us; the launch traced here: 161 us
  waiting for transfers between devices  70.8 us (44%)
  starting transfers between devices  68.9 us (43%)
  Pallas kernels  15.3 us (9%)
  local copies, waits for them, and re-layouts  3.46 us (2%)
  between operations  1.65 us (1%)
    all_to_all x1, starting transfers between devices, on_device(): back = lax.all_to_all(back, SRC, 0, 0, tiled=True)  34.2 us
    ppermute x11, waiting for transfers between devices, permute(): return lax.ppermute(value, axes, pairs)  32.5 us
    all_to_all x1, waiting for transfers between devices, on_device(): back = lax.all_to_all(back, SRC, 0, 0, tiled=True)  29.5 us
    ppermute x11, starting transfers between devices, permute(): return lax.ppermute(value, axes, pairs)  18 us
    all_to_all x1, starting transfers between devices, on_device(): lax.all_to_all(jnp.broadcast_to(ids, (devices, ids.shape[1])), SRC, 0, 0,...  12.4 us
    all_to_all x1, waiting for transfers between devices, on_device(): lax.all_to_all(jnp.broadcast_to(ids, (devices, ids.shape[1])), SRC, 0, 0,...  8.81 us
    pallas_call x1, Pallas kernels, edge_step(): pl.pallas_call(functools.partial(edge_kernel, own, SLOTS, BACK_SLOTS), ou...  5.1 us
    all_to_all x1, starting transfers between devices, on_device(): got = lax.all_to_all(after(send, near, *spread), 'zl', 0, 0, tiled=True)  4.34 us
  transfers between devices with their start and end apart: 14, of which 5 were waited for; matrix products, arithmetic and copies ran while one was open for 1% of the time, Pallas kernels for 4%

profile of v5, /device:TPU:33, one launch (start us, length us, event | category | flops | bytes accessed | tf_op | source)
XLA Modules:
  0.0 161.1 jit_solution(17567906113336997193)
XLA Ops:
  0.6 0.0 copy-start.29
  0.6 0.0 copy-start
  0.7 1.2 copy-done
  1.9 0.0 copy-start.1
  1.9 0.7 copy-done.1
  2.6 0.0 copy-start.21
  2.6 0.0 copy-start.27
  2.6 0.1 with_state.1
  2.6 3.3 %collective-permute-start.1 = (f32[1032,256]{1,0:T(8,128)S(1)}, f32[1032,256]{1,0:T(8,128)S(1)}, u32[]{:S(2)}, u32[]{:S(2)}) collective-permute-start(f32[1032,256]{1,0:T(8,128)S(1)} %with_state.1), channel_id=1, source_target_pairs={{0,1},{1,2},{2,3},{3,4},{4,5},{5,6},{6,7},{7,8},{8,9},{9,10},{10,1... | collective-permute-start | bytes 3170312 | tf_op jit(solution)/shard_map/ppermute | solution.py:375
  5.9 2.9 %collective-permute-start = (f32[384,256]{1,0:T(8,128)}, f32[384,256]{1,0:T(8,128)S(1)}, u32[]{:S(2)}, u32[]{:S(2)}) collective-permute-start(f32[384,256]{1,0:T(8,128)} %bitcast.53), channel_id=1, source_target_pairs={{0,32},{32,0},{1,33},{33,1},{2,34},{34,2},{3,35},{35,3},{4,36},{36... | collective-permute-start | bytes 1179656 | tf_op jit(solution)/shard_map/ppermute | solution.py:375
  8.8 0.9 fusion.26
  9.7 1.3 collective-permute-start.2
  11.0 1.3 collective-permute-start.3
  12.4 1.4 collective-permute-start.4
  14.4 0.0 collective-permute-done.other_ref
  14.4 1.4 collective-permute-start.5
  15.7 0.0 copy-done.29
  15.8 0.6 broadcast_in_dim.44
  16.4 12.4 %all-to-all-start.2 = ((s32[16,1,256]{2,1,0:T(1,128)}), s32[16,1,256]{2,1,0:T(1,128)S(1)}, u32[]{:S(2)}, u32[]{:S(2)}) async-start(s32[16,1,256]{2,1,0:T(1,128)} %broadcast_in_dim.44), calls=%async_computation.2 | async-start | bytes 32768 | tf_op jit(solution)/shard_map/all_to_all | solution.py:427
  28.8 0.1 pad_add_fusion.place_ref.first_ref
  28.9 8.8 %all-to-all-done.2 = s32[16,1,256]{2,1,0:T(1,128)S(1)} async-done(((s32[16,1,256]{2,1,0:T(1,128)}), s32[16,1,256]{2,1,0:T(1,128)S(1)}, u32[]{:S(2)}, u32[]{:S(2)}) %all-to-all-start.2) | async-done | bytes 16416 | tf_op jit(solution)/shard_map/all_to_all | solution.py:427
  37.7 3.1 %pack_rows.1 = f32[448,256]{1,0:T(8,128)} custom-call(s32[3]{0:T(128)S(1)} %pad_add_fusion.place_ref.first_ref, s32[16,256]{1,0:T(8,128)S(1)} %bitcast.57, f32[384,256]{1,0:T(8,128)} %bitcast.54, f32[384,256]{1,0:T(8,128)S(1)} %collective-permute-done.other_ref), custom_call_target="tpu_custom_call" | custom-call | tf_op jit(solution)/shard_map/pack_rows/pallas_call | solution.py:101
  40.7 0.0 copy-start.25
  40.7 0.0 collective-permute-done.2
  40.7 0.0 collective-permute-done.3
  40.7 0.0 collective-permute-done.4
  40.8 0.0 collective-permute-done.5
  40.8 0.0 collective-permute-done.1.near_ref
  40.8 4.3 %all-to-all-start.3 = ((f32[8,56,256]{2,1,0:T(8,128)}), f32[8,56,256]{2,1,0:T(8,128)S(1)}, u32[]{:S(2)}, u32[]{:S(2)}) async-start(f32[8,56,256]{2,1,0:T(8,128)} %bitcast.20), calls=%async_computation.3 | async-start | bytes 917504 | tf_op jit(solution)/shard_map/all_to_all | solution.py:430
  45.1 1.3 collective-permute-start.6
  46.4 1.3 collective-permute-start.10
  47.7 1.3 collective-permute-start.7
  49.0 1.3 collective-permute-start.8
  50.3 1.3 collective-permute-start.9
  51.6 0.0 copy-start.7
  51.6 22.5 %collective-permute-done.6.refs_0_ = f32[208,256]{1,0:T(8,128)S(1)} collective-permute-done((f32[208,256]{1,0:T(8,128)S(1)}, f32[208,256]{1,0:T(8,128)S(1)}, u32[]{:S(2)}, u32[]{:S(2)}) %collective-permute-start.6) | collective-permute-done | bytes 213024 | tf_op jit(solution)/shard_map/ppermute | solution.py:375
  74.1 0.0 collective-permute-done.10.refs_4_
  74.1 0.0 collective-permute-done.7.refs_1_
  74.1 8.4 %collective-permute-done.8.refs_2_ = f32[208,256]{1,0:T(8,128)S(1)} collective-permute-done((f32[208,256]{1,0:T(8,128)}, f32[208,256]{1,0:T(8,128)S(1)}, u32[]{:S(2)}, u32[]{:S(2)}) %collective-permute-start.8) | collective-permute-done | bytes 213024 | tf_op jit(solution)/shard_map/ppermute | solution.py:375
  82.5 1.7 %collective-permute-done.9.refs_3_ = f32[208,256]{1,0:T(8,128)S(1)} collective-permute-done((f32[208,256]{1,0:T(8,128)}, f32[208,256]{1,0:T(8,128)S(1)}, u32[]{:S(2)}, u32[]{:S(2)}) %collective-permute-start.9) | collective-permute-done | bytes 213024 | tf_op jit(solution)/shard_map/ppermute | solution.py:375
  84.1 1.5 join.1
  85.7 0.0 all-to-all-done.3
  85.7 0.0 copy-done.21
  85.7 0.0 copy-done.27
  85.7 5.1 %edge_step.1 = (f32[1,256]{1,0:T(1,128)}, f32[640,256]{1,0:T(8,128)}, f32[256,256]{1,0:T(8,128)S(1)}, f32[256,1024]{1,0:T(8,128)S(1)}) custom-call(s32[1,1]{1,0:T(1,128)} %copy.41.count_ref, s32[1,256]{1,0:T(1,128)S(1)} %compare_select_fusion.1.ids_ref, s32[1,256]{1,0:T(1,128)S(1)} %bitcast.66, s32[1,1024]{1,0:T(1,128)S(1)} %bitcast.73, ...), custom_call_target="tpu_custom_call" | custom-call | tf_op jit(solution)/shard_map/edge_step/pallas_call | solution.py:212
  90.8 34.2 %all-to-all-start.4 = ((f32[16,40,256]{2,1,0:T(8,128)}), f32[16,40,256]{2,1,0:T(8,128)S(1)}, u32[]{:S(2)}, u32[]{:S(2)}) async-start(f32[16,40,256]{2,1,0:T(8,128)} %bitcast.24), calls=%async_computation.4 | async-start | bytes 1310720 | tf_op jit(solution)/shard_map/all_to_all | solution.py:433
  125.0 0.0 copy-done.7
  125.0 2.6 %table_step.1 = (f32[1024,256]{1,0:T(8,128)}, f32[1,1024]{1,0:T(1,128)}, f32[1,1]{1,0:T(1,128)}, f32[640,1]{1,0:T(8,128)S(1)}) custom-call(s32[3]{0:T(128)S(1)} %pad_add_fusion.place_ref.first_ref, f32[256,1024]{1,0:T(8,128)S(1)} %get-tuple-element.106.weight_ref, f32[256,256]{1,0:T(8,128)S(1)} %get-tuple-element.107.source_ref, ...), custom_call_target="tpu_custom_call" | custom-call | tf_op jit(solution)/shard_map/table_step/pallas_call | solution.py:264
  127.6 29.5 %all-to-all-done.4 = f32[16,40,256]{2,1,0:T(8,128)S(1)} async-done(((f32[16,40,256]{2,1,0:T(8,128)}), f32[16,40,256]{2,1,0:T(8,128)S(1)}, u32[]{:S(2)}, u32[]{:S(2)}) %all-to-all-start.4) | async-done | bytes 655392 | tf_op jit(solution)/shard_map/all_to_all | solution.py:433
  157.2 0.0 copy-done.25
  157.2 2.9 %source_step.1 = (f32[384,256]{1,0:T(8,128)}, f32[1,384]{1,0:T(1,128)}) custom-call(f32[640,1]{1,0:T(8,128)S(1)} %get-tuple-element.110.local_ref, f32[640,256]{1,0:T(8,128)S(1)} %bitcast.49, f32[384,256]{1,0:T(8,128)} %bitcast.55, f32[1,384]{1,0:T(1,128)S(1)} %bitcast.69), custom_call_target="tpu_custom_call" | custom-call | tf_op jit(solution)/shard_map/source_step/pallas_call | solution.py:288
  160.0 0.9 while.17
  (3 shorter events, 0.0 us)
Async XLA Ops:
  0.6 15.1 %copy-start.29 = (s32[1,1,256]{2,1,0:T(1,128)S(1)}, s32[1,1,256]{2,1,0:T(1,128)}, u32[]{:S(2)}) copy-start(s32[1,1,256]{2,1,0:T(1,128)} %param.14) | copy-start | bytes 3076
  0.6 1.2 copy-start
  1.9 0.7 copy-start.1
  2.6 83.1 %copy-start.21 = (s32[1,1,256]{2,1,0:T(1,128)S(1)}, s32[1,1,256]{2,1,0:T(1,128)}, u32[]{:S(2)}) copy-start(s32[1,1,256]{2,1,0:T(1,128)} %param.15) | copy-start | bytes 3076
  2.6 83.1 %copy-start.27 = (s32[1,1,1024]{2,1,0:T(1,128)S(1)}, s32[1,1,1024]{2,1,0:T(1,128)}, u32[]{:S(2)}) copy-start(s32[1,1,1024]{2,1,0:T(1,128)} %param.16) | copy-start | bytes 12292
  2.6 38.1 %collective-permute-start.1 = (f32[1032,256]{1,0:T(8,128)S(1)}, f32[1032,256]{1,0:T(8,128)S(1)}, u32[]{:S(2)}, u32[]{:S(2)}) collective-permute-start(f32[1032,256]{1,0:T(8,128)S(1)} %with_state.1), channel_id=1, source_target_pairs={{0,1},{1,2},{2,3},{3,4},{4,5},{5,6},{6,7},{7,8},{8,9},{9,10},{10,1... | collective-permute-start | bytes 3170312 | tf_op jit(solution)/shard_map/ppermute | solution.py:375
  5.9 8.5 %collective-permute-start = (f32[384,256]{1,0:T(8,128)}, f32[384,256]{1,0:T(8,128)S(1)}, u32[]{:S(2)}, u32[]{:S(2)}) collective-permute-start(f32[384,256]{1,0:T(8,128)} %bitcast.53), channel_id=1, source_target_pairs={{0,32},{32,0},{1,33},{33,1},{2,34},{34,2},{3,35},{35,3},{4,36},{36... | collective-permute-start | bytes 1179656 | tf_op jit(solution)/shard_map/ppermute | solution.py:375
  9.7 31.0 %collective-permute-start.2 = (f32[208,256]{1,0:T(8,128)}, f32[208,256]{1,0:T(8,128)}, u32[]{:S(2)}, u32[]{:S(2)}) collective-permute-start(f32[208,256]{1,0:T(8,128)} %get-tuple-element.164), channel_id=1, source_target_pairs={{15,3},{31,19},{47,35},{63,51},{79,67},{95,83},{111,99},{127,115},... | collective-permute-start | bytes 638984 | tf_op jit(solution)/shard_map/ppermute | solution.py:375
  11.0 29.7 %collective-permute-start.3 = (f32[208,256]{1,0:T(8,128)}, f32[208,256]{1,0:T(8,128)}, u32[]{:S(2)}, u32[]{:S(2)}) collective-permute-start(f32[208,256]{1,0:T(8,128)} %get-tuple-element.163), channel_id=1, source_target_pairs={{15,11},{31,27},{47,43},{63,59},{79,75},{95,91},{111,107},{127,123... | collective-permute-start | bytes 638984 | tf_op jit(solution)/shard_map/ppermute | solution.py:375
  12.4 28.4 %collective-permute-start.4 = (f32[208,256]{1,0:T(8,128)}, f32[208,256]{1,0:T(8,128)}, u32[]{:S(2)}, u32[]{:S(2)}) collective-permute-start(f32[208,256]{1,0:T(8,128)} %get-tuple-element.162), channel_id=1, source_target_pairs={{15,14},{31,30},{47,46},{63,62},{79,78},{95,94},{111,110},{127,126... | collective-permute-start | bytes 638984 | tf_op jit(solution)/shard_map/ppermute | solution.py:375
  14.4 26.4 %collective-permute-start.5 = (f32[208,256]{1,0:T(8,128)}, f32[208,256]{1,0:T(8,128)}, u32[]{:S(2)}, u32[]{:S(2)}) collective-permute-start(f32[208,256]{1,0:T(8,128)} %get-tuple-element.161), channel_id=1, source_target_pairs={{15,2},{31,18},{47,34},{63,50},{79,66},{95,82},{111,98},{127,114},... | collective-permute-start | bytes 638984 | tf_op jit(solution)/shard_map/ppermute | solution.py:375
  16.4 21.3 %all-to-all-start.2 = ((s32[16,1,256]{2,1,0:T(1,128)}), s32[16,1,256]{2,1,0:T(1,128)S(1)}, u32[]{:S(2)}, u32[]{:S(2)}) async-start(s32[16,1,256]{2,1,0:T(1,128)} %broadcast_in_dim.44), calls=%async_computation.2 | async-start | bytes 32768 | tf_op jit(solution)/shard_map/all_to_all | solution.py:427
  40.7 116.4 %copy-start.25 = (f32[1,1,384]{2,1,0:T(1,128)S(1)}, f32[1,1,384]{2,1,0:T(1,128)}, u32[]{:S(2)}) copy-start(f32[1,1,384]{2,1,0:T(1,128)} %param.11) | copy-start | bytes 4612
  40.8 44.9 %all-to-all-start.3 = ((f32[8,56,256]{2,1,0:T(8,128)}), f32[8,56,256]{2,1,0:T(8,128)S(1)}, u32[]{:S(2)}, u32[]{:S(2)}) async-start(f32[8,56,256]{2,1,0:T(8,128)} %bitcast.20), calls=%async_computation.3 | async-start | bytes 917504 | tf_op jit(solution)/shard_map/all_to_all | solution.py:430
  45.1 29.0 %collective-permute-start.6 = (f32[208,256]{1,0:T(8,128)S(1)}, f32[208,256]{1,0:T(8,128)S(1)}, u32[]{:S(2)}, u32[]{:S(2)}) collective-permute-start(f32[208,256]{1,0:T(8,128)S(1)} %get-tuple-element.160), channel_id=1, source_target_pairs={{15,16},{31,0},{47,48},{63,32},{79,80},{95,64},{111,112},{127,96},... | collective-permute-start | bytes 638984 | tf_op jit(solution)/shard_map/ppermute | solution.py:375
  46.4 27.7 %collective-permute-start.10 = (f32[208,256]{1,0:T(8,128)}, f32[208,256]{1,0:T(8,128)S(1)}, u32[]{:S(2)}, u32[]{:S(2)}) collective-permute-start(f32[208,256]{1,0:T(8,128)} %collective-permute-done.5), channel_id=1, source_target_pairs={{2,16},{18,0},{34,48},{50,32},{66,80},{82,64},{98,112},{114,96},{1... | collective-permute-start | bytes 638984 | tf_op jit(solution)/shard_map/ppermute | solution.py:375
  47.7 26.4 %collective-permute-start.7 = (f32[208,256]{1,0:T(8,128)}, f32[208,256]{1,0:T(8,128)S(1)}, u32[]{:S(2)}, u32[]{:S(2)}) collective-permute-start(f32[208,256]{1,0:T(8,128)} %collective-permute-done.2), channel_id=1, source_target_pairs={{3,16},{19,0},{35,48},{51,32},{67,80},{83,64},{99,112},{115,96},{1... | collective-permute-start | bytes 638984 | tf_op jit(solution)/shard_map/ppermute | solution.py:375
  49.0 33.5 %collective-permute-start.8 = (f32[208,256]{1,0:T(8,128)}, f32[208,256]{1,0:T(8,128)S(1)}, u32[]{:S(2)}, u32[]{:S(2)}) collective-permute-start(f32[208,256]{1,0:T(8,128)} %collective-permute-done.3), channel_id=1, source_target_pairs={{11,16},{27,0},{43,48},{59,32},{75,80},{91,64},{107,112},{123,96},... | collective-permute-start | bytes 638984 | tf_op jit(solution)/shard_map/ppermute | solution.py:375
  50.3 33.8 %collective-permute-start.9 = (f32[208,256]{1,0:T(8,128)}, f32[208,256]{1,0:T(8,128)S(1)}, u32[]{:S(2)}, u32[]{:S(2)}) collective-permute-start(f32[208,256]{1,0:T(8,128)} %collective-permute-done.4), channel_id=1, source_target_pairs={{14,16},{30,0},{46,48},{62,32},{78,80},{94,64},{110,112},{126,96},... | collective-permute-start | bytes 638984 | tf_op jit(solution)/shard_map/ppermute | solution.py:375
  51.6 73.4 %copy-start.7 = (s32[1,256]{1,0:T(1,128)}, s32[1,256]{1,0:T(1,128)S(1)}, u32[]{:S(2)}) copy-start(s32[1,256]{1,0:T(1,128)S(1)} %compare_select_fusion.1.ids_ref) | copy-start | bytes 3076
  90.8 66.3 %all-to-all-start.4 = ((f32[16,40,256]{2,1,0:T(8,128)}), f32[16,40,256]{2,1,0:T(8,128)S(1)}, u32[]{:S(2)}, u32[]{:S(2)}) async-start(f32[16,40,256]{2,1,0:T(8,128)} %bitcast.24), calls=%async_computation.4 | async-start | bytes 1310720 | tf_op jit(solution)/shard_map/all_to_all | solution.py:433

commit v6 on v5

--- a/solution.py
+++ b/solution.py
@@ -10,7 +10,8 @@
 
 SLOTS = 56
 BACK_SLOTS = 40
-LEAVE = ((-1, -1), (0, -1), (-2, -1), (-1, -2), (0, -2))
+LEAVE = ((-1, -1), (-1, 0), (0, -1), (-1, -2), (-2, -1), (-1, 1))
+LAND = ((0, 0), (2, 0), (1, -1), (0, 1), (1, 0), (1, 1))
 SRC = ("zl", "core")
 DST = ("zh", "x", "y")
 F32 = jnp.float32
@@ -103,7 +104,7 @@
         out_shape=jax.ShapeDtypeStruct((chips * slots, rows.shape[1]), F32),
         in_specs=[SMEM, VMEM, VMEM, VMEM],
         out_specs=VMEM,
-        compiler_params=pltpu.CompilerParams(vmem_limit_bytes=16 << 20),
+        compiler_params=pltpu.CompilerParams(vmem_limit_bytes=8 << 20),
         name="pack_rows",
     )(place, ids, rows, other)
 
@@ -219,7 +220,7 @@
         ),
         in_specs=[SMEM] + [VMEM] * 5,
         out_specs=(VMEM,) * 4,
-        compiler_params=pltpu.CompilerParams(vmem_limit_bytes=24 << 20),
+        compiler_params=pltpu.CompilerParams(vmem_limit_bytes=16 << 20),
         name="edge_step",
     )(count, ids, dest, negative, got, table)
 
@@ -271,7 +272,7 @@
         ),
         in_specs=[SMEM] + [VMEM] * 5,
         out_specs=(VMEM,) * 4,
-        compiler_params=pltpu.CompilerParams(vmem_limit_bytes=24 << 20),
+        compiler_params=pltpu.CompilerParams(vmem_limit_bytes=16 << 20),
         name="table_step",
     )(place, weight, source, table, state, ids)
 
@@ -293,7 +294,7 @@
         ),
         in_specs=[VMEM] * 4,
         out_specs=(VMEM, VMEM),
-        compiler_params=pltpu.CompilerParams(vmem_limit_bytes=16 << 20),
+        compiler_params=pltpu.CompilerParams(vmem_limit_bytes=8 << 20),
         name="source_step",
     )(local, back, rows, state)
 
@@ -313,7 +314,7 @@
         out_shape=(jax.ShapeDtypeStruct(rows.shape, F32), jax.ShapeDtypeStruct(table.shape, F32)),
         in_specs=[VMEM] * 2,
         out_specs=(VMEM, VMEM),
-        compiler_params=pltpu.CompilerParams(vmem_limit_bytes=16 << 20),
+        compiler_params=pltpu.CompilerParams(vmem_limit_bytes=8 << 20),
         name="held",
     )(rows, table)
 
@@ -328,7 +329,7 @@
         out_shape=(jax.ShapeDtypeStruct(emb.shape, F32), jax.ShapeDtypeStruct(state.shape, F32)),
         in_specs=[VMEM] * 3,
         out_specs=(VMEM, VMEM),
-        compiler_params=pltpu.CompilerParams(vmem_limit_bytes=16 << 20),
+        compiler_params=pltpu.CompilerParams(vmem_limit_bytes=8 << 20),
         name="update",
     )(emb, state, grad)
 
@@ -395,21 +396,29 @@
     )(table, state)
 
 
-def shifted(table):
-    height = table.shape[0]
+def shifted(table, state):
     wide, deep = lax.axis_size("x"), lax.axis_size("y")
     plane = wide * deep
     count = len(LEAVE)
-    size = -(-height // (16 * count)) * 16
-    starts = [min(size * piece, height - size) for piece in range(count)]
-    leave = [(x % wide) * deep + y % deep for x, y in LEAVE]
-    near = permute(table, DST, [(j, j + 1) for j in range(2 * plane - 1) if j != plane - 1])
-    pieces = [table[start : start + size] for start in starts]
-    for k in range(1, count):
-        pieces[k] = permute(pieces[k], ("x", "y"), [(leave[0], leave[k])])
-    joined = [permute(pieces[k], DST, [(z * plane + leave[k], (1 - z) * plane) for z in range(2)]) for k in range(count)]
+    full = with_state(table, state)
+    size = -(-full.shape[0] // (8 * count)) * 8
+    rest = full.shape[0] - size
+    starts = [rest] + [min(size * piece, rest - size) for piece in range(count - 1)]
+    spot = lambda at: (at[0] % wide) * deep + at[1] % deep
+    leave, land = [spot(at) for at in LEAVE], [spot(at) for at in LAND]
+    spread = [
+        permute(table[starts[k] : starts[k] + size], ("x", "y"), [(leave[0], leave[k])]) for k in range(1, count)
+    ]
     at = lax.axis_index("x") * deep + lax.axis_index("y")
-    return near, joined, starts, (at == 0).astype(jnp.int32), pieces[1:]
+    going = jnp.where(at == leave[0], full[starts[0] :], sum(spread))
+    near = permute(after(full, *spread), DST, [(j, j + 1) for j in range(2 * plane - 1) if j != plane - 1])
+    come = permute(
+        going,
+        DST,
+        [(z * plane + leave[k], (1 - z) * plane + land[k]) for z in range(2) for k in range(count)],
+    )
+    joined = [come] + [permute(come, ("x", "y"), [(land[k], land[0])]) for k in range(1, count)]
+    return near, joined, starts, (at == land[0]).astype(jnp.int32), spread[-1]
 
 
 def on_device(src_emb, src_state, dst_emb, dst_state, src_ids, dst_ids, neg_ids, counts):
@@ -422,12 +431,12 @@
     ids = src_ids[0]
     edge = lax.broadcasted_iota(jnp.int32, ids.shape, 1)
     ids = jnp.where(edge < counts[0, 0], ids, -1)
-    near, joined, starts, crossed, spread = shifted(with_state(dst_emb[0, 0], dst_state[0]))
-    other = permute(rows, "core", [(0, 1), (1, 0)])
+    near, joined, starts, crossed, spread = shifted(dst_emb[0, 0], dst_state[0])
+    other = permute(after(rows, spread), "core", [(0, 1), (1, 0)])
     all_ids = lax.all_to_all(jnp.broadcast_to(ids, (devices, ids.shape[1])), SRC, 0, 0, tiled=True)
 
     send = pack_rows(place, all_ids, rows, other, SLOTS)
-    got = lax.all_to_all(after(send, near, *spread), "zl", 0, 0, tiled=True)
+    got = lax.all_to_all(after(send, near, joined[0]), "zl", 0, 0, tiled=True)
     table, table_state = join(crossed.reshape(1), near, joined, starts, dst_emb.shape[2])
     loss, back, source, weight = edge_step(counts, ids, dst_ids[0], neg_ids[0], got, table, devices, own)
     back = lax.all_to_all(back, SRC, 0, 0, tiled=True)

time: 162 us -> 135 us (0.83)
  the two profiles are of different devices: /device:TPU:33 before, /device:TPU:47 now
where the time goes in v6:
time: 135 us; the launch traced here: 134 us
  waiting for transfers between devices  62.8 us (47%)
  starting transfers between devices  48.9 us (36%)
  Pallas kernels  14.6 us (11%)
  local copies, waits for them, and re-layouts  3.86 us (3%)
  between operations  1.71 us (1%)
    all_to_all x1, waiting for transfers between devices, on_device(): back = lax.all_to_all(back, SRC, 0, 0, tiled=True)  29.5 us
    ppermute x13, starting transfers between devices, permute(): return lax.ppermute(value, axes, pairs)  26.7 us
    all_to_all x1, waiting for transfers between devices, on_device(): got = lax.all_to_all(after(send, near, joined[0]), 'zl', 0, 0, tiled=True)  19.9 us
    all_to_all x1, waiting for transfers between devices, on_device(): lax.all_to_all(jnp.broadcast_to(ids, (devices, ids.shape[1])), SRC, 0, 0,...  11.2 us
    all_to_all x1, starting transfers between devices, on_device(): got = lax.all_to_all(after(send, near, joined[0]), 'zl', 0, 0, tiled=True)  8.64 us
    all_to_all x1, starting transfers between devices, on_device(): back = lax.all_to_all(back, SRC, 0, 0, tiled=True)  7.54 us
    all_to_all x1, starting transfers between devices, on_device(): lax.all_to_all(jnp.broadcast_to(ids, (devices, ids.shape[1])), SRC, 0, 0,...  5.97 us
    pallas_call x1, Pallas kernels, edge_step(): pl.pallas_call(functools.partial(edge_kernel, own, SLOTS, BACK_SLOTS), ou...  5.78 us
  transfers between devices with their start and end apart: 16, of which 4 were waited for; matrix products, arithmetic and copies ran while one was open for 1% of the time, Pallas kernels for 4%

profile of v6, /device:TPU:47, one launch (start us, length us, event | category | flops | bytes accessed | tf_op | source)
XLA Modules:
  0.0 133.8 jit_solution(10589392338853841231)
XLA Ops:
  0.6 0.0 copy-start.27
  0.6 1.3 slice_bitcast_fusion
  2.0 0.0 copy-start.21
  2.0 1.3 collective-permute-start
  3.3 0.7 collective-permute-start.2
  4.0 0.7 collective-permute-start.3
  4.6 0.7 collective-permute-start.4
  5.3 1.3 collective-permute-start.5
  6.7 0.0 copy-start
  6.7 1.2 copy-done
  7.9 0.0 copy-start.1
  7.9 0.7 copy-done.1
  8.6 0.1 with_state.1
  8.6 2.2 %collective-permute-done = f32[176,256]{1,0:T(8,128)S(1)} collective-permute-done((f32[176,256]{1,0:T(8,128)S(1)}, f32[176,256]{1,0:T(8,128)S(1)}, u32[]{:S(2)}, u32[]{:S(2)}) %collective-permute-start) | collective-permute-done | bytes 180256 | tf_op jit(solution)/shard_map/ppermute | solution.py:376
  10.8 0.0 collective-permute-done.2
  10.8 0.0 collective-permute-done.3
  10.8 0.0 collective-permute-done.4
  10.8 0.0 collective-permute-done.5
  10.8 6.1 %collective-permute-start.6 = (f32[1032,256]{1,0:T(8,128)S(1)}, f32[1032,256]{1,0:T(8,128)S(1)}, u32[]{:S(2)}, u32[]{:S(2)}) collective-permute-start(f32[1032,256]{1,0:T(8,128)S(1)} %with_state.1), channel_id=1, source_target_pairs={{0,1},{1,2},{2,3},{3,4},{4,5},{5,6},{6,7},{7,8},{8,9},{9,10},{10,1... | collective-permute-start | bytes 3170312 | tf_op jit(solution)/shard_map/ppermute | solution.py:376
  17.6 3.7 %collective-permute-start.1 = (f32[384,256]{1,0:T(8,128)}, f32[384,256]{1,0:T(8,128)S(1)}, u32[]{:S(2)}, u32[]{:S(2)}) collective-permute-start(f32[384,256]{1,0:T(8,128)} %bitcast.63), channel_id=1, source_target_pairs={{0,32},{32,0},{1,33},{33,1},{2,34},{34,2},{3,35},{35,3},{4,36},{36... | collective-permute-start | bytes 1179656 | tf_op jit(solution)/shard_map/ppermute | solution.py:376
  21.3 1.0 slice_select_fusion
  22.3 8.9 %collective-permute-start.7 = (f32[176,256]{1,0:T(8,128)S(1)}, f32[176,256]{1,0:T(8,128)S(1)}, u32[]{:S(2)}, u32[]{:S(2)}) collective-permute-start(f32[176,256]{1,0:T(8,128)S(1)} %slice_select_fusion), channel_id=1, source_target_pairs={{15,16},{12,24},{3,23},{14,17},{11,20},{13,21},{31,0},{28,8},{19,7... | collective-permute-start | bytes 540680 | tf_op jit(solution)/shard_map/ppermute | solution.py:376
  31.2 0.0 copy-done.27
  31.3 0.6 broadcast_in_dim.44
  31.9 6.0 %all-to-all-start.2 = ((s32[16,1,256]{2,1,0:T(1,128)}), s32[16,1,256]{2,1,0:T(1,128)S(1)}, u32[]{:S(2)}, u32[]{:S(2)}) async-start(s32[16,1,256]{2,1,0:T(1,128)} %broadcast_in_dim.44), calls=%async_computation.2 | async-start | bytes 32768 | tf_op jit(solution)/shard_map/all_to_all | solution.py:436
  37.9 0.1 pad_add_fusion.place_ref.first_ref
  37.9 11.2 %all-to-all-done.2 = s32[16,1,256]{2,1,0:T(1,128)S(1)} async-done(((s32[16,1,256]{2,1,0:T(1,128)}), s32[16,1,256]{2,1,0:T(1,128)S(1)}, u32[]{:S(2)}, u32[]{:S(2)}) %all-to-all-start.2) | async-done | bytes 16416 | tf_op jit(solution)/shard_map/all_to_all | solution.py:436
  49.1 0.0 collective-permute-done.1.other_ref
  49.1 3.1 %pack_rows.1 = f32[448,256]{1,0:T(8,128)} custom-call(s32[3]{0:T(128)S(1)} %pad_add_fusion.place_ref.first_ref, s32[16,256]{1,0:T(8,128)S(1)} %bitcast.67, f32[384,256]{1,0:T(8,128)} %bitcast.64, f32[384,256]{1,0:T(8,128)S(1)} %collective-permute-done.1.other_ref), custom_call_target="tpu_custom_call" | custom-call | tf_op jit(solution)/shard_map/pack_rows/pallas_call | solution.py:102
  52.2 0.0 copy-start.25
  52.2 0.0 collective-permute-done.7.refs_0_
  52.2 0.0 collective-permute-done.6.near_ref
  52.2 8.6 %all-to-all-start.3 = ((f32[8,56,256]{2,1,0:T(8,128)}), f32[8,56,256]{2,1,0:T(8,128)S(1)}, u32[]{:S(2)}, u32[]{:S(2)}) async-start(f32[8,56,256]{2,1,0:T(8,128)} %bitcast.25), calls=%async_computation.3 | async-start | bytes 917504 | tf_op jit(solution)/shard_map/all_to_all | solution.py:439
  60.8 0.7 collective-permute-start.10
  61.5 0.7 collective-permute-start.11
  62.2 0.7 collective-permute-start.12
  62.9 0.7 collective-permute-start.8
  63.5 0.7 collective-permute-start.9
  64.2 0.0 copy-start.7
  64.2 0.0 collective-permute-done.10.refs_3_
  64.2 0.0 collective-permute-done.11.refs_4_
  64.3 0.0 collective-permute-done.12.refs_5_
  64.3 0.0 collective-permute-done.8.refs_1_
  64.3 0.0 collective-permute-done.9.refs_2_
  64.3 0.2 join.1
  64.5 19.9 %all-to-all-done.3 = f32[8,56,256]{2,1,0:T(8,128)S(1)} async-done(((f32[8,56,256]{2,1,0:T(8,128)}), f32[8,56,256]{2,1,0:T(8,128)S(1)}, u32[]{:S(2)}, u32[]{:S(2)}) %all-to-all-start.3) | async-done | bytes 458784 | tf_op jit(solution)/shard_map/all_to_all | solution.py:439
  84.3 0.0 copy-done.21
  84.3 5.8 %edge_step.1 = (f32[1,256]{1,0:T(1,128)}, f32[640,256]{1,0:T(8,128)}, f32[256,256]{1,0:T(8,128)S(1)}, f32[256,1024]{1,0:T(8,128)S(1)}) custom-call(s32[1,1]{1,0:T(1,128)} %copy.41.count_ref, s32[1,256]{1,0:T(1,128)S(1)} %compare_select_fusion.1.ids_ref, s32[1,256]{1,0:T(1,128)S(1)} %bitcast.76, s32[1,1024]{1,0:T(1,128)} %bitcast.15.negative_ref, ...), custom_call_target="tpu_custom_call" | custom-call | tf_op jit(solution)/shard_map/edge_step/pallas_call | solution.py:213
  90.1 7.5 %all-to-all-start.4 = ((f32[16,40,256]{2,1,0:T(8,128)}), f32[16,40,256]{2,1,0:T(8,128)S(1)}, u32[]{:S(2)}, u32[]{:S(2)}) async-start(f32[16,40,256]{2,1,0:T(8,128)} %bitcast.29), calls=%async_computation.4 | async-start | bytes 1310720 | tf_op jit(solution)/shard_map/all_to_all | solution.py:442
  97.7 0.0 copy-done.7
  97.7 2.6 %table_step.1 = (f32[1024,256]{1,0:T(8,128)}, f32[1,1024]{1,0:T(1,128)}, f32[1,1]{1,0:T(1,128)}, f32[640,1]{1,0:T(8,128)S(1)}) custom-call(s32[3]{0:T(128)S(1)} %pad_add_fusion.place_ref.first_ref, f32[256,1024]{1,0:T(8,128)S(1)} %get-tuple-element.110.weight_ref, f32[256,256]{1,0:T(8,128)S(1)} %get-tuple-element.111.source_ref, ...), custom_call_target="tpu_custom_call" | custom-call | tf_op jit(solution)/shard_map/table_step/pallas_call | solution.py:265
  100.3 29.5 %all-to-all-done.4 = f32[16,40,256]{2,1,0:T(8,128)S(1)} async-done(((f32[16,40,256]{2,1,0:T(8,128)}), f32[16,40,256]{2,1,0:T(8,128)S(1)}, u32[]{:S(2)}, u32[]{:S(2)}) %all-to-all-start.4) | async-done | bytes 655392 | tf_op jit(solution)/shard_map/all_to_all | solution.py:442
  129.8 0.0 copy-done.25
  129.8 2.9 %source_step.1 = (f32[384,256]{1,0:T(8,128)}, f32[1,384]{1,0:T(1,128)}) custom-call(f32[640,1]{1,0:T(8,128)S(1)} %get-tuple-element.114.local_ref, f32[640,256]{1,0:T(8,128)S(1)} %bitcast.60, f32[384,256]{1,0:T(8,128)} %bitcast.65, f32[1,384]{1,0:T(1,128)S(1)} %bitcast.79), custom_call_target="tpu_custom_call" | custom-call | tf_op jit(solution)/shard_map/source_step/pallas_call | solution.py:289
  132.7 0.9 while.17
  (3 shorter events, 0.0 us)
Async XLA Ops:
  0.6 30.6 %copy-start.27 = (s32[1,1,256]{2,1,0:T(1,128)S(1)}, s32[1,1,256]{2,1,0:T(1,128)}, u32[]{:S(2)}) copy-start(s32[1,1,256]{2,1,0:T(1,128)} %param.14) | copy-start | bytes 3076
  2.0 82.4 %copy-start.21 = (s32[1,1,256]{2,1,0:T(1,128)S(1)}, s32[1,1,256]{2,1,0:T(1,128)}, u32[]{:S(2)}) copy-start(s32[1,1,256]{2,1,0:T(1,128)} %param.15) | copy-start | bytes 3076
  2.0 8.8 %collective-permute-start = (f32[176,256]{1,0:T(8,128)S(1)}, f32[176,256]{1,0:T(8,128)S(1)}, u32[]{:S(2)}, u32[]{:S(2)}) collective-permute-start(f32[176,256]{1,0:T(8,128)S(1)} %get-tuple-element.167), channel_id=1, source_target_pairs={{15,13},{31,29},{47,45},{63,61},{79,77},{95,93},{111,109},{127,125... | collective-permute-start | bytes 540680 | tf_op jit(solution)/shard_map/ppermute | solution.py:376
  3.3 7.5 %collective-permute-start.2 = (f32[176,256]{1,0:T(8,128)S(1)}, f32[176,256]{1,0:T(8,128)S(1)}, u32[]{:S(2)}, u32[]{:S(2)}) collective-permute-start(f32[176,256]{1,0:T(8,128)S(1)} %get-tuple-element.166), channel_id=1, source_target_pairs={{15,12},{31,28},{47,44},{63,60},{79,76},{95,92},{111,108},{127,124... | collective-permute-start | bytes 540680 | tf_op jit(solution)/shard_map/ppermute | solution.py:376
  4.0 6.8 %collective-permute-start.3 = (f32[176,256]{1,0:T(8,128)S(1)}, f32[176,256]{1,0:T(8,128)S(1)}, u32[]{:S(2)}, u32[]{:S(2)}) collective-permute-start(f32[176,256]{1,0:T(8,128)S(1)} %get-tuple-element.165), channel_id=1, source_target_pairs={{15,3},{31,19},{47,35},{63,51},{79,67},{95,83},{111,99},{127,115},... | collective-permute-start | bytes 540680 | tf_op jit(solution)/shard_map/ppermute | solution.py:376
  4.6 6.2 %collective-permute-start.4 = (f32[176,256]{1,0:T(8,128)S(1)}, f32[176,256]{1,0:T(8,128)S(1)}, u32[]{:S(2)}, u32[]{:S(2)}) collective-permute-start(f32[176,256]{1,0:T(8,128)S(1)} %get-tuple-element.168), channel_id=1, source_target_pairs={{15,14},{31,30},{47,46},{63,62},{79,78},{95,94},{111,110},{127,126... | collective-permute-start | bytes 540680 | tf_op jit(solution)/shard_map/ppermute | solution.py:376
  5.3 5.5 %collective-permute-start.5 = (f32[176,256]{1,0:T(8,128)S(1)}, f32[176,256]{1,0:T(8,128)}, u32[]{:S(2)}, u32[]{:S(2)}) collective-permute-start(f32[176,256]{1,0:T(8,128)S(1)} %get-tuple-element.164), channel_id=1, source_target_pairs={{15,11},{31,27},{47,43},{63,59},{79,75},{95,91},{111,107},{127,123... | collective-permute-start | bytes 540680 | tf_op jit(solution)/shard_map/ppermute | solution.py:376
  6.7 1.2 copy-start
  7.9 0.7 copy-start.1
  10.8 41.4 %collective-permute-start.6 = (f32[1032,256]{1,0:T(8,128)S(1)}, f32[1032,256]{1,0:T(8,128)S(1)}, u32[]{:S(2)}, u32[]{:S(2)}) collective-permute-start(f32[1032,256]{1,0:T(8,128)S(1)} %with_state.1), channel_id=1, source_target_pairs={{0,1},{1,2},{2,3},{3,4},{4,5},{5,6},{6,7},{7,8},{8,9},{9,10},{10,1... | collective-permute-start | bytes 3170312 | tf_op jit(solution)/shard_map/ppermute | solution.py:376
  17.6 31.5 %collective-permute-start.1 = (f32[384,256]{1,0:T(8,128)}, f32[384,256]{1,0:T(8,128)S(1)}, u32[]{:S(2)}, u32[]{:S(2)}) collective-permute-start(f32[384,256]{1,0:T(8,128)} %bitcast.63), channel_id=1, source_target_pairs={{0,32},{32,0},{1,33},{33,1},{2,34},{34,2},{3,35},{35,3},{4,36},{36... | collective-permute-start | bytes 1179656 | tf_op jit(solution)/shard_map/ppermute | solution.py:376
  22.3 29.8 %collective-permute-start.7 = (f32[176,256]{1,0:T(8,128)S(1)}, f32[176,256]{1,0:T(8,128)S(1)}, u32[]{:S(2)}, u32[]{:S(2)}) collective-permute-start(f32[176,256]{1,0:T(8,128)S(1)} %slice_select_fusion), channel_id=1, source_target_pairs={{15,16},{12,24},{3,23},{14,17},{11,20},{13,21},{31,0},{28,8},{19,7... | collective-permute-start | bytes 540680 | tf_op jit(solution)/shard_map/ppermute | solution.py:376
  31.9 17.2 %all-to-all-start.2 = ((s32[16,1,256]{2,1,0:T(1,128)}), s32[16,1,256]{2,1,0:T(1,128)S(1)}, u32[]{:S(2)}, u32[]{:S(2)}) async-start(s32[16,1,256]{2,1,0:T(1,128)} %broadcast_in_dim.44), calls=%async_computation.2 | async-start | bytes 32768 | tf_op jit(solution)/shard_map/all_to_all | solution.py:436
  52.2 77.6 %copy-start.25 = (f32[1,1,384]{2,1,0:T(1,128)S(1)}, f32[1,1,384]{2,1,0:T(1,128)}, u32[]{:S(2)}) copy-start(f32[1,1,384]{2,1,0:T(1,128)} %param.11) | copy-start | bytes 4612
  52.2 32.2 %all-to-all-start.3 = ((f32[8,56,256]{2,1,0:T(8,128)}), f32[8,56,256]{2,1,0:T(8,128)S(1)}, u32[]{:S(2)}, u32[]{:S(2)}) async-start(f32[8,56,256]{2,1,0:T(8,128)} %bitcast.25), calls=%async_computation.3 | async-start | bytes 917504 | tf_op jit(solution)/shard_map/all_to_all | solution.py:439
  60.8 3.4 %collective-permute-start.10 = (f32[176,256]{1,0:T(8,128)S(1)}, f32[176,256]{1,0:T(8,128)S(1)}, u32[]{:S(2)}, u32[]{:S(2)}) collective-permute-start(f32[176,256]{1,0:T(8,128)S(1)} %collective-permute-done.7.refs_0_), channel_id=1, source_target_pairs={{1,0},{17,16},{33,32},{49,48},{65,64},{81,80},{97,96},{113,112},{1... | collective-permute-start | bytes 540680 | tf_op jit(solution)/shard_map/ppermute | solution.py:376
  61.5 2.8 %collective-permute-start.11 = (f32[176,256]{1,0:T(8,128)S(1)}, f32[176,256]{1,0:T(8,128)S(1)}, u32[]{:S(2)}, u32[]{:S(2)}) collective-permute-start(f32[176,256]{1,0:T(8,128)S(1)} %collective-permute-done.7.refs_0_), channel_id=1, source_target_pairs={{4,0},{20,16},{36,32},{52,48},{68,64},{84,80},{100,96},{116,112},{... | collective-permute-start | bytes 540680 | tf_op jit(solution)/shard_map/ppermute | solution.py:376
  62.2 2.1 %collective-permute-start.12 = (f32[176,256]{1,0:T(8,128)S(1)}, f32[176,256]{1,0:T(8,128)S(1)}, u32[]{:S(2)}, u32[]{:S(2)}) collective-permute-start(f32[176,256]{1,0:T(8,128)S(1)} %collective-permute-done.7.refs_0_), channel_id=1, source_target_pairs={{5,0},{21,16},{37,32},{53,48},{69,64},{85,80},{101,96},{117,112},{... | collective-permute-start | bytes 540680 | tf_op jit(solution)/shard_map/ppermute | solution.py:376
  62.9 1.4 %collective-permute-start.8 = (f32[176,256]{1,0:T(8,128)S(1)}, f32[176,256]{1,0:T(8,128)S(1)}, u32[]{:S(2)}, u32[]{:S(2)}) collective-permute-start(f32[176,256]{1,0:T(8,128)S(1)} %collective-permute-done.7.refs_0_), channel_id=1, source_target_pairs={{8,0},{24,16},{40,32},{56,48},{72,64},{88,80},{104,96},{120,112},{... | collective-permute-start | bytes 540680 | tf_op jit(solution)/shard_map/ppermute | solution.py:376
  63.5 0.7 collective-permute-start.9
  64.2 33.5 %copy-start.7 = (s32[1,256]{1,0:T(1,128)}, s32[1,256]{1,0:T(1,128)S(1)}, u32[]{:S(2)}) copy-start(s32[1,256]{1,0:T(1,128)S(1)} %compare_select_fusion.1.ids_ref) | copy-start | bytes 3076
  90.1 39.7 %all-to-all-start.4 = ((f32[16,40,256]{2,1,0:T(8,128)}), f32[16,40,256]{2,1,0:T(8,128)S(1)}, u32[]{:S(2)}, u32[]{:S(2)}) async-start(f32[16,40,256]{2,1,0:T(8,128)} %bitcast.29), calls=%async_computation.4 | async-start | bytes 1310720 | tf_op jit(solution)/shard_map/all_to_all | solution.py:442

commit v7 on v6

--- a/solution.py
+++ b/solution.py
@@ -104,7 +104,7 @@
         out_shape=jax.ShapeDtypeStruct((chips * slots, rows.shape[1]), F32),
         in_specs=[SMEM, VMEM, VMEM, VMEM],
         out_specs=VMEM,
-        compiler_params=pltpu.CompilerParams(vmem_limit_bytes=8 << 20),
+        compiler_params=pltpu.CompilerParams(vmem_limit_bytes=4 << 20),
         name="pack_rows",
     )(place, ids, rows, other)
 
@@ -122,9 +122,25 @@
     return jnp.where((rank < slots) & (owner >= 0.0), owner * slots + rank, -1.0)
 
 
-def join_kernel(starts, crossed_ref, near_ref, *refs):
+def join_kernel(own, devices, slots, back_slots, starts, crossed_ref, near_ref, ids_ref, dest_ref, negative_ref, *refs):
     joined = refs[: len(starts)]
-    table_ref, state_ref, full_ref, done = refs[len(starts) :]
+    table_ref, state_ref, parts_ref, times_ref, place_ref, full_ref, done = refs[len(starts) :]
+    ids = ids_ref[...]
+    place_ref[0:1] = place_of(ids, 2 * own, devices // 2, slots)
+    place_ref[1:2] = place_of(ids, own, devices, back_slots)
+    place_ref[2:3] = dest_ref[...].astype(F32)
+    place_ref[3:] = jnp.zeros((place_ref.shape[0] - 3, ids.shape[1]), F32)
+
+    negative = negative_ref[...]
+    low = 128
+    high = table_ref.shape[0] // low
+    row = lax.broadcasted_iota(jnp.int32, (high, negative.shape[1]), 0)
+    hot_high = flag(row == lax.shift_right_logical(negative, 7)).astype(BF16)
+    row = lax.broadcasted_iota(jnp.int32, (low, negative.shape[1]), 0)
+    hot_low = flag(row == (negative & (low - 1))).astype(BF16)
+    grid = mxu(hot_high, hot_low, LANES)
+    times_ref[...] = jnp.concatenate([grid[i : i + 1] for i in range(high)], axis=1)
+
     height, width = table_ref.shape
     full_ref[...] = near_ref[...]
 
@@ -135,56 +151,46 @@
             copy.start()
             copy.wait()
 
-    table_ref[...] = full_ref[:height]
+    table = full_ref[:height]
+    table_ref[...] = table
+    for place, part in enumerate(parts_of(table, 3)):
+        parts_ref[place] = part
     rows = [full_ref[row : row + 1] for row in range(height, height + height // width)]
     state_ref[...] = jnp.concatenate(rows, axis=1)
 
 
-def join(crossed, near, joined, starts, height):
-    return pl.pallas_call(
-        functools.partial(join_kernel, tuple(starts)),
+def join(crossed, near, ids, dest, negative, joined, starts, height, devices, own):
+    edges = ids.shape[1]
+    return pl.pallas_call(
+        functools.partial(join_kernel, own, devices, SLOTS, BACK_SLOTS, tuple(starts)),
         out_shape=(
             jax.ShapeDtypeStruct((height, near.shape[1]), F32),
             jax.ShapeDtypeStruct((1, height), F32),
+            jax.ShapeDtypeStruct((3, height, near.shape[1]), BF16),
+            jax.ShapeDtypeStruct((1, height), F32),
+            jax.ShapeDtypeStruct((8, edges), F32),
         ),
-        in_specs=[SMEM, VMEM] + [pl.BlockSpec(memory_space=pl.ANY)] * len(joined),
-        out_specs=(VMEM, VMEM),
+        in_specs=[SMEM] + [VMEM] * 4 + [pl.BlockSpec(memory_space=pl.ANY)] * len(joined),
+        out_specs=(VMEM,) * 5,
         scratch_shapes=[pltpu.VMEM(near.shape, F32), pltpu.SemaphoreType.DMA],
         compiler_params=pltpu.CompilerParams(vmem_limit_bytes=8 << 20),
         name="join",
-    )(crossed, near, *joined)
+    )(crossed, near, ids, dest, negative, *joined)
 
 
 def edge_kernel(
-    own, slots, back_slots, count_ref, ids_ref, dest_ref, negative_ref, got_ref, table_ref,
-    loss_ref, back_ref, source_ref, weight_ref,
+    count_ref, got_ref, parts_ref, times_ref, place_ref, loss_ref, back_ref, source_ref, weight_ref
 ):
-    edges = ids_ref.shape[1]
-    height = table_ref.shape[0]
-    ids = ids_ref[...]
-    got_rows, back_rows = got_ref.shape[0], back_ref.shape[0]
-    place_column = to_column(place_of(ids, 2 * own, got_rows // slots, slots))
-    place = place_of(ids, own, back_rows // back_slots, back_slots)
-    across = lax.broadcasted_iota(jnp.int32, (edges, got_rows), 1).astype(F32)
-    source = pick(flag(across == place_column).astype(BF16), parts_of(got_ref[...], 3))
+    across = lax.broadcasted_iota(jnp.int32, (source_ref.shape[0], got_ref.shape[0]), 1).astype(F32)
+    got_hot = flag(across == to_column(place_ref[0:1])).astype(BF16)
+    source = pick(got_hot, parts_of(got_ref[...], 3))
     source_ref[...] = source
-
-    table = parts_of(table_ref[...], 3)
+    table = [parts_ref[part] for part in range(3)]
     scores = product(parts_of(source, 3), table, LANES)
-
-    negative = negative_ref[...]
-    low = 128
-    high = height // low
-    row = lax.broadcasted_iota(jnp.int32, (high, negative.shape[1]), 0)
-    hot_high = flag(row == lax.shift_right_logical(negative, 7)).astype(BF16)
-    row = lax.broadcasted_iota(jnp.int32, (low, negative.shape[1]), 0)
-    hot_low = flag(row == (negative & (low - 1))).astype(BF16)
-    grid = mxu(hot_high, hot_low, LANES)
-    times = jnp.concatenate([grid[i : i + 1] for i in range(high)], axis=1)
-
-    dest = to_column(dest_ref[...].astype(F32))
+    edges, height = scores.shape
+    times = times_ref[...]
     across = lax.broadcasted_iota(jnp.int32, (edges, height), 1).astype(F32)
-    hot = across == dest
+    hot = across == to_column(place_ref[2:3])
     positive = jnp.sum(jnp.where(hot, scores, 0.0), axis=1, keepdims=True)
     seen = times > 0.0
     top = jnp.max(jnp.where(seen, scores, -jnp.inf), axis=1, keepdims=True)
@@ -203,26 +209,27 @@
     weight_ref[...] = weight
 
     grad = product(parts_of(weight, 2), table)
-    down = lax.broadcasted_iota(jnp.int32, (back_rows, edges), 0).astype(F32)
-    back_ref[...] = pick(flag(down == place).astype(BF16), parts_of(grad, 3))
-
-
-def edge_step(count, ids, dest, negative, got, table, devices, own):
-    edges = ids.shape[1]
-    height, width = table.shape
-    return pl.pallas_call(
-        functools.partial(edge_kernel, own, SLOTS, BACK_SLOTS),
+    down = lax.broadcasted_iota(jnp.int32, (back_ref.shape[0], edges), 0).astype(F32)
+    back_hot = flag(down == place_ref[1:2]).astype(BF16)
+    back_ref[...] = pick(back_hot, parts_of(grad, 2))
+
+
+def edge_step(count, got, parts, times, place, devices):
+    edges = place.shape[1]
+    height, width = parts.shape[1:]
+    return pl.pallas_call(
+        edge_kernel,
         out_shape=(
             jax.ShapeDtypeStruct((1, edges), F32),
             jax.ShapeDtypeStruct((devices * BACK_SLOTS, width), F32),
             jax.ShapeDtypeStruct((edges, width), F32),
             jax.ShapeDtypeStruct((edges, height), F32),
         ),
-        in_specs=[SMEM] + [VMEM] * 5,
+        in_specs=[SMEM] + [VMEM] * 4,
         out_specs=(VMEM,) * 4,
-        compiler_params=pltpu.CompilerParams(vmem_limit_bytes=16 << 20),
+        compiler_params=pltpu.CompilerParams(vmem_limit_bytes=8 << 20),
         name="edge_step",
-    )(count, ids, dest, negative, got, table)
+    )(count, got, parts, times, place)
 
 
 def row_of(column):
@@ -256,7 +263,9 @@
     used_ref[...] = jnp.max(most, axis=0, keepdims=True)
     local = ids - first_ref[0]
     rank = rank_of(flag((local >= 0) & (local < own)))
-    local_ref[...] = slot_column(rank, local.astype(F32) + 1.0, back_slots)
+    row = row_of(slot_column(rank, local.astype(F32) + 1.0, back_slots))
+    down = lax.broadcasted_iota(jnp.int32, local_ref.shape, 0).astype(F32)
+    local_ref[...] = flag(down == row).astype(BF16)
     grad = product(parts_of(weight_ref[...], 2), parts_of(source_ref[...], 2), FIRST)
     new_ref[...], state_new_ref[...] = adagrad_rows(table_ref[...], state_ref[...], grad)
 
@@ -268,20 +277,17 @@
             jax.ShapeDtypeStruct(table.shape, F32),
             jax.ShapeDtypeStruct(state.shape, F32),
             jax.ShapeDtypeStruct((1, 1), F32),
-            jax.ShapeDtypeStruct((ids.shape[0] * BACK_SLOTS, 1), F32),
+            jax.ShapeDtypeStruct((own, ids.shape[0] * BACK_SLOTS), BF16),
         ),
         in_specs=[SMEM] + [VMEM] * 5,
         out_specs=(VMEM,) * 4,
-        compiler_params=pltpu.CompilerParams(vmem_limit_bytes=16 << 20),
+        compiler_params=pltpu.CompilerParams(vmem_limit_bytes=8 << 20),
         name="table_step",
     )(place, weight, source, table, state, ids)
 
 
 def source_kernel(local_ref, back_ref, rows_ref, state_ref, new_ref, state_new_ref):
-    own = rows_ref.shape[0]
-    across = lax.broadcasted_iota(jnp.int32, (local_ref.shape[0], own), 1).astype(F32)
-    hot = flag(across == local_ref[...]).astype(BF16)
-    grad = pick(hot, parts_of(back_ref[...], 3), FIRST)
+    grad = pick(local_ref[...], parts_of(back_ref[...], 2))
     new_ref[...], state_new_ref[...] = adagrad_rows(rows_ref[...], state_ref[...], grad)
 
 
@@ -294,7 +300,7 @@
         ),
         in_specs=[VMEM] * 4,
         out_specs=(VMEM, VMEM),
-        compiler_params=pltpu.CompilerParams(vmem_limit_bytes=8 << 20),
+        compiler_params=pltpu.CompilerParams(vmem_limit_bytes=4 << 20),
         name="source_step",
     )(local, back, rows, state)
 
@@ -314,7 +320,7 @@
         out_shape=(jax.ShapeDtypeStruct(rows.shape, F32), jax.ShapeDtypeStruct(table.shape, F32)),
         in_specs=[VMEM] * 2,
         out_specs=(VMEM, VMEM),
-        compiler_params=pltpu.CompilerParams(vmem_limit_bytes=8 << 20),
+        compiler_params=pltpu.CompilerParams(vmem_limit_bytes=4 << 20),
         name="held",
     )(rows, table)
 
@@ -329,7 +335,7 @@
         out_shape=(jax.ShapeDtypeStruct(emb.shape, F32), jax.ShapeDtypeStruct(state.shape, F32)),
         in_specs=[VMEM] * 3,
         out_specs=(VMEM, VMEM),
-        compiler_params=pltpu.CompilerParams(vmem_limit_bytes=8 << 20),
+        compiler_params=pltpu.CompilerParams(vmem_limit_bytes=6 << 20),
         name="update",
     )(emb, state, grad)
 
@@ -391,7 +397,7 @@
         out_shape=jax.ShapeDtypeStruct((height + -(-height // (8 * width)) * 8, width), F32),
         in_specs=[VMEM] * 2,
         out_specs=VMEM,
-        compiler_params=pltpu.CompilerParams(vmem_limit_bytes=8 << 20),
+        compiler_params=pltpu.CompilerParams(vmem_limit_bytes=4 << 20),
         name="with_state",
     )(table, state)
 
@@ -418,7 +424,7 @@
         [(z * plane + leave[k], (1 - z) * plane + land[k]) for z in range(2) for k in range(count)],
     )
     joined = [come] + [permute(come, ("x", "y"), [(land[k], land[0])]) for k in range(1, count)]
-    return near, joined, starts, (at == land[0]).astype(jnp.int32), spread[-1]
+    return near, joined, starts, (at == land[0]).astype(jnp.int32), spread[0]
 
 
 def on_device(src_emb, src_state, dst_emb, dst_state, src_ids, dst_ids, neg_ids, counts):
@@ -437,8 +443,10 @@
 
     send = pack_rows(place, all_ids, rows, other, SLOTS)
     got = lax.all_to_all(after(send, near, joined[0]), "zl", 0, 0, tiled=True)
-    table, table_state = join(crossed.reshape(1), near, joined, starts, dst_emb.shape[2])
-    loss, back, source, weight = edge_step(counts, ids, dst_ids[0], neg_ids[0], got, table, devices, own)
+    table, table_state, *prepared = join(
+        crossed.reshape(1), near, ids, dst_ids[0], neg_ids[0], joined, starts, dst_emb.shape[2], devices, own
+    )
+    loss, back, source, weight = edge_step(counts, got, *prepared, devices)
     back = lax.all_to_all(back, SRC, 0, 0, tiled=True)
     dst_new, dst_state_new, over, local = table_step(place, weight, source, table, table_state, all_ids, own)
     src_new, src_state_new = source_step(local, back, rows, rows_state)

time: 135 us -> 134 us (level)
  the two profiles are of different devices: /device:TPU:47 before, /device:TPU:37 now
where the time goes in v7:
time: 134 us; the launch traced here: 133 us
  waiting for transfers between devices  65.8 us (49%)
  starting transfers between devices  43.2 us (32%)
  Pallas kernels  15.4 us (11%)
  local copies, waits for them, and re-layouts  4.77 us (4%)
  between operations  1.76 us (1%)
    all_to_all x1, waiting for transfers between devices, on_device(): back = lax.all_to_all(back, SRC, 0, 0, tiled=True)  28.3 us
    ppermute x13, starting transfers between devices, permute(): return lax.ppermute(value, axes, pairs)  16 us
    all_to_all x1, waiting for transfers between devices, on_device(): got = lax.all_to_all(after(send, near, joined[0]), 'zl', 0, 0, tiled=True)  14.9 us
    ppermute x13, waiting for transfers between devices, permute(): return lax.ppermute(value, axes, pairs)  13.8 us
    all_to_all x1, starting transfers between devices, on_device(): lax.all_to_all(jnp.broadcast_to(ids, (devices, ids.shape[1])), SRC, 0, 0,...  12.4 us
    all_to_all x1, waiting for transfers between devices, on_device(): lax.all_to_all(jnp.broadcast_to(ids, (devices, ids.shape[1])), SRC, 0, 0,...  8.81 us
    all_to_all x1, starting transfers between devices, on_device(): back = lax.all_to_all(back, SRC, 0, 0, tiled=True)  7.69 us
    all_to_all x1, starting transfers between devices, on_device(): got = lax.all_to_all(after(send, near, joined[0]), 'zl', 0, 0, tiled=True)  7.09 us
  transfers between devices with their start and end apart: 16, of which 5 were waited for; matrix products, arithmetic and copies ran while one was open for 1% of the time, Pallas kernels for 6%

profile of v7, /device:TPU:37, one launch (start us, length us, event | category | flops | bytes accessed | tf_op | source)
XLA Modules:
  0.0 133.2 jit_solution(3318899415805434130)
XLA Ops:
  0.6 0.0 copy-start.6
  0.6 0.0 copy-start.30
  0.7 0.0 copy-start.24
  0.7 1.4 %slice_bitcast_fusion = (f32[176,256]{1,0:T(8,128)S(1)}, f32[176,256]{1,0:T(8,128)S(1)}, f32[176,256]{1,0:T(8,128)S(1)}, f32[176,256]{1,0:T(8,128)S(1)}, f32[176,256]{1,0:T(8,128)S(1)}) fusion(f32[1,1,1024,256]{3,2,1,0:T(8,128)} %param.12), kind=kLoop, calls=%fused_computation.37 | loop fusion | bytes 1802240 | tf_op jit(solution)/shard_map/slice | solution.py:416
  2.0 0.7 collective-permute-start
  2.7 0.7 collective-permute-start.2
  3.4 0.7 collective-permute-start.3
  4.1 0.7 collective-permute-start.4
  4.7 1.3 %collective-permute-start.5 = (f32[176,256]{1,0:T(8,128)S(1)}, f32[176,256]{1,0:T(8,128)}, u32[]{:S(2)}, u32[]{:S(2)}) collective-permute-start(f32[176,256]{1,0:T(8,128)S(1)} %get-tuple-element.170), channel_id=1, source_target_pairs={{15,13},{31,29},{47,45},{63,61},{79,77},{95,93},{111,109},{127,125... | collective-permute-start | bytes 540680 | tf_op jit(solution)/shard_map/ppermute | solution.py:382
  6.1 0.0 copy-start
  6.1 1.2 copy-done
  7.3 0.0 copy-start.2
  7.3 0.7 copy-done.2
  8.0 0.1 with_state.1
  8.1 0.0 collective-permute-done
  8.1 0.0 collective-permute-done.2
  8.1 0.0 collective-permute-done.3
  8.1 0.0 copy-start.20
  8.1 0.0 collective-permute-done.4
  8.1 0.0 copy-start.21
  8.1 0.0 collective-permute-done.5
  8.2 3.2 %collective-permute-start.6 = (f32[1032,256]{1,0:T(8,128)S(1)}, f32[1032,256]{1,0:T(8,128)S(1)}, u32[]{:S(2)}, u32[]{:S(2)}) collective-permute-start(f32[1032,256]{1,0:T(8,128)S(1)} %with_state.1), channel_id=1, source_target_pairs={{0,1},{1,2},{2,3},{3,4},{4,5},{5,6},{6,7},{7,8},{8,9},{9,10},{10,1... | collective-permute-start | bytes 3170312 | tf_op jit(solution)/shard_map/ppermute | solution.py:382
  12.0 0.0 copy-done.20
  12.0 0.0 copy-done.21
  12.0 2.9 %collective-permute-start.1 = (f32[384,256]{1,0:T(8,128)}, f32[384,256]{1,0:T(8,128)S(1)}, u32[]{:S(2)}, u32[]{:S(2)}) collective-permute-start(f32[384,256]{1,0:T(8,128)} %bitcast.64), channel_id=1, source_target_pairs={{0,32},{32,0},{1,33},{33,1},{2,34},{34,2},{3,35},{35,3},{4,36},{36... | collective-permute-start | bytes 1179656 | tf_op jit(solution)/shard_map/ppermute | solution.py:382
  14.9 1.2 slice_select_fusion
  16.1 1.3 collective-permute-start.7
  17.4 0.0 copy-done.30
  17.4 0.6 broadcast_in_dim.43
  18.1 12.4 %all-to-all-start.2 = ((s32[16,1,256]{2,1,0:T(1,128)}), s32[16,1,256]{2,1,0:T(1,128)S(1)}, u32[]{:S(2)}, u32[]{:S(2)}) async-start(s32[16,1,256]{2,1,0:T(1,128)} %broadcast_in_dim.43), calls=%async_computation.2 | async-start | bytes 32768 | tf_op jit(solution)/shard_map/all_to_all | solution.py:442
  30.5 0.1 pad_add_fusion.place_ref.first_ref
  30.5 8.8 %all-to-all-done.2 = s32[16,1,256]{2,1,0:T(1,128)S(1)} async-done(((s32[16,1,256]{2,1,0:T(1,128)}), s32[16,1,256]{2,1,0:T(1,128)S(1)}, u32[]{:S(2)}, u32[]{:S(2)}) %all-to-all-start.2) | async-done | bytes 16416 | tf_op jit(solution)/shard_map/all_to_all | solution.py:442
  39.4 0.0 collective-permute-done.1.other_ref
  39.4 0.0 copy-done.6
  39.4 2.6 %pack_rows.1 = f32[448,256]{1,0:T(8,128)} custom-call(s32[3]{0:T(128)S(1)} %pad_add_fusion.place_ref.first_ref, s32[16,256]{1,0:T(8,128)S(1)} %bitcast.68, f32[384,256]{1,0:T(8,128)S(1)} %bitcast.67, f32[384,256]{1,0:T(8,128)S(1)} %collective-permute-done.1.other_ref), custom_call_target="tpu_custom_call" | custom-call | tf_op jit(solution)/shard_map/pack_rows/pallas_call | solution.py:102
  42.0 12.1 %collective-permute-done.7.refs_0_ = f32[176,256]{1,0:T(8,128)S(1)} collective-permute-done((f32[176,256]{1,0:T(8,128)S(1)}, f32[176,256]{1,0:T(8,128)S(1)}, u32[]{:S(2)}, u32[]{:S(2)}) %collective-permute-start.7) | collective-permute-done | bytes 180256 | tf_op jit(solution)/shard_map/ppermute | solution.py:382
  54.1 0.0 collective-permute-done.6.near_ref
  54.1 0.0 copy-start.28
  54.1 7.1 %all-to-all-start.3 = ((f32[8,56,256]{2,1,0:T(8,128)}), f32[8,56,256]{2,1,0:T(8,128)S(1)}, u32[]{:S(2)}, u32[]{:S(2)}) async-start(f32[8,56,256]{2,1,0:T(8,128)} %bitcast.22), calls=%async_computation.3 | async-start | bytes 917504 | tf_op jit(solution)/shard_map/all_to_all | solution.py:445
  61.2 0.7 collective-permute-start.10
  61.8 0.7 collective-permute-start.11
  62.5 0.7 collective-permute-start.12
  63.2 1.9 %collective-permute-start.8 = (f32[176,256]{1,0:T(8,128)S(1)}, f32[176,256]{1,0:T(8,128)S(1)}, u32[]{:S(2)}, u32[]{:S(2)}) collective-permute-start(f32[176,256]{1,0:T(8,128)S(1)} %collective-permute-done.7.refs_0_), channel_id=1, source_target_pairs={{8,0},{24,16},{40,32},{56,48},{72,64},{88,80},{104,96},{120,112},{... | collective-permute-start | bytes 540680 | tf_op jit(solution)/shard_map/ppermute | solution.py:382
  65.1 0.7 collective-permute-start.9
  65.8 0.0 copy-start.7
  65.8 0.0 collective-permute-done.10.refs_3_
  65.8 0.0 collective-permute-done.11.refs_4_
  65.9 0.0 collective-permute-done.12.refs_5_
  65.9 1.7 %collective-permute-done.8.refs_1_ = f32[176,256]{1,0:T(8,128)S(1)} collective-permute-done((f32[176,256]{1,0:T(8,128)S(1)}, f32[176,256]{1,0:T(8,128)S(1)}, u32[]{:S(2)}, u32[]{:S(2)}) %collective-permute-start.8) | collective-permute-done | bytes 180256 | tf_op jit(solution)/shard_map/ppermute | solution.py:382
  67.5 0.0 collective-permute-done.9.refs_2_
  67.5 0.0 copy-done.24
  67.5 2.1 %join.1 = (f32[1024,256]{1,0:T(8,128)}, f32[1,1024]{1,0:T(1,128)S(1)}, bf16[3,1024,256]{2,1,0:T(8,128)(2,1)S(1)}, f32[1,1024]{1,0:T(1,128)S(1)}, f32[8,256]{1,0:T(8,128)S(1)}) custom-call(s32[1]{0:T(128)} %bitcast.24.crossed_ref, f32[1032,256]{1,0:T(8,128)S(1)} %collective-permute-done.6.near_ref, s32[1,256]{1,0:T(1,128)S(1)} %compare_select_fusion.1.ids_ref, ...), custom_call_target="tpu_custom_call" | custom-call | tf_op jit(solution)/shard_map/join/pallas_call | solution.py:164
  69.6 14.9 %all-to-all-done.3 = f32[8,56,256]{2,1,0:T(8,128)S(1)} async-done(((f32[8,56,256]{2,1,0:T(8,128)}), f32[8,56,256]{2,1,0:T(8,128)S(1)}, u32[]{:S(2)}, u32[]{:S(2)}) %all-to-all-start.3) | async-done | bytes 458784 | tf_op jit(solution)/shard_map/all_to_all | solution.py:445
  84.5 0.0 copy-done.7
  84.5 4.4 %edge_step.1 = (f32[1,256]{1,0:T(1,128)}, f32[640,256]{1,0:T(8,128)S(1)}, f32[256,256]{1,0:T(8,128)S(1)}, f32[256,1024]{1,0:T(8,128)S(1)}) custom-call(s32[1,1]{1,0:T(1,128)} %copy.41.count_ref, f32[448,256]{1,0:T(8,128)S(1)} %bitcast.61, bf16[3,1024,256]{2,1,0:T(8,128)(2,1)S(1)} %get-tuple-element.112.parts_ref, ...), custom_call_target="tpu_custom_call" | custom-call | tf_op jit(solution)/shard_map/edge_step/pallas_call | solution.py:220
  88.9 0.0 copy-start.8
  88.9 0.9 copy-done.1
  89.8 7.7 %all-to-all-start.4 = ((f32[16,40,256]{2,1,0:T(8,128)}), f32[16,40,256]{2,1,0:T(8,128)S(1)}, u32[]{:S(2)}, u32[]{:S(2)}) async-start(f32[16,40,256]{2,1,0:T(8,128)} %bitcast.62), calls=%async_computation.4 | async-start | bytes 1310720 | tf_op jit(solution)/shard_map/all_to_all | solution.py:450
  97.5 3.8 %table_step.1 = (f32[1024,256]{1,0:T(8,128)}, f32[1,1024]{1,0:T(1,128)}, f32[1,1]{1,0:T(1,128)}, bf16[384,640]{1,0:T(8,128)(2,1)S(1)}) custom-call(s32[3]{0:T(128)S(1)} %pad_add_fusion.place_ref.first_ref, f32[256,1024]{1,0:T(8,128)S(1)} %get-tuple-element.115.weight_ref, f32[256,256]{1,0:T(8,128)S(1)} %get-tuple-element.116.source_ref, ...), custom_call_target="tpu_custom_call" | custom-call | tf_op jit(solution)/shard_map/table_step/pallas_call | solution.py:274
  101.3 28.3 %all-to-all-done.4 = f32[16,40,256]{2,1,0:T(8,128)S(1)} async-done(((f32[16,40,256]{2,1,0:T(8,128)}), f32[16,40,256]{2,1,0:T(8,128)S(1)}, u32[]{:S(2)}, u32[]{:S(2)}) %all-to-all-start.4) | async-done | bytes 655392 | tf_op jit(solution)/shard_map/all_to_all | solution.py:450
  129.6 0.0 copy-done.28
  129.6 2.5 %source_step.1 = (f32[384,256]{1,0:T(8,128)}, f32[1,384]{1,0:T(1,128)}) custom-call(bf16[384,640]{1,0:T(8,128)(2,1)S(1)} %get-tuple-element.120.local_ref, f32[640,256]{1,0:T(8,128)S(1)} %bitcast.60, f32[384,256]{1,0:T(8,128)} %bitcast.65, f32[1,384]{1,0:T(1,128)S(1)} %bitcast.80), custom_call_target="tpu_custom_call" | custom-call | tf_op jit(solution)/shard_map/source_step/pallas_call | solution.py:295
  132.1 0.0 copy-done.8
  132.1 0.9 while.17
  (4 shorter events, 0.0 us)
Async XLA Ops:
  0.6 38.7 %copy-start.6 = (f32[1,1,384,256]{3,2,1,0:T(8,128)S(1)}, f32[1,1,384,256]{3,2,1,0:T(8,128)}, u32[]{:S(2)}) copy-start(f32[1,1,384,256]{3,2,1,0:T(8,128)} %param.10) | copy-start | bytes 1179652
  0.6 16.8 %copy-start.30 = (s32[1,1,256]{2,1,0:T(1,128)S(1)}, s32[1,1,256]{2,1,0:T(1,128)}, u32[]{:S(2)}) copy-start(s32[1,1,256]{2,1,0:T(1,128)} %param.14) | copy-start | bytes 3076
  0.7 66.9 %copy-start.24 = (s32[1,1,256]{2,1,0:T(1,128)S(1)}, s32[1,1,256]{2,1,0:T(1,128)}, u32[]{:S(2)}) copy-start(s32[1,1,256]{2,1,0:T(1,128)} %param.15) | copy-start | bytes 3076
  2.0 6.1 %collective-permute-start = (f32[176,256]{1,0:T(8,128)S(1)}, f32[176,256]{1,0:T(8,128)S(1)}, u32[]{:S(2)}, u32[]{:S(2)}) collective-permute-start(f32[176,256]{1,0:T(8,128)S(1)} %get-tuple-element.173), channel_id=1, source_target_pairs={{15,12},{31,28},{47,44},{63,60},{79,76},{95,92},{111,108},{127,124... | collective-permute-start | bytes 540680 | tf_op jit(solution)/shard_map/ppermute | solution.py:382
  2.7 5.4 %collective-permute-start.2 = (f32[176,256]{1,0:T(8,128)S(1)}, f32[176,256]{1,0:T(8,128)S(1)}, u32[]{:S(2)}, u32[]{:S(2)}) collective-permute-start(f32[176,256]{1,0:T(8,128)S(1)} %get-tuple-element.172), channel_id=1, source_target_pairs={{15,3},{31,19},{47,35},{63,51},{79,67},{95,83},{111,99},{127,115},... | collective-permute-start | bytes 540680 | tf_op jit(solution)/shard_map/ppermute | solution.py:382
  3.4 4.7 %collective-permute-start.3 = (f32[176,256]{1,0:T(8,128)S(1)}, f32[176,256]{1,0:T(8,128)S(1)}, u32[]{:S(2)}, u32[]{:S(2)}) collective-permute-start(f32[176,256]{1,0:T(8,128)S(1)} %get-tuple-element.171), channel_id=1, source_target_pairs={{15,14},{31,30},{47,46},{63,62},{79,78},{95,94},{111,110},{127,126... | collective-permute-start | bytes 540680 | tf_op jit(solution)/shard_map/ppermute | solution.py:382
  4.1 4.1 %collective-permute-start.4 = (f32[176,256]{1,0:T(8,128)S(1)}, f32[176,256]{1,0:T(8,128)S(1)}, u32[]{:S(2)}, u32[]{:S(2)}) collective-permute-start(f32[176,256]{1,0:T(8,128)S(1)} %get-tuple-element.174), channel_id=1, source_target_pairs={{15,11},{31,27},{47,43},{63,59},{79,75},{95,91},{111,107},{127,123... | collective-permute-start | bytes 540680 | tf_op jit(solution)/shard_map/ppermute | solution.py:382
  4.7 3.4 %collective-permute-start.5 = (f32[176,256]{1,0:T(8,128)S(1)}, f32[176,256]{1,0:T(8,128)}, u32[]{:S(2)}, u32[]{:S(2)}) collective-permute-start(f32[176,256]{1,0:T(8,128)S(1)} %get-tuple-element.170), channel_id=1, source_target_pairs={{15,13},{31,29},{47,45},{63,61},{79,77},{95,93},{111,109},{127,125... | collective-permute-start | bytes 540680 | tf_op jit(solution)/shard_map/ppermute | solution.py:382
  6.1 1.2 copy-start
  7.3 0.7 copy-start.2
  8.1 3.9 %copy-start.20 = (f32[176,256]{1,0:T(8,128)}, f32[176,256]{1,0:T(8,128)S(1)}, u32[]{:S(2)}) copy-start(f32[176,256]{1,0:T(8,128)S(1)} %collective-permute-done.3) | copy-start | bytes 540676
  8.1 3.9 %copy-start.21 = (f32[176,256]{1,0:T(8,128)}, f32[176,256]{1,0:T(8,128)S(1)}, u32[]{:S(2)}) copy-start(f32[176,256]{1,0:T(8,128)S(1)} %collective-permute-done.4) | copy-start | bytes 540676
  8.2 45.9 %collective-permute-start.6 = (f32[1032,256]{1,0:T(8,128)S(1)}, f32[1032,256]{1,0:T(8,128)S(1)}, u32[]{:S(2)}, u32[]{:S(2)}) collective-permute-start(f32[1032,256]{1,0:T(8,128)S(1)} %with_state.1), channel_id=1, source_target_pairs={{0,1},{1,2},{2,3},{3,4},{4,5},{5,6},{6,7},{7,8},{8,9},{9,10},{10,1... | collective-permute-start | bytes 3170312 | tf_op jit(solution)/shard_map/ppermute | solution.py:382
  12.0 27.3 %collective-permute-start.1 = (f32[384,256]{1,0:T(8,128)}, f32[384,256]{1,0:T(8,128)S(1)}, u32[]{:S(2)}, u32[]{:S(2)}) collective-permute-start(f32[384,256]{1,0:T(8,128)} %bitcast.64), channel_id=1, source_target_pairs={{0,32},{32,0},{1,33},{33,1},{2,34},{34,2},{3,35},{35,3},{4,36},{36... | collective-permute-start | bytes 1179656 | tf_op jit(solution)/shard_map/ppermute | solution.py:382
  16.1 37.9 %collective-permute-start.7 = (f32[176,256]{1,0:T(8,128)S(1)}, f32[176,256]{1,0:T(8,128)S(1)}, u32[]{:S(2)}, u32[]{:S(2)}) collective-permute-start(f32[176,256]{1,0:T(8,128)S(1)} %slice_select_fusion), channel_id=1, source_target_pairs={{15,16},{12,24},{3,23},{14,17},{11,20},{13,21},{31,0},{28,8},{19,7... | collective-permute-start | bytes 540680 | tf_op jit(solution)/shard_map/ppermute | solution.py:382
  18.1 21.3 %all-to-all-start.2 = ((s32[16,1,256]{2,1,0:T(1,128)}), s32[16,1,256]{2,1,0:T(1,128)S(1)}, u32[]{:S(2)}, u32[]{:S(2)}) async-start(s32[16,1,256]{2,1,0:T(1,128)} %broadcast_in_dim.43), calls=%async_computation.2 | async-start | bytes 32768 | tf_op jit(solution)/shard_map/all_to_all | solution.py:442
  54.1 75.5 %copy-start.28 = (f32[1,1,384]{2,1,0:T(1,128)S(1)}, f32[1,1,384]{2,1,0:T(1,128)}, u32[]{:S(2)}) copy-start(f32[1,1,384]{2,1,0:T(1,128)} %param.11) | copy-start | bytes 4612
  54.1 30.5 %all-to-all-start.3 = ((f32[8,56,256]{2,1,0:T(8,128)}), f32[8,56,256]{2,1,0:T(8,128)S(1)}, u32[]{:S(2)}, u32[]{:S(2)}) async-start(f32[8,56,256]{2,1,0:T(8,128)} %bitcast.22), calls=%async_computation.3 | async-start | bytes 917504 | tf_op jit(solution)/shard_map/all_to_all | solution.py:445
  61.2 4.7 %collective-permute-start.10 = (f32[176,256]{1,0:T(8,128)S(1)}, f32[176,256]{1,0:T(8,128)S(1)}, u32[]{:S(2)}, u32[]{:S(2)}) collective-permute-start(f32[176,256]{1,0:T(8,128)S(1)} %collective-permute-done.7.refs_0_), channel_id=1, source_target_pairs={{1,0},{17,16},{33,32},{49,48},{65,64},{81,80},{97,96},{113,112},{1... | collective-permute-start | bytes 540680 | tf_op jit(solution)/shard_map/ppermute | solution.py:382
  61.8 4.0 %collective-permute-start.11 = (f32[176,256]{1,0:T(8,128)S(1)}, f32[176,256]{1,0:T(8,128)S(1)}, u32[]{:S(2)}, u32[]{:S(2)}) collective-permute-start(f32[176,256]{1,0:T(8,128)S(1)} %collective-permute-done.7.refs_0_), channel_id=1, source_target_pairs={{4,0},{20,16},{36,32},{52,48},{68,64},{84,80},{100,96},{116,112},{... | collective-permute-start | bytes 540680 | tf_op jit(solution)/shard_map/ppermute | solution.py:382
  62.5 3.4 %collective-permute-start.12 = (f32[176,256]{1,0:T(8,128)S(1)}, f32[176,256]{1,0:T(8,128)S(1)}, u32[]{:S(2)}, u32[]{:S(2)}) collective-permute-start(f32[176,256]{1,0:T(8,128)S(1)} %collective-permute-done.7.refs_0_), channel_id=1, source_target_pairs={{5,0},{21,16},{37,32},{53,48},{69,64},{85,80},{101,96},{117,112},{... | collective-permute-start | bytes 540680 | tf_op jit(solution)/shard_map/ppermute | solution.py:382
  63.2 4.4 %collective-permute-start.8 = (f32[176,256]{1,0:T(8,128)S(1)}, f32[176,256]{1,0:T(8,128)S(1)}, u32[]{:S(2)}, u32[]{:S(2)}) collective-permute-start(f32[176,256]{1,0:T(8,128)S(1)} %collective-permute-done.7.refs_0_), channel_id=1, source_target_pairs={{8,0},{24,16},{40,32},{56,48},{72,64},{88,80},{104,96},{120,112},{... | collective-permute-start | bytes 540680 | tf_op jit(solution)/shard_map/ppermute | solution.py:382
  65.1 2.4 %collective-permute-start.9 = (f32[176,256]{1,0:T(8,128)S(1)}, f32[176,256]{1,0:T(8,128)S(1)}, u32[]{:S(2)}, u32[]{:S(2)}) collective-permute-start(f32[176,256]{1,0:T(8,128)S(1)} %collective-permute-done.7.refs_0_), channel_id=1, source_target_pairs={{7,0},{23,16},{39,32},{55,48},{71,64},{87,80},{103,96},{119,112},{... | collective-permute-start | bytes 540680 | tf_op jit(solution)/shard_map/ppermute | solution.py:382
  65.8 18.7 %copy-start.7 = (s32[1,256]{1,0:T(1,128)}, s32[1,256]{1,0:T(1,128)S(1)}, u32[]{:S(2)}) copy-start(s32[1,256]{1,0:T(1,128)S(1)} %compare_select_fusion.1.ids_ref) | copy-start | bytes 3076
  88.9 0.9 copy-start.1
  88.9 43.1 %copy-start.8 = (s32[1,256]{1,0:T(1,128)S(1)}, s32[1,256]{1,0:T(1,128)}, u32[]{:S(2)}) copy-start(s32[1,256]{1,0:T(1,128)} %copy-done.7) | copy-start | bytes 3076
  89.8 39.8 %all-to-all-start.4 = ((f32[16,40,256]{2,1,0:T(8,128)}), f32[16,40,256]{2,1,0:T(8,128)S(1)}, u32[]{:S(2)}, u32[]{:S(2)}) async-start(f32[16,40,256]{2,1,0:T(8,128)} %bitcast.62), calls=%async_computation.4 | async-start | bytes 1310720 | tf_op jit(solution)/shard_map/all_to_all | solution.py:450

commit v8 on v7

--- a/solution.py
+++ b/solution.py
@@ -247,9 +247,10 @@
 
 
 def table_kernel(
-    own, slots, back_slots, first_ref, weight_ref, source_ref, table_ref, state_ref, ids_ref,
-    new_ref, state_new_ref, used_ref, local_ref,
+    own, slots, back_slots, first_ref, weight_ref, source_ref, table_ref, state_ref, ids_ref, rows_ref,
+    new_ref, state_new_ref, used_ref, local_ref, held_ref,
 ):
+    held_ref[...] = rows_ref[...]
     ids = ids_ref[...]
     devices = ids.shape[0]
     most = jnp.zeros((devices, 1), F32)
@@ -270,7 +271,8 @@
     new_ref[...], state_new_ref[...] = adagrad_rows(table_ref[...], state_ref[...], grad)
 
 
-def table_step(place, weight, source, table, state, ids, own):
+def table_step(place, weight, source, table, state, ids, rows):
+    own = rows.shape[0]
     return pl.pallas_call(
         functools.partial(table_kernel, own, SLOTS, BACK_SLOTS),
         out_shape=(
@@ -278,12 +280,13 @@
             jax.ShapeDtypeStruct(state.shape, F32),
             jax.ShapeDtypeStruct((1, 1), F32),
             jax.ShapeDtypeStruct((own, ids.shape[0] * BACK_SLOTS), BF16),
+            jax.ShapeDtypeStruct(rows.shape, F32),
         ),
-        in_specs=[SMEM] + [VMEM] * 5,
-        out_specs=(VMEM,) * 4,
+        in_specs=[SMEM] + [VMEM] * 6,
+        out_specs=(VMEM,) * 5,
         compiler_params=pltpu.CompilerParams(vmem_limit_bytes=8 << 20),
         name="table_step",
-    )(place, weight, source, table, state, ids)
+    )(place, weight, source, table, state, ids, rows)
 
 
 def source_kernel(local_ref, back_ref, rows_ref, state_ref, new_ref, state_new_ref):
@@ -448,8 +451,8 @@
     )
     loss, back, source, weight = edge_step(counts, got, *prepared, devices)
     back = lax.all_to_all(back, SRC, 0, 0, tiled=True)
-    dst_new, dst_state_new, over, local = table_step(place, weight, source, table, table_state, all_ids, own)
-    src_new, src_state_new = source_step(local, back, rows, rows_state)
+    dst_new, dst_state_new, over, local, kept = table_step(place, weight, source, table, table_state, all_ids, rows)
+    src_new, src_state_new = source_step(local, back, kept, rows_state)
 
     def again(carry):
         found = whole_step(

time: 134 us -> 133 us (level)
  transfers between devices with their start and end apart: 16 -> 16, of which waited for: 5 -> 5; matrix products, arithmetic and copies ran while one was open for 1% -> 1% of each run, Pallas kernels for 6% -> 7%
where the time goes in v8:
time: 133 us; the launch traced here: 132 us
  waiting for transfers between devices  65.7 us (49%)
  starting transfers between devices  43.1 us (32%)
  Pallas kernels  14.5 us (11%)
  local copies, waits for them, and re-layouts  4.77 us (4%)
  between operations  1.76 us (1%)
    all_to_all x1, waiting for transfers between devices, on_device(): back = lax.all_to_all(back, SRC, 0, 0, tiled=True)  28.2 us
    ppermute x13, starting transfers between devices, permute(): return lax.ppermute(value, axes, pairs)  16 us
    all_to_all x1, waiting for transfers between devices, on_device(): got = lax.all_to_all(after(send, near, joined[0]), 'zl', 0, 0, tiled=True)  14.9 us
    ppermute x13, waiting for transfers between devices, permute(): return lax.ppermute(value, axes, pairs)  13.8 us
    all_to_all x1, starting transfers between devices, on_device(): lax.all_to_all(jnp.broadcast_to(ids, (devices, ids.shape[1])), SRC, 0, 0,...  12.4 us
    all_to_all x1, waiting for transfers between devices, on_device(): lax.all_to_all(jnp.broadcast_to(ids, (devices, ids.shape[1])), SRC, 0, 0,...  8.81 us
    all_to_all x1, starting transfers between devices, on_device(): back = lax.all_to_all(back, SRC, 0, 0, tiled=True)  7.69 us
    all_to_all x1, starting transfers between devices, on_device(): got = lax.all_to_all(after(send, near, joined[0]), 'zl', 0, 0, tiled=True)  6.96 us
  transfers between devices with their start and end apart: 16, of which 5 were waited for; matrix products, arithmetic and copies ran while one was open for 1% of the time, Pallas kernels for 7%

profile of v8, /device:TPU:37, one launch (start us, length us, event | category | flops | bytes accessed | tf_op | source)
XLA Modules:
  0.0 132.0 jit_solution(18412316160878473162)
XLA Ops:
  0.6 0.0 copy-start.6
  0.6 0.0 copy-start.30
  0.7 0.0 copy-start.24
  0.7 1.4 %slice_bitcast_fusion = (f32[176,256]{1,0:T(8,128)S(1)}, f32[176,256]{1,0:T(8,128)S(1)}, f32[176,256]{1,0:T(8,128)S(1)}, f32[176,256]{1,0:T(8,128)S(1)}, f32[176,256]{1,0:T(8,128)S(1)}) fusion(f32[1,1,1024,256]{3,2,1,0:T(8,128)} %param.12), kind=kLoop, calls=%fused_computation.37 | loop fusion | bytes 1802240 | tf_op jit(solution)/shard_map/slice | solution.py:419
  2.0 0.7 collective-permute-start
  2.7 0.7 collective-permute-start.2
  3.4 0.7 collective-permute-start.3
  4.1 0.7 collective-permute-start.4
  4.7 1.3 %collective-permute-start.5 = (f32[176,256]{1,0:T(8,128)S(1)}, f32[176,256]{1,0:T(8,128)}, u32[]{:S(2)}, u32[]{:S(2)}) collective-permute-start(f32[176,256]{1,0:T(8,128)S(1)} %get-tuple-element.172), channel_id=1, source_target_pairs={{15,13},{31,29},{47,45},{63,61},{79,77},{95,93},{111,109},{127,125... | collective-permute-start | bytes 540680 | tf_op jit(solution)/shard_map/ppermute | solution.py:385
  6.1 0.0 copy-start
  6.1 1.2 copy-done
  7.3 0.0 copy-start.2
  7.3 0.7 copy-done.2
  8.0 0.1 with_state.1
  8.1 0.0 collective-permute-done
  8.1 0.0 collective-permute-done.2
  8.1 0.0 collective-permute-done.3
  8.1 0.0 copy-start.20
  8.1 0.0 collective-permute-done.4
  8.1 0.0 copy-start.21
  8.1 0.0 collective-permute-done.5
  8.2 3.2 %collective-permute-start.6 = (f32[1032,256]{1,0:T(8,128)S(1)}, f32[1032,256]{1,0:T(8,128)S(1)}, u32[]{:S(2)}, u32[]{:S(2)}) collective-permute-start(f32[1032,256]{1,0:T(8,128)S(1)} %with_state.1), channel_id=1, source_target_pairs={{0,1},{1,2},{2,3},{3,4},{4,5},{5,6},{6,7},{7,8},{8,9},{9,10},{10,1... | collective-permute-start | bytes 3170312 | tf_op jit(solution)/shard_map/ppermute | solution.py:385
  12.0 0.0 copy-done.20
  12.0 0.0 copy-done.21
  12.0 2.9 %collective-permute-start.1 = (f32[384,256]{1,0:T(8,128)}, f32[384,256]{1,0:T(8,128)S(1)}, u32[]{:S(2)}, u32[]{:S(2)}) collective-permute-start(f32[384,256]{1,0:T(8,128)} %bitcast.64), channel_id=1, source_target_pairs={{0,32},{32,0},{1,33},{33,1},{2,34},{34,2},{3,35},{35,3},{4,36},{36... | collective-permute-start | bytes 1179656 | tf_op jit(solution)/shard_map/ppermute | solution.py:385
  14.9 1.2 slice_select_fusion
  16.1 1.3 collective-permute-start.7
  17.4 0.0 copy-done.30
  17.4 0.6 broadcast_in_dim.43
  18.1 12.4 %all-to-all-start.2 = ((s32[16,1,256]{2,1,0:T(1,128)}), s32[16,1,256]{2,1,0:T(1,128)S(1)}, u32[]{:S(2)}, u32[]{:S(2)}) async-start(s32[16,1,256]{2,1,0:T(1,128)} %broadcast_in_dim.43), calls=%async_computation.2 | async-start | bytes 32768 | tf_op jit(solution)/shard_map/all_to_all | solution.py:445
  30.5 0.1 pad_add_fusion.place_ref.first_ref
  30.5 8.8 %all-to-all-done.2 = s32[16,1,256]{2,1,0:T(1,128)S(1)} async-done(((s32[16,1,256]{2,1,0:T(1,128)}), s32[16,1,256]{2,1,0:T(1,128)S(1)}, u32[]{:S(2)}, u32[]{:S(2)}) %all-to-all-start.2) | async-done | bytes 16416 | tf_op jit(solution)/shard_map/all_to_all | solution.py:445
  39.4 0.0 collective-permute-done.1.other_ref
  39.4 0.0 copy-done.6
  39.4 2.6 %pack_rows.1 = f32[448,256]{1,0:T(8,128)} custom-call(s32[3]{0:T(128)S(1)} %pad_add_fusion.place_ref.first_ref, s32[16,256]{1,0:T(8,128)S(1)} %bitcast.68, f32[384,256]{1,0:T(8,128)S(1)} %bitcast.67, f32[384,256]{1,0:T(8,128)S(1)} %collective-permute-done.1.other_ref), custom_call_target="tpu_custom_call" | custom-call | tf_op jit(solution)/shard_map/pack_rows/pallas_call | solution.py:102
  42.0 12.1 %collective-permute-done.7.refs_0_ = f32[176,256]{1,0:T(8,128)S(1)} collective-permute-done((f32[176,256]{1,0:T(8,128)S(1)}, f32[176,256]{1,0:T(8,128)S(1)}, u32[]{:S(2)}, u32[]{:S(2)}) %collective-permute-start.7) | collective-permute-done | bytes 180256 | tf_op jit(solution)/shard_map/ppermute | solution.py:385
  54.1 0.0 collective-permute-done.6.near_ref
  54.1 7.0 %all-to-all-start.3 = ((f32[8,56,256]{2,1,0:T(8,128)}), f32[8,56,256]{2,1,0:T(8,128)S(1)}, u32[]{:S(2)}, u32[]{:S(2)}) async-start(f32[8,56,256]{2,1,0:T(8,128)} %bitcast.22), calls=%async_computation.3 | async-start | bytes 917504 | tf_op jit(solution)/shard_map/all_to_all | solution.py:448
  61.0 0.0 copy-start.28
  61.0 0.8 collective-permute-start.10
  61.8 0.7 collective-permute-start.11
  62.5 0.7 collective-permute-start.12
  63.2 1.8 %collective-permute-start.8 = (f32[176,256]{1,0:T(8,128)S(1)}, f32[176,256]{1,0:T(8,128)S(1)}, u32[]{:S(2)}, u32[]{:S(2)}) collective-permute-start(f32[176,256]{1,0:T(8,128)S(1)} %collective-permute-done.7.refs_0_), channel_id=1, source_target_pairs={{8,0},{24,16},{40,32},{56,48},{72,64},{88,80},{104,96},{120,112},{... | collective-permute-start | bytes 540680 | tf_op jit(solution)/shard_map/ppermute | solution.py:385
  65.0 0.7 collective-permute-start.9
  65.7 0.0 copy-start.7
  65.7 0.0 collective-permute-done.10.refs_3_
  65.7 0.0 collective-permute-done.11.refs_4_
  65.7 0.0 collective-permute-done.12.refs_5_
  65.7 1.7 %collective-permute-done.8.refs_1_ = f32[176,256]{1,0:T(8,128)S(1)} collective-permute-done((f32[176,256]{1,0:T(8,128)S(1)}, f32[176,256]{1,0:T(8,128)S(1)}, u32[]{:S(2)}, u32[]{:S(2)}) %collective-permute-start.8) | collective-permute-done | bytes 180256 | tf_op jit(solution)/shard_map/ppermute | solution.py:385
  67.4 0.0 collective-permute-done.9.refs_2_
  67.4 0.0 copy-done.24
  67.4 2.1 %join.1 = (f32[1024,256]{1,0:T(8,128)}, f32[1,1024]{1,0:T(1,128)S(1)}, bf16[3,1024,256]{2,1,0:T(8,128)(2,1)S(1)}, f32[1,1024]{1,0:T(1,128)S(1)}, f32[8,256]{1,0:T(8,128)S(1)}) custom-call(s32[1]{0:T(128)} %bitcast.24.crossed_ref, f32[1032,256]{1,0:T(8,128)S(1)} %collective-permute-done.6.near_ref, s32[1,256]{1,0:T(1,128)S(1)} %compare_select_fusion.1.ids_ref, ...), custom_call_target="tpu_custom_call" | custom-call | tf_op jit(solution)/shard_map/join/pallas_call | solution.py:164
  69.5 14.9 %all-to-all-done.3 = f32[8,56,256]{2,1,0:T(8,128)S(1)} async-done(((f32[8,56,256]{2,1,0:T(8,128)}), f32[8,56,256]{2,1,0:T(8,128)S(1)}, u32[]{:S(2)}, u32[]{:S(2)}) %all-to-all-start.3) | async-done | bytes 458784 | tf_op jit(solution)/shard_map/all_to_all | solution.py:448
  84.4 0.0 copy-done.7
  84.4 4.4 %edge_step.1 = (f32[1,256]{1,0:T(1,128)}, f32[640,256]{1,0:T(8,128)S(1)}, f32[256,256]{1,0:T(8,128)S(1)}, f32[256,1024]{1,0:T(8,128)S(1)}) custom-call(s32[1,1]{1,0:T(1,128)} %copy.41.count_ref, f32[448,256]{1,0:T(8,128)S(1)} %bitcast.61, bf16[3,1024,256]{2,1,0:T(8,128)(2,1)S(1)} %get-tuple-element.113.parts_ref, ...), custom_call_target="tpu_custom_call" | custom-call | tf_op jit(solution)/shard_map/edge_step/pallas_call | solution.py:220
  88.8 0.0 copy-start.1
  88.8 0.9 copy-done.1
  89.7 7.7 %all-to-all-start.4 = ((f32[16,40,256]{2,1,0:T(8,128)}), f32[16,40,256]{2,1,0:T(8,128)S(1)}, u32[]{:S(2)}, u32[]{:S(2)}) async-start(f32[16,40,256]{2,1,0:T(8,128)} %bitcast.62), calls=%async_computation.4 | async-start | bytes 1310720 | tf_op jit(solution)/shard_map/all_to_all | solution.py:453
  97.3 3.9 %table_step.1 = (f32[1024,256]{1,0:T(8,128)}, f32[1,1024]{1,0:T(1,128)}, f32[1,1]{1,0:T(1,128)}, bf16[384,640]{1,0:T(8,128)(2,1)S(1)}, f32[384,256]{1,0:T(8,128)S(1)}) custom-call(s32[3]{0:T(128)S(1)} %pad_add_fusion.place_ref.first_ref, f32[256,1024]{1,0:T(8,128)S(1)} %get-tuple-element.116.weight_ref, f32[256,256]{1,0:T(8,128)S(1)} %get-tuple-element.117.source_ref, ...), custom_call_target="tpu_custom_call" | custom-call | tf_op jit(solution)/shard_map/table_step/pallas_call | solution.py:276
  101.2 28.2 %all-to-all-done.4 = f32[16,40,256]{2,1,0:T(8,128)S(1)} async-done(((f32[16,40,256]{2,1,0:T(8,128)}), f32[16,40,256]{2,1,0:T(8,128)S(1)}, u32[]{:S(2)}, u32[]{:S(2)}) %all-to-all-start.4) | async-done | bytes 655392 | tf_op jit(solution)/shard_map/all_to_all | solution.py:453
  129.5 0.0 copy-done.28
  129.5 1.5 %source_step.1 = (f32[384,256]{1,0:T(8,128)}, f32[1,384]{1,0:T(1,128)}) custom-call(bf16[384,640]{1,0:T(8,128)(2,1)S(1)} %get-tuple-element.121.local_ref, f32[640,256]{1,0:T(8,128)S(1)} %bitcast.60, f32[384,256]{1,0:T(8,128)S(1)} %get-tuple-element.123.rows_ref, f32[1,384]{1,0:T(1,128)S(1)} %bitcast.80), custom_call_target="tpu_custom_call" | custom-call | tf_op jit(solution)/shard_map/source_step/pallas_call | solution.py:298
  130.9 0.0 copy-done.8
  130.9 0.9 while.17
  (4 shorter events, 0.0 us)
Async XLA Ops:
  0.6 38.7 %copy-start.6 = (f32[1,1,384,256]{3,2,1,0:T(8,128)S(1)}, f32[1,1,384,256]{3,2,1,0:T(8,128)}, u32[]{:S(2)}) copy-start(f32[1,1,384,256]{3,2,1,0:T(8,128)} %param.10) | copy-start | bytes 1179652
  0.6 16.8 %copy-start.30 = (s32[1,1,256]{2,1,0:T(1,128)S(1)}, s32[1,1,256]{2,1,0:T(1,128)}, u32[]{:S(2)}) copy-start(s32[1,1,256]{2,1,0:T(1,128)} %param.14) | copy-start | bytes 3076
  0.7 66.8 %copy-start.24 = (s32[1,1,256]{2,1,0:T(1,128)S(1)}, s32[1,1,256]{2,1,0:T(1,128)}, u32[]{:S(2)}) copy-start(s32[1,1,256]{2,1,0:T(1,128)} %param.15) | copy-start | bytes 3076
  2.0 6.1 %collective-permute-start = (f32[176,256]{1,0:T(8,128)S(1)}, f32[176,256]{1,0:T(8,128)S(1)}, u32[]{:S(2)}, u32[]{:S(2)}) collective-permute-start(f32[176,256]{1,0:T(8,128)S(1)} %get-tuple-element.175), channel_id=1, source_target_pairs={{15,12},{31,28},{47,44},{63,60},{79,76},{95,92},{111,108},{127,124... | collective-permute-start | bytes 540680 | tf_op jit(solution)/shard_map/ppermute | solution.py:385
  2.7 5.4 %collective-permute-start.2 = (f32[176,256]{1,0:T(8,128)S(1)}, f32[176,256]{1,0:T(8,128)S(1)}, u32[]{:S(2)}, u32[]{:S(2)}) collective-permute-start(f32[176,256]{1,0:T(8,128)S(1)} %get-tuple-element.174), channel_id=1, source_target_pairs={{15,3},{31,19},{47,35},{63,51},{79,67},{95,83},{111,99},{127,115},... | collective-permute-start | bytes 540680 | tf_op jit(solution)/shard_map/ppermute | solution.py:385
  3.4 4.7 %collective-permute-start.3 = (f32[176,256]{1,0:T(8,128)S(1)}, f32[176,256]{1,0:T(8,128)S(1)}, u32[]{:S(2)}, u32[]{:S(2)}) collective-permute-start(f32[176,256]{1,0:T(8,128)S(1)} %get-tuple-element.173), channel_id=1, source_target_pairs={{15,14},{31,30},{47,46},{63,62},{79,78},{95,94},{111,110},{127,126... | collective-permute-start | bytes 540680 | tf_op jit(solution)/shard_map/ppermute | solution.py:385
  4.1 4.1 %collective-permute-start.4 = (f32[176,256]{1,0:T(8,128)S(1)}, f32[176,256]{1,0:T(8,128)S(1)}, u32[]{:S(2)}, u32[]{:S(2)}) collective-permute-start(f32[176,256]{1,0:T(8,128)S(1)} %get-tuple-element.176), channel_id=1, source_target_pairs={{15,11},{31,27},{47,43},{63,59},{79,75},{95,91},{111,107},{127,123... | collective-permute-start | bytes 540680 | tf_op jit(solution)/shard_map/ppermute | solution.py:385
  4.7 3.4 %collective-permute-start.5 = (f32[176,256]{1,0:T(8,128)S(1)}, f32[176,256]{1,0:T(8,128)}, u32[]{:S(2)}, u32[]{:S(2)}) collective-permute-start(f32[176,256]{1,0:T(8,128)S(1)} %get-tuple-element.172), channel_id=1, source_target_pairs={{15,13},{31,29},{47,45},{63,61},{79,77},{95,93},{111,109},{127,125... | collective-permute-start | bytes 540680 | tf_op jit(solution)/shard_map/ppermute | solution.py:385
  6.1 1.2 copy-start
  7.3 0.7 copy-start.2
  8.1 3.9 %copy-start.20 = (f32[176,256]{1,0:T(8,128)}, f32[176,256]{1,0:T(8,128)S(1)}, u32[]{:S(2)}) copy-start(f32[176,256]{1,0:T(8,128)S(1)} %collective-permute-done.3) | copy-start | bytes 540676
  8.1 3.9 %copy-start.21 = (f32[176,256]{1,0:T(8,128)}, f32[176,256]{1,0:T(8,128)S(1)}, u32[]{:S(2)}) copy-start(f32[176,256]{1,0:T(8,128)S(1)} %collective-permute-done.4) | copy-start | bytes 540676
  8.2 45.9 %collective-permute-start.6 = (f32[1032,256]{1,0:T(8,128)S(1)}, f32[1032,256]{1,0:T(8,128)S(1)}, u32[]{:S(2)}, u32[]{:S(2)}) collective-permute-start(f32[1032,256]{1,0:T(8,128)S(1)} %with_state.1), channel_id=1, source_target_pairs={{0,1},{1,2},{2,3},{3,4},{4,5},{5,6},{6,7},{7,8},{8,9},{9,10},{10,1... | collective-permute-start | bytes 3170312 | tf_op jit(solution)/shard_map/ppermute | solution.py:385
  12.0 27.3 %collective-permute-start.1 = (f32[384,256]{1,0:T(8,128)}, f32[384,256]{1,0:T(8,128)S(1)}, u32[]{:S(2)}, u32[]{:S(2)}) collective-permute-start(f32[384,256]{1,0:T(8,128)} %bitcast.64), channel_id=1, source_target_pairs={{0,32},{32,0},{1,33},{33,1},{2,34},{34,2},{3,35},{35,3},{4,36},{36... | collective-permute-start | bytes 1179656 | tf_op jit(solution)/shard_map/ppermute | solution.py:385
  16.1 37.9 %collective-permute-start.7 = (f32[176,256]{1,0:T(8,128)S(1)}, f32[176,256]{1,0:T(8,128)S(1)}, u32[]{:S(2)}, u32[]{:S(2)}) collective-permute-start(f32[176,256]{1,0:T(8,128)S(1)} %slice_select_fusion), channel_id=1, source_target_pairs={{15,16},{12,24},{3,23},{14,17},{11,20},{13,21},{31,0},{28,8},{19,7... | collective-permute-start | bytes 540680 | tf_op jit(solution)/shard_map/ppermute | solution.py:385
  18.1 21.3 %all-to-all-start.2 = ((s32[16,1,256]{2,1,0:T(1,128)}), s32[16,1,256]{2,1,0:T(1,128)S(1)}, u32[]{:S(2)}, u32[]{:S(2)}) async-start(s32[16,1,256]{2,1,0:T(1,128)} %broadcast_in_dim.43), calls=%async_computation.2 | async-start | bytes 32768 | tf_op jit(solution)/shard_map/all_to_all | solution.py:445
  54.1 30.3 %all-to-all-start.3 = ((f32[8,56,256]{2,1,0:T(8,128)}), f32[8,56,256]{2,1,0:T(8,128)S(1)}, u32[]{:S(2)}, u32[]{:S(2)}) async-start(f32[8,56,256]{2,1,0:T(8,128)} %bitcast.22), calls=%async_computation.3 | async-start | bytes 917504 | tf_op jit(solution)/shard_map/all_to_all | solution.py:448
  61.0 68.5 %copy-start.28 = (f32[1,1,384]{2,1,0:T(1,128)S(1)}, f32[1,1,384]{2,1,0:T(1,128)}, u32[]{:S(2)}) copy-start(f32[1,1,384]{2,1,0:T(1,128)} %param.11) | copy-start | bytes 4612
  61.0 4.7 %collective-permute-start.10 = (f32[176,256]{1,0:T(8,128)S(1)}, f32[176,256]{1,0:T(8,128)S(1)}, u32[]{:S(2)}, u32[]{:S(2)}) collective-permute-start(f32[176,256]{1,0:T(8,128)S(1)} %collective-permute-done.7.refs_0_), channel_id=1, source_target_pairs={{1,0},{17,16},{33,32},{49,48},{65,64},{81,80},{97,96},{113,112},{1... | collective-permute-start | bytes 540680 | tf_op jit(solution)/shard_map/ppermute | solution.py:385
  61.8 3.9 %collective-permute-start.11 = (f32[176,256]{1,0:T(8,128)S(1)}, f32[176,256]{1,0:T(8,128)S(1)}, u32[]{:S(2)}, u32[]{:S(2)}) collective-permute-start(f32[176,256]{1,0:T(8,128)S(1)} %collective-permute-done.7.refs_0_), channel_id=1, source_target_pairs={{4,0},{20,16},{36,32},{52,48},{68,64},{84,80},{100,96},{116,112},{... | collective-permute-start | bytes 540680 | tf_op jit(solution)/shard_map/ppermute | solution.py:385
  62.5 3.2 %collective-permute-start.12 = (f32[176,256]{1,0:T(8,128)S(1)}, f32[176,256]{1,0:T(8,128)S(1)}, u32[]{:S(2)}, u32[]{:S(2)}) collective-permute-start(f32[176,256]{1,0:T(8,128)S(1)} %collective-permute-done.7.refs_0_), channel_id=1, source_target_pairs={{5,0},{21,16},{37,32},{53,48},{69,64},{85,80},{101,96},{117,112},{... | collective-permute-start | bytes 540680 | tf_op jit(solution)/shard_map/ppermute | solution.py:385
  63.2 4.2 %collective-permute-start.8 = (f32[176,256]{1,0:T(8,128)S(1)}, f32[176,256]{1,0:T(8,128)S(1)}, u32[]{:S(2)}, u32[]{:S(2)}) collective-permute-start(f32[176,256]{1,0:T(8,128)S(1)} %collective-permute-done.7.refs_0_), channel_id=1, source_target_pairs={{8,0},{24,16},{40,32},{56,48},{72,64},{88,80},{104,96},{120,112},{... | collective-permute-start | bytes 540680 | tf_op jit(solution)/shard_map/ppermute | solution.py:385
  65.0 2.4 %collective-permute-start.9 = (f32[176,256]{1,0:T(8,128)S(1)}, f32[176,256]{1,0:T(8,128)S(1)}, u32[]{:S(2)}, u32[]{:S(2)}) collective-permute-start(f32[176,256]{1,0:T(8,128)S(1)} %collective-permute-done.7.refs_0_), channel_id=1, source_target_pairs={{7,0},{23,16},{39,32},{55,48},{71,64},{87,80},{103,96},{119,112},{... | collective-permute-start | bytes 540680 | tf_op jit(solution)/shard_map/ppermute | solution.py:385
  65.7 18.7 %copy-start.7 = (s32[1,256]{1,0:T(1,128)}, s32[1,256]{1,0:T(1,128)S(1)}, u32[]{:S(2)}) copy-start(s32[1,256]{1,0:T(1,128)S(1)} %compare_select_fusion.1.ids_ref) | copy-start | bytes 3076
  88.8 0.9 copy-start.1
  88.8 42.1 %copy-start.8 = (s32[1,256]{1,0:T(1,128)S(1)}, s32[1,256]{1,0:T(1,128)}, u32[]{:S(2)}) copy-start(s32[1,256]{1,0:T(1,128)} %copy-done.7) | copy-start | bytes 3076
  89.7 39.8 %all-to-all-start.4 = ((f32[16,40,256]{2,1,0:T(8,128)}), f32[16,40,256]{2,1,0:T(8,128)S(1)}, u32[]{:S(2)}, u32[]{:S(2)}) async-start(f32[16,40,256]{2,1,0:T(8,128)} %bitcast.62), calls=%async_computation.4 | async-start | bytes 1310720 | tf_op jit(solution)/shard_map/all_to_all | solution.py:453
